TPU v7x, 32 devices: a whole 2x2x4 slice. The times are simulated.
32 devices in a mesh: blk: 8 (over y, x, core), ch: 4 (over z).
Axes of the slice: x: 2, y: 2, z: 4, core: 2. Of those that a mesh axis runs over, the one named last changes fastest.
Arguments:
- block_input: bfloat16 [2, 64, 64, 512], P(None, 'blk', None, 'ch'), may hold values from -18 to 18
- cotangent: bfloat16 [2, 64, 64, 512], P(None, 'blk', None, 'ch'), may hold values from -6 to 6
- image_embed: float32 [2, 2048], replicated, may hold values from -6 to 6
- timesteps: int32 [2], replicated, may hold values from 0 to 999
- text_len: int32 [2], replicated, may hold values from 5 to 256, as said below
- context: bfloat16 [2, 260, 2048], P(None, None, 'ch'), may hold values from -6 to 6
- conv1_weight: bfloat16 [3, 3, 512, 512], P(None, None, None, 'ch'), may hold values from -0.09375 to 0.09375
- conv2_weight: bfloat16 [3, 3, 512, 512], P(None, None, None, 'ch'), may hold values from -0.09375 to 0.09375
- embed_weight: bfloat16 [2048, 2, 512], P(None, None, 'ch'), may hold values from -0.125 to 0.125
- embed_bias: float32 [2, 512], P(None, 'ch'), may hold values from -2 to 2
- norm1_gain: float32 [512], P('ch'), may hold values from 0.5 to 1.5
- norm1_bias: float32 [512], P('ch'), may hold values from -2 to 2
- norm2_gain: float32 [512], P('ch'), may hold values from 0.5 to 1.5
- norm2_bias: float32 [512], P('ch'), may hold values from -2 to 2
- norm3_gain: float32 [512], P('ch'), may hold values from 0.5 to 1.5
- norm3_bias: float32 [512], P('ch'), may hold values from -2 to 2
- qkv_weight: bfloat16 [512, 3, 512], P(None, None, 'ch'), may hold values from -0.25 to 0.25
- out_weight: bfloat16 [512, 512], P('ch'), may hold values from -2 to 2
- ctx_weight: bfloat16 [2048, 2, 512], P('ch'), may hold values from -0.125 to 0.125
Outputs:
- block_output: bfloat16 [2, 64, 64, 512], P(None, 'blk', None, 'ch')
- input_grad: float32 [2, 64, 64, 512], P(None, 'blk', None, 'ch')
- conv1_grad: float32 [3, 3, 512, 512], P(None, None, None, 'ch')
- conv2_grad: float32 [3, 3, 512, 512], P(None, None, None, 'ch')
- embed_weight_grad: float32 [2048, 2, 512], P(None, None, 'ch')
- embed_bias_grad: float32 [2, 512], P(None, 'ch')
- norm1_gain_grad: float32 [512], P('ch')
- norm1_bias_grad: float32 [512], P('ch')
- norm2_gain_grad: float32 [512], P('ch')
- norm2_bias_grad: float32 [512], P('ch')
- norm3_gain_grad: float32 [512], P('ch')
- norm3_bias_grad: float32 [512], P('ch')
- qkv_grad: float32 [512, 3, 512], P(None, None, 'ch')
- out_grad: float32 [512, 512], P('ch')
- ctx_grad: float32 [2048, 2, 512], P('ch')
Inputs may be any that keep to these rules, and one draw needn't show every extreme that they name: `text_len`: in every draw one image's text has exactly 256 tokens.
All inputs are finite; a program needn't handle non-finite values.
Results may differ from a plain program's by a relative error of at most 0.024.
Values may be sent and summed in bfloat16 or wider, within the bound.
No kernel may reach another device: no remote copies, remote signals or barrier semaphores. Data moves between devices by JAX's collectives and lax.ppermute only.
A program may use at most 192 MiB of HBM per device.

v0:
```python
import functools
import math

import jax
import jax.numpy as jnp
from jax import lax
from jax.experimental import pallas as pl
from jax.experimental.pallas import tpu as pltpu
from jax.sharding import PartitionSpec as P

HEAD = 64
GROUPS = 32
CLIPTOK = 4
LANES = 128
HALF = 256
COLS = 64
VMEM_BYTES = 56 * 2**20
BF = jnp.bfloat16
F32 = jnp.float32

H, I, UP1, DOWN1, UP2, DOWN2, Z, B = range(8)


def dot(a, b):
    return jnp.dot(a, b, preferred_element_type=F32)


def dot_t(a, b):
    return lax.dot_general(a, b, (((1,), (1,)), ((), ())), preferred_element_type=F32)


def group_sum(vec, size):
    lane = lax.broadcasted_iota(jnp.int32, vec.shape, 1)
    step = 1
    while step < size:
        low = pltpu.roll(vec, step, 1)
        high = pltpu.roll(vec, LANES - step, 1)
        vec = vec + jnp.where((lane & step) != 0, low, high)
        step *= 2
    return vec


def shards(scal):
    h = scal[H]
    return (h, h + 2, 1 - h, 3 - h)


def lanes_of(shard):
    return pl.ds(pl.multiple_of(shard * LANES, LANES), LANES)


def part_of(quarter):
    return slice((quarter % 2) * LANES, (quarter % 2 + 1) * LANES)


def norm_stats(scal, sums, quarter, cells, size):
    wide = sums.shape[2] == HALF
    kinds = 2 if wide else 4
    shard = shards(scal)[quarter]
    total = None
    for source in range(sums.shape[0] // kinds):
        row = source * kinds + (shard % 2 if wide else shard)
        piece = sums[pl.ds(row, 1)][0]
        total = piece if total is None else total + piece
    if wide:
        total = total[:, part_of(quarter)]
    total = group_sum(total, size)
    mean = total[0:1] / cells
    inv = lax.rsqrt(total[1:2] / cells - mean * mean + 1e-05)
    return mean, inv


def affine_of(scal, vec, quarter, which, mean, inv):
    row = vec[pl.ds(shards(scal)[quarter], 1)][0]
    gain = row[2 * which + 2 : 2 * which + 3]
    bias = row[2 * which + 3 : 2 * which + 4]
    if which == 1:
        first = scal[I] == 0
        grow = 1.0 + jnp.where(first, row[8:9], row[10:11])
        gain, bias = gain * grow, bias * grow + jnp.where(first, row[9:10], row[11:12])
    slope = inv * gain
    return gain, slope, bias - mean * slope


def column_sums(first, second):
    rows = jnp.concatenate(
        [jnp.sum(first, axis=0, keepdims=True), jnp.sum(second, axis=0, keepdims=True)], axis=0
    )
    return jnp.concatenate([rows, jnp.zeros((6, rows.shape[1]), F32)], axis=0)


def shift_columns(total, left, right):
    col = lax.broadcasted_iota(jnp.int32, total.shape, 0) % COLS
    rows = total.shape[0]
    total = total + jnp.where(col > 0, pltpu.roll(left, 1, 0), 0.0)
    return total + jnp.where(col < COLS - 1, pltpu.roll(right, rows - 1, 0), 0.0)


def silu_slope(field):
    sigma = jax.nn.sigmoid(field)
    return sigma * (1.0 + field * (1.0 - sigma))


def masked_rows(scal, value, flag):
    return jnp.where(scal[flag] > 0, value, 0.0)


def input_sums_kernel(scal, field, vec, out, *, blocks):
    for image in range(2):
        value = field[image].astype(F32)
        sums = column_sums(value, value * value)[:2]
        sums = jnp.concatenate([sums, vec[2:]], axis=0)
        for target in range(blocks):
            out[4 * target + 2 * image] = sums
            out[4 * target + 2 * image + 1] = sums


def image_split_kernel(scal, field, mine, theirs):
    mine[...] = field[pl.ds(scal[I], 1)][0]
    theirs[...] = field[pl.ds(1 - scal[I], 1)][0]


def spread(out, sums):
    for target in range(out.shape[0]):
        out[target] = sums


def conv1_kernel(scal, own, oth, top, bot, sums, weight, out, out_sums, act_out, vec, act_scr, *, cells, size):
    pix = own.shape[0]
    vec[...] = sums[0:4]
    rows = pix + 2 * COLS
    for quarter in range(4):
        shard = shards(scal)[quarter]
        mean, inv = norm_stats(scal, sums, quarter, cells, size)
        gain, slope, offset = affine_of(scal, vec, quarter, 0, mean, inv)
        lanes = slice(quarter * LANES, (quarter + 1) * LANES)

        def active(field):
            pre = field.astype(F32) * slope + offset
            return pre * jax.nn.sigmoid(pre)

        half = own if quarter < 2 else oth
        main = active(half[:, part_of(quarter)]).astype(BF)
        above, below = active(top[:, lanes]), active(bot[:, lanes])
        act_scr[2 * COLS : 2 * COLS + pix, lanes_of(shard)] = main
        act_out[:, lanes_of(shard)] = main
        act_scr[0:COLS, lanes_of(shard)] = masked_rows(scal, above[:COLS], UP2).astype(BF)
        act_scr[COLS : 2 * COLS, lanes_of(shard)] = masked_rows(scal, above[COLS:], UP1).astype(BF)
        end = 2 * COLS + pix
        act_scr[end : end + COLS, lanes_of(shard)] = masked_rows(scal, below[:COLS], DOWN1).astype(BF)
        act_scr[end + COLS :, lanes_of(shard)] = masked_rows(scal, below[COLS:], DOWN2).astype(BF)
    result = convolve(act_scr, weight, rows)
    out[...] = result.astype(BF)
    inner = result[COLS : COLS + pix]
    spread(out_sums, column_sums(inner, inner * inner))


def convolve(act_scr, weight, rows):
    channels = act_scr.shape[1]
    parts = []
    for kx in range(3):
        acc = None
        for ky in range(3):
            tap = (ky * 3 + kx) * channels
            term = dot(act_scr[ky * COLS : ky * COLS + rows, :], weight[tap : tap + channels, :])
            acc = term if acc is None else acc + term
        parts.append(acc)
    return shift_columns(parts[1], parts[0], parts[2])


def conv2_kernel(scal, own, oth, sums, vec, weight, base, act_below, out_f, out_low, out_sums, act_first, act_out, edges, act_scr, *, cells, size):
    pix = base.shape[0]
    cut = act_first.shape[0]
    act_first[...] = act_below[0:cut]
    act_out[0 : pix - cut, :] = act_below[cut:]
    for quarter in range(4):
        shard = shards(scal)[quarter]
        mean, inv = norm_stats(scal, sums, quarter, cells, size)
        gain, slope, offset = affine_of(scal, vec, quarter, 1, mean, inv)
        half = own if quarter < 2 else oth
        pre = half[:, part_of(quarter)].astype(F32) * slope + offset
        act = pre * jax.nn.sigmoid(pre)
        main = act[COLS : COLS + pix].astype(BF)
        act_scr[COLS : COLS + pix, lanes_of(shard)] = main
        act_out[pix - cut :, lanes_of(shard)] = main
        act_scr[0:COLS, lanes_of(shard)] = masked_rows(scal, act[:COLS], UP1).astype(BF)
        act_scr[COLS + pix :, lanes_of(shard)] = masked_rows(scal, act[COLS + pix :], DOWN1).astype(BF)
    result = convolve(act_scr, weight, pix) + base[...].astype(F32)
    out_f[...] = result
    low = result.astype(BF)
    out_low[...] = low
    if edges.shape[1] < pix:
        edges[0], edges[1] = low[: edges.shape[1]], low[pix - edges.shape[1] :]
    else:
        edges[0], edges[1] = low, low
    spread(out_sums, column_sums(result, result * result))


def qkv_kernel(scal, own, oth, sums, vec, cot_own, cot_oth, weight, out, act_out, cot_out, edges, *, cells, size):
    rows = edges.shape[1]
    edges[0], edges[1] = cot_own[0:rows], cot_own[cot_own.shape[0] - rows :]
    for quarter in range(4):
        shard = shards(scal)[quarter]
        mean, inv = norm_stats(scal, sums, quarter, cells, size)
        gain, slope, offset = affine_of(scal, vec, quarter, 2, mean, inv)
        half = own if quarter < 2 else oth
        cot = cot_own if quarter < 2 else cot_oth
        field = half[:, part_of(quarter)].astype(F32)
        act_out[:, lanes_of(shard)] = (field * slope + offset).astype(BF)
        cot_out[:, lanes_of(shard)] = cot[:, part_of(quarter)]
    for head in range(4):
        columns = weight[:, head * HALF : (head + 1) * HALF]
        fwd = dot(act_out[...], columns)
        back = dot(cot_out[...], columns[:, LANES:])
        out[head, :, :LANES] = fwd[:, :LANES].astype(BF)
        lane = lax.broadcasted_iota(jnp.int32, back.shape, 1)
        out[head, :, LANES:] = jnp.where(lane < HEAD, fwd[:, LANES:], back).astype(BF)


def below_stats(scal, total, own, oth, sums, vec, out_own, out_oth, out_stats, which, cells, size):
    rows = total.shape[0]
    pix = rows - 2 * COLS if which == 1 else rows
    inner = slice(COLS, COLS + pix) if which == 1 else slice(0, pix)
    for quarter in range(4):
        shard = shards(scal)[quarter]
        mean, inv = norm_stats(scal, sums, quarter, cells, size)
        gain, slope, offset = affine_of(scal, vec, quarter, which, mean, inv)
        half = own if quarter < 2 else oth
        part = part_of(quarter)
        if quarter < 2:
            out_own[:, part] = total[:, lanes_of(shard)]
        else:
            out_oth[:, part] = total[:, lanes_of(shard)].astype(BF)
        grad = total[inner, lanes_of(shard)]
        field = half[inner, part].astype(F32)
        if which < 2:
            grad = grad * silu_slope(field * slope + offset)
        result = column_sums(grad, grad * ((field - mean) * inv))
        slot = scal[H] if quarter < 2 else 1 - scal[H]
        for target in range(out_stats.shape[0] // 2):
            out_stats[pl.ds(2 * target + slot, 1), :, part] = result[None]


def qkv_back_kernel(scal, grads, weight, own, oth, sums, vec, out_own, out_oth, out_stats, tot_scr, *, cells, size):
    total = None
    for head in range(4):
        columns = weight[:, head * HALF : (head + 1) * HALF]
        grad = grads[head]
        lane = lax.broadcasted_iota(jnp.int32, grad.shape, 1)
        term = dot_t(jnp.where(lane < 3 * HEAD, grad, jnp.zeros_like(grad)), columns)
        total = term if total is None else total + term
    tot_scr[...] = total
    below_stats(scal, tot_scr, own, oth, sums, vec, out_own, out_oth, out_stats, 2, cells, size)


def out_kernel(scal, grads, weight, act, cot, proj_own, proj_oth, wgrad, tot_scr):
    channels = act.shape[1]
    act_t = act[...].astype(F32).T.astype(BF)
    total = None
    for pair in range(2):
        slot = jnp.where(scal[I] == pair, 0, 1)
        parts, outs = [], []
        for head in (2 * pair, 2 * pair + 1):
            columns = weight[:, head * HALF + LANES : (head + 1) * HALF]
            grad = grads[head]
            low = grad[:, LANES:]
            lane = lax.broadcasted_iota(jnp.int32, low.shape, 1)
            term = dot_t(jnp.where(lane < HEAD, jnp.zeros_like(low), low), columns)
            total = term if total is None else total + term
            parts.append(dot(act_t, grad))
            outs.append(dot(low.astype(F32).T[HEAD:].astype(BF), cot[...]))
        first, second = parts
        pieces = [
            jnp.concatenate([first[:, LANES : LANES + HEAD], second[:, LANES : LANES + HEAD]], axis=1)
            * 0.125,
            jnp.concatenate([first[:, :HEAD], second[:, :HEAD]], axis=1),
            jnp.concatenate([first[:, HEAD:LANES], second[:, HEAD:LANES]], axis=1),
        ]
        both = jnp.concatenate(outs, axis=0)
        pieces += [both[:, n * LANES : (n + 1) * LANES] for n in range(channels // LANES)]
        wgrad[pl.ds(slot, 1)] = jnp.concatenate(pieces, axis=0).astype(BF)[None]
    tot_scr[...] = total
    for quarter, shard in enumerate(shards(scal)):
        if quarter < 2:
            proj_own[:, part_of(quarter)] = tot_scr[:, lanes_of(shard)]
        else:
            proj_oth[:, part_of(quarter)] = tot_scr[:, lanes_of(shard)].astype(BF)


def total_stats(stats):
    total = stats[0]
    for source in range(1, stats.shape[0]):
        total = total + stats[source]
    return total


def norm_back(scal, quarter, sums, stats, vec, which, cells, size):
    mean, inv = norm_stats(scal, sums, quarter, cells, size)
    gain, slope, offset = affine_of(scal, vec, quarter, which, mean, inv)
    means = group_sum(total_stats(stats)[:, part_of(quarter)] * gain, size) / cells

    def back(grad, field):
        field = field.astype(F32)
        hat = (field - mean) * inv
        if which < 2:
            grad = grad * silu_slope(field * slope + offset)
        return (grad * gain - means[0:1] - hat * means[1:2]) * inv

    return back


def norm3_back_kernel(
    scal, part, recv, dtop, dbot, field, ftop, fbot, cot, ctop, cbot, sums, stats, vec, out_f, ext, away, *, cells, size
):
    pix = part.shape[0]
    end = 2 * COLS + pix
    for quarter in range(2):
        lanes = part_of(quarter)
        back = norm_back(scal, quarter, sums, stats, vec, 2, cells, size)
        main = back(part[:, lanes] + recv[:, lanes].astype(F32), field[:, lanes])
        main = main + cot[:, lanes].astype(F32)
        out_f[:, lanes] = main
        ext[2 * COLS : end, lanes] = main.astype(BF)
        head = back(dtop[:, lanes].astype(F32), ftop[:, lanes]) + ctop[:, lanes].astype(F32)
        tail = back(dbot[:, lanes].astype(F32), fbot[:, lanes]) + cbot[:, lanes].astype(F32)
        ext[0:COLS, lanes] = masked_rows(scal, head[:COLS], UP2).astype(BF)
        ext[COLS : 2 * COLS, lanes] = masked_rows(scal, head[COLS:], UP1).astype(BF)
        ext[end : end + COLS, lanes] = masked_rows(scal, tail[:COLS], DOWN1).astype(BF)
        ext[end + COLS :, lanes] = masked_rows(scal, tail[COLS:], DOWN2).astype(BF)
    away[...] = ext[COLS : end + COLS, lanes_of(1 - scal[I])]


def norm2_back_kernel(scal, part, recv, field, sums, stats, vec, ext, away, *, cells, size):
    rows = part.shape[0]
    for quarter in range(2):
        lanes = part_of(quarter)
        back = norm_back(scal, quarter, sums, stats, vec, 1, cells, size)
        main = back(part[:, lanes] + recv[:, lanes].astype(F32), field[:, lanes])
        ext[0:COLS, lanes] = masked_rows(scal, main[:COLS], UP1).astype(BF)
        ext[COLS : rows - COLS, lanes] = main[COLS : rows - COLS].astype(BF)
        ext[rows - COLS :, lanes] = masked_rows(scal, main[rows - COLS :], DOWN1).astype(BF)
    away[...] = ext[:, lanes_of(1 - scal[I])]


def conv_back_kernel(scal, ext, weight, own, oth, sums, vec, out_own, out_oth, out_stats, tot_scr, *, which, cells, size):
    rows, channels = tot_scr.shape
    parts = []
    for kx in range(3):
        acc = None
        for ky in range(3):
            tap = (ky * 3 + kx) * channels
            start = (2 - ky) * COLS
            term = dot_t(ext[start : start + rows, :], weight[tap : tap + channels, :])
            acc = term if acc is None else acc + term
        parts.append(acc)
    tot_scr[...] = shift_columns(parts[1], parts[2], parts[0])
    below_stats(scal, tot_scr, own, oth, sums, vec, out_own, out_oth, out_stats, which, cells, size)


def last_kernel(scal, part, recv, field, sums, stats, vec, resid_grad, keep, send, tot_scr, *, cells, size):
    i = scal[I]
    for quarter in range(2):
        lanes = part_of(quarter)
        back = norm_back(scal, quarter, sums, stats, vec, 0, cells, size)
        main = back(part[:, lanes] + recv[:, lanes].astype(F32), field[:, lanes])
        tot_scr[:, lanes] = main + resid_grad[:, lanes]
    keep[...] = tot_scr[:, lanes_of(i)]
    send[...] = tot_scr[:, lanes_of(1 - i)].astype(BF)


def weight_grads(scal, act_one, act_two, ext_one, ext_two, rhs_scr, out_scr):
    pix, channels = act_one.shape
    rows = ext_two.shape[0]
    first = (ext_one.shape[0] - rows) // 2
    own = ext_one[first : first + rows, lanes_of(scal[I])]
    for image, wide in enumerate((own, ext_two[...])):
        wide = wide.astype(F32)
        col = lax.broadcasted_iota(jnp.int32, wide.shape, 0) % COLS
        for kx in range(3):
            if kx == 0:
                moved = jnp.where(col < COLS - 1, pltpu.roll(wide, rows - 1, 0), 0.0)
            elif kx == 2:
                moved = jnp.where(col > 0, pltpu.roll(wide, 1, 0), 0.0)
            else:
                moved = wide
            moved = moved.astype(BF)
            for ky in range(3):
                start = (2 - ky) * COLS
                tap = ky * 3 + kx
                lanes = slice(tap * LANES, (tap + 1) * LANES)
                rhs_scr[image * pix : (image + 1) * pix, lanes] = moved[start : start + pix]
    both = jnp.concatenate([act_one, act_two], axis=0)
    for tap in range(0, 9, 2):
        count = min(2, 9 - tap)
        total = lax.dot_general(
            both,
            rhs_scr[:, tap * LANES : (tap + count) * LANES],
            (((0,), (0,)), ((), ())),
            preferred_element_type=F32,
        )
        for n in range(count):
            out_scr[(tap + n) * channels : (tap + n + 1) * channels, :] = total[
                :, n * LANES : (n + 1) * LANES
            ]


def weight_grad_one_kernel(
    scal, up, low, up_there, low_there, ext_one, ext_two, keep, send, rhs_scr, out_scr
):
    cut = up.shape[0]
    mine = jnp.concatenate([up[...], low[0:cut]], axis=0)
    theirs = jnp.concatenate([up_there[...], low_there[0:cut]], axis=0)
    weight_grads(scal, mine, theirs, ext_one, ext_two, rhs_scr, out_scr)
    core = scal[B] % 2
    count = out_scr.shape[0] // 2
    at = lambda n: pl.ds(pl.multiple_of(n * count, count), count)
    keep[...] = out_scr[at(core), :].reshape(keep.shape)
    send[...] = out_scr[at(1 - core), :].astype(BF).reshape(send.shape)


def weight_grad_two_kernel(scal, act, act_there, ext_one, ext_two, wp, out, rhs_scr, out_scr):
    cut = act.shape[0] // 3
    weight_grads(scal, act[cut:], act_there[cut:], ext_one, ext_two, rhs_scr, out_scr)
    blocks = out.shape[0]
    rows = out_scr.shape[0] // blocks
    extra = wp.shape[1] // blocks
    out[:, :rows] = out_scr[...].astype(BF).reshape(blocks, rows, LANES)
    for part in range(2):
        first = rows + part * extra
        out[:, first : first + extra] = wp[part].reshape(blocks, extra, LANES)


def other_sum_kernel(scal, parts, out):
    first = parts.shape[1] - out.shape[0]
    total = parts[0, first:].astype(F32)
    for source in range(1, parts.shape[0]):
        total = total + parts[source, first:].astype(F32)
    out[...] = total.astype(BF)


def total_kernel(scal, own, parts, other, one, two, three, out):
    count = own.shape[0]
    extra = other.shape[0]
    first = own[...] + one[...].astype(F32) + two[...].astype(F32) + three[...].astype(F32)
    out[0:count] = first.astype(BF)
    second = parts[0, : count + extra].astype(F32)
    for source in range(1, parts.shape[0]):
        second = second + parts[source, : count + extra].astype(F32)
    out[count : 2 * count] = second[:count].astype(BF)
    out[2 * count :] = (second[count:] + other[...].astype(F32)).astype(BF)


def scatter_kernel(scal, keep, recv, own, *sends):
    chip = scal[B] // 2
    for mask in range(4):
        chunk = pl.ds(chip ^ mask, 1)
        value = (keep[chunk] + recv[chunk].astype(F32))[0]
        if mask == 0:
            own[...] = value
        else:
            sends[mask - 1][...] = value.astype(BF)


def place_kernel(scal, *refs):
    pieces, (one, two, qkv, out) = refs[:8], refs[8:]
    core, chip = scal[B] % 2, scal[B] // 2
    count = one.shape[0] // 8
    rows = qkv.shape[0] // 6
    for n, piece in enumerate(pieces):
        half = core if n < 4 else 1 - core
        source = chip ^ (n % 4)
        at = lambda slot, size: pl.ds(pl.multiple_of(slot * size, size), size)
        slot = 2 * source + half
        one[at(4 * half + source, count), :] = piece[:count].astype(F32)
        two[at(slot, count), :] = piece[count : 2 * count].astype(F32)
        extra = piece[2 * count :].astype(F32)

        @pl.when(slot < 6)
        def _(extra=extra, slot=slot):
            qkv[at(slot, rows), :] = extra

        @pl.when(slot >= 6)
        def _(extra=extra, slot=slot):
            for m in range(rows // LANES):
                column = (slot - 6) * (rows // LANES) + m
                out[:, lanes_of(column)] = extra[m * LANES : (m + 1) * LANES]


def channel_sums_kernel(scal, one, two, three, mine, theirs):
    rows = jnp.concatenate([total_stats(stats)[0:2] for stats in (one, two, three)], axis=0)
    rows = jnp.concatenate([rows, jnp.zeros((2, rows.shape[1]), F32)], axis=0)
    first, second = rows[:, :LANES], rows[:, LANES:]
    here = scal[I] == 0
    mine[...] = jnp.where(here, first, second)
    theirs[...] = jnp.where(here, second, first)


def channel_grads_kernel(scal, mine, recv, vec, emb, bias_grad, *outs):
    here = scal[I] == 0
    images = (
        jnp.where(here, mine[...], recv[...]),
        jnp.where(here, recv[...], mine[...]),
    )
    gain, bias = vec[4:5], vec[5:6]
    scales = [gain * rows[3:4] + bias * rows[2:3] for rows in images]
    shifts = [rows[2:3] for rows in images]
    grown = [1.0 + vec[8:9], 1.0 + vec[10:11]]
    both = images[0] + images[1]
    bias_grad[0:1] = scales[0] + scales[1]
    bias_grad[1:2] = shifts[0] + shifts[1]
    values = [
        both[1:2],
        both[0:1],
        grown[0] * images[0][3:4] + grown[1] * images[1][3:4],
        grown[0] * images[0][2:3] + grown[1] * images[1][2:3],
        both[5:6],
        both[4:5],
    ]
    for out, value in zip(outs, values):
        out[...] = value
    weight_grad = outs[6]
    turned = emb[...].T
    total = None
    for n, row in enumerate(scales + shifts):
        term = turned[:, n : n + 1] * row
        total = term if total is None else total + term
    weight_grad[...] = total


def out_add_kernel(scal, resid, part, recv, keep, send):
    total = resid[...] + part[...] + recv[...].astype(F32)
    first, second = total[:, :LANES].astype(BF), total[:, LANES:].astype(BF)
    here = scal[I] == 0
    keep[...] = jnp.where(here, first, second)
    send[...] = jnp.where(here, second, first)


def by_images_kernel(scal, out_keep, out_recv, in_keep, in_recv, block_output, input_grad):
    i = scal[I]
    for keep, recv, out in ((out_keep, out_recv, block_output), (in_keep, in_recv, input_grad)):
        out[pl.ds(i, 1)] = keep[...][None]
        out[pl.ds(1 - i, 1)] = recv[...].astype(out.dtype)[None]


def merge_kernel(scal, mine, recv, rest, out):
    out[:, :LANES] = (mine[...] + recv[...].astype(F32)).astype(BF)
    out[:, LANES:] = rest[...]


def context_grad_kernel(scal, context, d_zero, d_one, d_two, d_three, out, tot_scr, *, split):
    rows = out.shape[0]
    turned = [context[image].astype(F32).T.astype(BF) for image in range(2)]
    pieces = (d_zero, d_one, d_two, d_three)
    for h in range(2):
        total = None
        for image in range(2):
            slot = (2 * image + h) ^ scal[Z]
            chosen = pieces[0][...]
            for n in range(1, 4):
                chosen = jnp.where(slot == n, pieces[n][...], chosen)
            term = dot(turned[image], chosen)
            total = term if total is None else total + term
        tot_scr[:, h * LANES : (h + 1) * LANES] = total
    part = scal[B] % split
    out[...] = tot_scr[pl.ds(pl.multiple_of(part * rows, rows), rows), :].astype(BF)


def context_place_kernel(scal, pieces, out, *, split):
    rows = pieces.shape[1]
    for part in range(split):
        for t in range(2):
            first, second = ((2 * t + n) * split + part for n in range(2))
            for h in range(2):
                for kind in range(2):
                    start = h * LANES + kind * HEAD
                    value = jnp.concatenate(
                        [pieces[n, :, start : start + HEAD] for n in (first, second)], axis=1
                    )
                    column = (h + 2 * t) * LANES
                    out[part * rows : (part + 1) * rows, kind, column : column + LANES] = (
                        value.astype(F32)
                    )


def join_kernel(scal, own, *refs):
    pieces, out = refs[:8], refs[8]
    i, b = scal[I], scal[B]
    out[:, lanes_of(i)] = own[...]
    size = own.shape[0] // 8
    for core in range(2):
        for mask in range(4):
            source = b ^ (2 * mask + core)
            target = pl.ds(pl.multiple_of(source * size, size), size)
            out[target, lanes_of(1 - i)] = pieces[4 * core + mask][...]


def place_weight_kernel(scal, own, chunks, out, *, start, width):
    i = scal[I]
    rows = own.shape[0] // width
    size = own.shape[0] // chunks.shape[0]
    for n in range(width):
        out[:, lanes_of(i * width + n)] = own[n * rows : (n + 1) * rows]
    for source in range(chunks.shape[0]):
        n, first = divmod(source * size, rows)
        out[first : first + size, lanes_of((1 - i) * width + n)] = chunks[
            source, start : start + size
        ]


def attend_kernel(
    live, qd, kva, kvb, ctx, dqo, dkva, dkvb, dctx,
    kv_scr, kt_scr, vt_scr, s_scr, e_scr, acc_scr, *, chunk, unroll,
):
    step = pl.program_id(0)
    half_a, half_b, extra = kva.shape[0], kvb.shape[0], ctx.shape[0]
    keys = half_a + half_b
    total = keys + extra
    block = qd.shape[0]

    @pl.when(step == 0)
    def _():
        kv_scr[0:half_a, :] = kva[...]
        kv_scr[half_a:keys, :] = kvb[...]
        kv_scr[keys:total, :] = ctx[...]
        acc_scr[...] = jnp.zeros_like(acc_scr)

        def turn(rows):
            flipped = kv_scr[rows, :].astype(F32).T.astype(BF)
            kt_scr[:, rows] = flipped[:HEAD]
            vt_scr[0:HEAD, rows] = flipped[HEAD:]

        def turn_step(n, carry):
            turn(pl.ds(pl.multiple_of(n * 256, 256), 256))
            return carry

        lax.fori_loop(0, keys // 256, turn_step, 0)
        turn(slice(keys, total))
        vt_scr[HEAD:, :] = jnp.ones((16, total), BF)

    both = qd[...].astype(F32).T
    q_t = both[:HEAD].astype(BF)
    zero = jnp.zeros((HEAD, block), BF)
    q_side = jnp.concatenate([q_t, zero], axis=0)

    def score(rows, top, masked):
        s = dot(kv_scr[rows, :], q_side)
        if masked:
            index = lax.broadcasted_iota(jnp.int32, s.shape, 0)
            s = jnp.where(index < live[0], s, -1e30)
        s_scr[rows, :] = s
        return jnp.maximum(top, jnp.max(s.reshape(-1, 8, block), axis=0))

    def span(n):
        return pl.ds(pl.multiple_of(n * chunk, chunk), chunk)

    def over_keys(func, carry):
        return lax.fori_loop(
            0, keys // chunk, lambda n, c: func(span(n), c), carry, unroll=unroll
        )

    tail = pl.ds(keys, extra)
    top = score(tail, jnp.full((8, block), -1e30, F32), True)
    top = over_keys(lambda rows, c: score(rows, c, False), top)
    top = jnp.max(top, axis=0, keepdims=True)

    def weigh(rows, acc):
        e = jnp.exp(s_scr[rows, :] - top).astype(BF)
        e_scr[rows, :] = e
        return acc + dot(vt_scr[:, rows], e)

    out_t = weigh(tail, jnp.zeros((HEAD + 16, block), F32))
    out_t = over_keys(weigh, out_t)
    inv = 1.0 / out_t[HEAD : HEAD + 1]
    out_t = out_t[:HEAD] * inv
    d_t = both[HEAD:]
    delta = jnp.sum(d_t * out_t, axis=0, keepdims=True) * inv
    d_t = d_t * inv
    d_low = d_t.astype(BF)
    d_side = jnp.concatenate([zero, d_low], axis=0)

    def back(rows, acc):
        d_prob = dot(kv_scr[rows, :], d_side)
        e = e_scr[rows, :]
        d_score = (e.astype(F32) * (d_prob - delta)).astype(BF)
        acc_scr[0:HEAD, rows] += dot_t(q_t, d_score)
        acc_scr[HEAD:, rows] += dot_t(d_low, e)
        return acc + dot(kt_scr[:, rows], d_score)

    dq_t = back(tail, jnp.zeros((HEAD, block), F32))
    dq_t = over_keys(back, dq_t)
    dqo[...] = jnp.concatenate([dq_t, out_t], axis=0).T.astype(BF)

    @pl.when(step == pl.num_programs(0) - 1)
    def _():
        dkva[...] = acc_scr[:, 0:half_a].T
        dkvb[...] = acc_scr[:, half_a:keys].T.astype(BF)
        dctx[...] = acc_scr[:, keys:total].T


def attend(live, recv, kva, kvb, ctx, deps):
    queries = recv.shape[0]
    block = min(1024, queries)
    half_a, half_b, extra = recv.shape[0] if kva is recv else kva.shape[0], kvb.shape[0], ctx.shape[0]
    total = half_a + half_b + extra
    whole = lambda shape: pl.BlockSpec(shape, lambda n: (0, 0))
    kernel = functools.partial(attend_kernel, chunk=512, unroll=8)

    def inner(*refs):
        kernel(*refs[:5], *refs[5 + len(deps) :])

    return pl.pallas_call(
        inner,
        grid=(queries // block,),
        in_specs=[
            pl.BlockSpec(memory_space=pltpu.SMEM),
            pl.BlockSpec((block, LANES), lambda n: (n, 1)),
            whole((half_a, LANES)),
            whole((half_b, LANES)),
            whole((extra, LANES)),
        ]
        + [pl.BlockSpec(memory_space=pl.ANY)] * len(deps),
        out_specs=[
            pl.BlockSpec((block, LANES), lambda n: (n, 0)),
            whole((half_a, LANES)),
            whole((half_b, LANES)),
            whole((extra, LANES)),
        ],
        out_shape=[
            jax.ShapeDtypeStruct((queries, LANES), BF),
            jax.ShapeDtypeStruct((half_a, LANES), F32),
            jax.ShapeDtypeStruct((half_b, LANES), BF),
            jax.ShapeDtypeStruct((extra, LANES), F32),
        ],
        scratch_shapes=[
            pltpu.VMEM((total, LANES), BF),
            pltpu.VMEM((HEAD, total), BF),
            pltpu.VMEM((HEAD + 16, total), BF),
            pltpu.VMEM((total, block), F32),
            pltpu.VMEM((total, block), BF),
            pltpu.VMEM((LANES, total), F32),
        ],
        compiler_params=pltpu.CompilerParams(vmem_limit_bytes=VMEM_BYTES),
        cost_estimate=pl.CostEstimate(
            flops=int(38 * 1.15e9), bytes_accessed=1, transcendentals=0
        ),
    )(live, recv, kva, kvb, ctx, *deps)


def call(kernel, args, outs, scratch=(), deps=(), time=0.0):
    in_vmem = pl.BlockSpec(memory_space=pltpu.VMEM)
    in_smem = pl.BlockSpec(memory_space=pltpu.SMEM)
    anywhere = pl.BlockSpec(memory_space=pl.ANY)
    count = len(args)

    def inner(*refs):
        kernel(*refs[:count], *refs[count + len(deps) :])

    return pl.pallas_call(
        inner,
        in_specs=[in_smem] + [in_vmem] * (count - 1) + [anywhere] * len(deps),
        out_specs=[in_vmem] * len(outs),
        out_shape=[jax.ShapeDtypeStruct(s, d) for s, d in outs],
        scratch_shapes=[pltpu.VMEM(s, d) for s, d in scratch],
        compiler_params=pltpu.CompilerParams(vmem_limit_bytes=VMEM_BYTES),
        cost_estimate=pl.CostEstimate(
            flops=1 + int(time * 1.15e9), bytes_accessed=1, transcendentals=0
        ),
    )(*args, *deps)


def after(values, *deps):
    anywhere = pl.BlockSpec(memory_space=pl.ANY)
    count = len(values)

    def inner(*refs):
        pass

    return pl.pallas_call(
        inner,
        in_specs=[anywhere] * (count + len(deps)),
        out_specs=[anywhere] * count,
        out_shape=[jax.ShapeDtypeStruct(v.shape, v.dtype) for v in values],
        input_output_aliases={n: n for n in range(count)},
        cost_estimate=pl.CostEstimate(flops=1, bytes_accessed=1, transcendentals=0),
    )(*values, *deps)


def embed_features(timesteps, image_embed):
    half_width = image_embed.shape[1] // 2
    freqs = jnp.exp(-math.log(10000.0) * jnp.arange(half_width, dtype=F32) / half_width)
    angles = timesteps.astype(F32)[:, None] * freqs[None, :]
    return jax.nn.silu(jnp.concatenate([jnp.cos(angles), jnp.sin(angles)], axis=1) + image_embed)


def body(
    block_input,
    cotangent,
    image_embed,
    timesteps,
    text_len,
    context,
    conv1_weight,
    conv2_weight,
    embed_weight,
    embed_bias,
    norm1_gain,
    norm1_bias,
    norm2_gain,
    norm2_bias,
    norm3_gain,
    norm3_bias,
    qkv_weight,
    out_weight,
    ctx_weight,
):
    images, row_count, col_count, width = block_input.shape
    channels = qkv_weight.shape[0]
    size = channels // GROUPS
    blocks = lax.axis_size("blk")
    pix = row_count * col_count
    cells = float(pix * blocks * size)
    split = blocks // 4
    ctx_len = context.shape[1]
    b = lax.axis_index("blk")
    z = lax.axis_index("ch")
    h, i = z % 2, z // 2
    row, rows_all = b * row_count, blocks * row_count
    inside = [row >= 1, row + row_count < rows_all, row >= 2, row + row_count + 1 < rows_all]
    scal = jnp.stack([h, i] + [flag.astype(jnp.int32) for flag in inside] + [z, b]).astype(jnp.int32)


    def over_ch(value, mask):
        return lax.ppermute(value, "ch", [(n, n ^ mask) for n in range(4)])

    def over_blk(value, mask):
        return lax.ppermute(value, "blk", [(n, n ^ mask) for n in range(blocks)])

    def ring(value, step):
        return lax.ppermute(value, "blk", [(n, (n + step) % blocks) for n in range(blocks)])

    def halo(first, last):
        if row_count >= 2:
            return ring(last, 1), ring(first, -1)
        return (
            jnp.concatenate([ring(last, 2), ring(last, 1)], axis=0),
            jnp.concatenate([ring(first, -1), ring(first, -2)], axis=0),
        )

    pairs = [[n * 4 + 2 * m + k for n in range(blocks) for k in range(2)] for m in range(2)]

    def to_image(value):
        return lax.all_to_all(value, ("blk", "ch"), 0, 0, axis_index_groups=pairs)

    def by_image(first, second):
        return jnp.where(i == 0, first, second), jnp.where(i == 0, second, first)

    def plane(value):
        mine = [value] + [over_blk(value, 2 * mask) for mask in (1, 2, 3)]
        return mine + [over_blk(piece, 1) for piece in mine]

    w1_own = conv1_weight.reshape(-1, width)
    w2_own = conv2_weight.reshape(-1, width)
    heads = lambda v: v.reshape(channels, 2, HEAD)
    wp_own = jnp.stack(
        [
            jnp.concatenate([heads(qkv_weight[:, 1]), heads(qkv_weight[:, 2])], axis=2),
            jnp.concatenate([heads(qkv_weight[:, 0] * 0.125), heads(out_weight.T)], axis=2),
        ],
        axis=0,
    )
    wp_own = jnp.transpose(wp_own, (2, 0, 1, 3)).reshape(-1, LANES)
    w1_rows, w2_rows, wp_rows = (w.shape[0] // blocks for w in (w1_own, w2_own, wp_own))
    chunk_of = lambda w: lax.dynamic_slice_in_dim(w, b * (w.shape[0] // blocks), w.shape[0] // blocks, 0)
    w1_slice = chunk_of(w1_own)

    emb_act = embed_features(timesteps, image_embed).astype(BF)
    scale_shift = (
        jnp.einsum("ie,esc->isc", emb_act, embed_weight, preferred_element_type=F32) + embed_bias
    )
    local_vec = jnp.concatenate(
        [
            jnp.zeros((2, width), F32),
            jnp.stack([norm1_gain, norm1_bias, norm2_gain, norm2_bias, norm3_gain, norm3_bias]),
            scale_shift.reshape(4, width),
            jnp.zeros((4, width), F32),
        ],
        axis=0,
    )
    x_mine, x_theirs = call(
        image_split_kernel,
        [scal, block_input.reshape(images, pix, width)],
        [((pix, width), BF)] * 2,
        deps=[w1_slice],
    )
    w1_chunk = over_ch(w1_slice, 2)
    x_two, x_one = over_ch(x_theirs, 2), over_ch(x_mine, 1)
    x_three = over_ch(x_two, 1)
    if blocks == 8:
        w1_pieces = plane(w1_chunk)
    else:
        w1_pieces = [lax.all_gather(w1_chunk, "blk", axis=0, tiled=True)]
    x_sums = call(
        functools.partial(input_sums_kernel, blocks=blocks),
        [scal, block_input.reshape(images, pix, width), local_vec],
        [((4 * blocks, 16, width), F32)],
        deps=[x_mine],
    )[0]
    sums1 = lax.all_to_all(x_sums, ("blk", "ch"), 0, 0)
    two_source = jnp.concatenate([chunk_of(w2_own), chunk_of(wp_own)], axis=0)
    (two_source,) = after((two_source,), x_two, x_one, x_sums)
    two_chunk = over_ch(two_source, 2)
    (two_chunk,) = after((two_chunk,), x_three, *w1_pieces[1:4])
    wide = dict(axis=1)
    x_own = jnp.concatenate(by_image(x_mine, x_two), **wide)
    x_oth = jnp.concatenate(by_image(x_one, x_three), **wide)
    edge = min(2 * COLS, pix)
    x_top, x_bot = halo(
        jnp.concatenate([x_own[:edge], x_oth[:edge]], **wide),
        jnp.concatenate([x_own[pix - edge :], x_oth[pix - edge :]], **wide),
    )
    if blocks == 8:
        w1 = call(join_kernel, [scal, w1_own] + w1_pieces, [((w1_own.shape[0], HALF), BF)])[0]
    else:
        w1_oth = w1_pieces[0]
        w1 = jnp.concatenate(by_image(w1_own, w1_oth), **wide)
    two = lax.all_gather(two_chunk, "blk", axis=0)
    w2 = call(
        functools.partial(place_weight_kernel, start=0, width=1),
        [scal, w2_own, two],
        [((w2_own.shape[0], HALF), BF)],
    )[0]
    j = b // split
    ctx_rows = -(-ctx_len // 16) * 16
    ctx_w = jnp.stack(
        [
            lax.dynamic_slice_in_dim(
                ctx_weight, 128 * (hh + 2 * (j // 2)) + HEAD * (j % 2), HEAD, 2
            ).reshape(-1, 2 * HEAD)
            for hh in range(2)
        ]
    )
    ctx_term = jnp.einsum("itx,hxk->ihtk", context, ctx_w, preferred_element_type=F32)
    ctx_term = jnp.pad(
        ctx_term.astype(BF).reshape(4, ctx_len, 2 * HEAD),
        ((0, 0), (0, ctx_rows - ctx_len), (0, 0)),
    )
    ctx_kv = lax.psum_scatter(ctx_term, "ch", scatter_dimension=0)
    live = (CLIPTOK + jnp.where(i == 0, text_len[0], text_len[1])).astype(jnp.int32)[None]

    emb_f = jnp.repeat(emb_act.astype(F32), 2, axis=1)
    odd = (jnp.arange(emb_f.shape[1]) % 2)[None]
    emb_rows = jnp.concatenate(
        [emb_f * (1 - odd), emb_f * odd, jnp.zeros((4, emb_f.shape[1]), F32)], axis=0
    )
    kind = dict(cells=cells, size=size)
    ext = pix + 2 * COLS
    stat_shape = ((2 * blocks, 8, HALF), F32)

    c_mine, c_theirs = call(
        image_split_kernel,
        [scal, cotangent.reshape(images, pix, width)],
        [((pix, width), BF)] * 2,
        deps=[x_sums],
    )

    hid_own, hid_stat, act1, vec = call(
        functools.partial(conv1_kernel, **kind),
        [scal, x_own, x_oth, x_top, x_bot, sums1, w1],
        [((ext, HALF), BF), stat_shape, ((pix, channels), BF), ((4, 16, LANES), F32)],
        [((ext + 2 * COLS, channels), BF)],
        deps=[ctx_term, c_mine, emb_rows, live],
    )
    hid_oth = over_ch(hid_own, 1)
    sums2 = to_image(hid_stat)

    c_mine, c_theirs = after((c_mine, c_theirs), hid_oth, w2)
    c_one, c_two = over_ch(c_mine, 1), over_ch(c_theirs, 2)
    c_three = over_ch(c_two, 1)
    cot_own = jnp.concatenate(by_image(c_mine, c_two), **wide)
    cot_oth = jnp.concatenate(by_image(c_one, c_three), **wide)

    edges = ((2, edge, HALF), BF)
    res_f, res_own, res_stat, act_first, act_rest, res_edges = call(
        functools.partial(conv2_kernel, **kind),
        [scal, hid_own, hid_oth, sums2, vec, w2, x_own, act1],
        [
            ((pix, HALF), F32),
            ((pix, HALF), BF),
            stat_shape,
            ((pix // 2, channels), BF),
            ((pix + pix // 2, channels), BF),
            edges,
        ],
        [((ext, channels), BF)],
    )
    res_oth = over_ch(res_own, 1)
    sums3 = to_image(res_stat)
    wp = call(
        functools.partial(place_weight_kernel, start=w2_rows, width=4),
        [scal, wp_own, two],
        [((channels, 4 * HALF), BF)],
        deps=[res_oth],
    )[0]
    packed, act3, cot_all, cot_edges = call(
        functools.partial(qkv_kernel, **kind),
        [scal, res_own, res_oth, sums3, vec, cot_own, cot_oth, wp],
        [((4, pix, HALF), BF), ((pix, channels), BF), ((pix, channels), BF), edges],
        deps=[ctx_kv],
    )
    recv = lax.all_to_all(packed.reshape(blocks, pix // split, HALF), "blk", 0, 0)
    res_edges, act_first = after((res_edges, act_first), packed)
    res_top, res_bot = halo(res_edges[0], res_edges[1])
    cot_top, cot_bot = halo(cot_edges[0], cot_edges[1])
    first_there = over_ch(act_first, 2)
    (recv,) = after((recv,), res_top, res_bot, cot_top, cot_bot, first_there)
    recv = recv.reshape(-1, HALF)
    rest_there = over_ch(act_rest, 2)
    if split == 2:
        kva, kvb = recv, over_blk(recv[:, :LANES], 1)
    else:
        groups = [[n * split + m for m in range(split)] for n in range(4)]
        kv_all = lax.all_gather(
            recv[:, :LANES], "blk", axis=0, tiled=True, axis_index_groups=groups
        )
        kva, kvb = kv_all[: kv_all.shape[0] // 2], kv_all[kv_all.shape[0] // 2 :]
    dqo, dkva, dkvb, dctx = attend(live, recv, kva, kvb, ctx_kv, [])
    if split == 2:
        d_ctx = dctx + over_blk(dctx, 1)
        back = call(
            merge_kernel,
            [scal, dkva, over_blk(dkvb, 1), dqo],
            [((dqo.shape[0], HALF), BF)],
            deps=[rest_there],
        )[0]
    else:
        d_ctx = lax.psum(dctx, "blk", axis_index_groups=groups)
        d_kv = lax.psum_scatter(
            jnp.concatenate([dkva, dkvb.astype(F32)], axis=0),
            "blk",
            scatter_dimension=0,
            axis_index_groups=groups,
            tiled=True,
        )
        back = jnp.concatenate([d_kv.astype(BF), dqo], axis=1)
    grads = lax.all_to_all(back.reshape(blocks, pix // split, HALF), "blk", 0, 0)
    grads = grads.reshape(4, pix, HALF)

    features = context.shape[2] // split
    d_ctx = d_ctx[:ctx_len].astype(BF)
    ctx_part = call(
        functools.partial(context_grad_kernel, split=split),
        [scal, context, d_ctx] + [over_ch(d_ctx, mask) for mask in (1, 2, 3)],
        [((features, HALF), BF)],
        [((context.shape[2], HALF), F32)],
    )[0]
    ctx_all = lax.all_gather(ctx_part, "blk", axis=0)

    def low_grad(rows):
        return [((rows, HALF), F32), ((rows, HALF), BF), stat_shape]

    p3_own, p3_oth, st3 = call(
        functools.partial(qkv_back_kernel, **kind),
        [scal, grads, wp, res_own, res_oth, sums3, vec],
        low_grad(pix),
        [((pix, channels), F32)],
        deps=[ctx_part],
    )
    r3 = over_ch(p3_oth, 1)
    stats3 = to_image(st3)
    proj_own, proj_oth, wp_part = call(
        out_kernel,
        [scal, grads, wp, act3, cot_all],
        [((pix, HALF), F32), ((pix, HALF), BF), ((2, 4 * channels, LANES), BF)],
        [((pix, channels), F32)],
        deps=[r3],
    )
    first3 = (p3_own[:edge] + r3[:edge].astype(F32)).astype(BF)
    last3 = (p3_own[pix - edge :] + r3[pix - edge :].astype(F32)).astype(BF)
    d_top3, d_bot3 = halo(first3, last3)
    d_resid, ext2, away2 = call(
        functools.partial(norm3_back_kernel, **kind),
        [
            scal, p3_own, r3, d_top3, d_bot3, res_own, res_top, res_bot, cot_own, cot_top, cot_bot,
            sums3, stats3, vec,
        ],
        [((pix, HALF), F32), ((ext + 2 * COLS, HALF), BF), ((ext, LANES), BF)],
        deps=[proj_own],
    )
    there2 = over_ch(away2, 2)
    p2_own, p2_oth, st2 = call(
        functools.partial(conv_back_kernel, which=1, **kind),
        [scal, ext2, w2, hid_own, hid_oth, sums2, vec],
        low_grad(ext),
        [((ext, channels), F32)],
        time=8.0,
    )
    r2 = over_ch(p2_oth, 1)
    (st2,) = after((st2,), there2)
    stats2 = to_image(st2)
    conv_rows, wp_rows = 9 * channels // blocks, 4 * channels // blocks
    part2 = call(
        weight_grad_two_kernel,
        [scal, act_rest, rest_there, ext2, there2, wp_part],
        [((blocks, conv_rows + 2 * wp_rows, LANES), BF)],
        [((2 * pix, 9 * LANES), BF), ((9 * channels, LANES), F32)],
        deps=[r2],
    )[0]
    ext1, away1 = call(
        functools.partial(norm2_back_kernel, **kind),
        [scal, p2_own, r2, hid_own, sums2, stats2, vec],
        [((ext, HALF), BF), ((ext, LANES), BF)],
        deps=[part2, ctx_all],
    )
    parts2 = lax.all_to_all(part2, "blk", 0, 0)
    there1 = over_ch(away1, 2)
    p1_own, p1_oth, st1 = call(
        functools.partial(conv_back_kernel, which=0, **kind),
        [scal, ext1, w1, x_own, x_oth, sums1, vec],
        low_grad(pix),
        [((pix, channels), F32)],
        time=8.0,
    )
    (st1,) = after((st1,), there1, parts2)
    (proj_late,) = after((proj_oth,), there1)
    r1 = over_ch(p1_oth, 1)
    stats1 = to_image(st1)
    half_shape = (4, 9 * channels // 8, LANES)
    keep1, send1 = call(
        weight_grad_one_kernel,
        [scal, act_first, act_rest, first_there, rest_there, ext1, there1],
        [(half_shape, F32), (half_shape, BF)],
        [((2 * pix, 9 * LANES), BF), ((9 * channels, LANES), F32)],
        deps=[p1_own],
        time=20.0,
    )
    if blocks == 8:
        own1, *sends = call(
            scatter_kernel,
            [scal, keep1, over_blk(send1, 1)],
            [((conv_rows, LANES), F32)] + [((conv_rows, LANES), BF)] * 3,
        )
    else:
        own1 = keep1
    if blocks == 8:
        other = call(other_sum_kernel, [scal, parts2], [((wp_rows, LANES), BF)], deps=[own1])[0]
        total = call(
            total_kernel,
            [scal, own1, parts2, over_ch(other, 2)]
            + [over_blk(v, 2 * n + 2) for n, v in enumerate(sends)],
            [((2 * conv_rows + wp_rows, LANES), BF)],
        )[0]
    else:
        total = own1
    out_keep, out_send = call(
        out_add_kernel,
        [scal, res_f, proj_own, over_ch(proj_late, 1)],
        [((pix, width), BF)] * 2,
        deps=[total],
    )
    in_keep, in_send = call(
        functools.partial(last_kernel, **kind),
        [scal, p1_own, r1, x_own, sums1, stats1, vec, d_resid],
        [((pix, width), F32), ((pix, width), BF)],
        [((pix, HALF), F32)],
        deps=[total],
        time=40.0,
    )
    sums_here, sums_away = call(
        channel_sums_kernel,
        [scal, stats1, stats2, stats3],
        [((8, LANES), F32)] * 2,
        deps=[total],
    )
    sums_recv = over_ch(sums_away, 2)
    out_recv, in_recv = over_ch(out_send, 2), over_ch(in_send, 2)
    bias_grad, *smalls, embed_weight_grad = call(
        channel_grads_kernel,
        [scal, sums_here, sums_recv, local_vec, emb_rows],
        [((2, LANES), F32)] + [((1, LANES), F32)] * 6 + [((emb_rows.shape[1], LANES), F32)],
        deps=[total],
        time=15.0,
    )
    block_output, input_grad = call(
        by_images_kernel,
        [scal, out_keep, out_recv, in_keep, in_recv],
        [((images, pix, width), BF), ((images, pix, width), F32)],
        deps=[total],
        time=10.0,
    )
    if blocks == 8:
        ctx_grad = call(
            functools.partial(context_place_kernel, split=split),
            [scal, ctx_all],
            [((context.shape[2], 2, channels), F32)],
            deps=[total],
            time=10.0,
        )[0]
        grad1, grad2, qkv_grad, out_grad = call(
            place_kernel,
            [scal] + plane(total),
            [((9 * channels, LANES), F32)] * 2
            + [((3 * channels, LANES), F32), ((LANES, channels), F32)],
            deps=[block_output, ctx_grad, bias_grad],
        )
    else:
        ctx_grad = ctx_all.reshape(2, 2, split, features, 2, 2, HEAD)
        ctx_grad = jnp.transpose(ctx_grad, (2, 3, 5, 0, 4, 1, 6)).astype(F32)
        flip = lambda c: jnp.where(b % 2 == 0, *((keep1.astype(BF), send1)[:: 1 - 2 * c]))
        grad1 = lax.psum(jnp.concatenate([flip(0), flip(1)], axis=0), "blk").astype(F32)
        sums = lax.psum(part2, "blk").astype(F32)
        cut = conv_rows + wp_rows
        grad2 = sums[:, :conv_rows]
        wp_grad = sums[:, conv_rows:cut] + over_ch(sums[:, cut:].astype(BF), 2).astype(F32)
        wp_grad = wp_grad.reshape(-1, LANES)
        qkv_grad, out_grad = wp_grad[: 3 * channels], wp_grad[3 * channels :]
        out_grad = jnp.concatenate(list(out_grad.reshape(-1, LANES, LANES)), axis=1)
    qkv_grad = jnp.transpose(qkv_grad.reshape(3, channels, LANES), (1, 0, 2))

    return (
        block_output.reshape(block_input.shape),
        input_grad.reshape(block_input.shape),
        grad1.reshape(conv1_weight.shape),
        grad2.reshape(conv2_weight.shape),
        embed_weight_grad.reshape(embed_weight.shape),
        bias_grad,
        *(value.reshape(width) for value in smalls),
        qkv_grad,
        out_grad,
        ctx_grad.reshape(ctx_weight.shape),
    )


def solution(mesh):
    return jax.shard_map(
        body,
        mesh=mesh,
        in_specs=(
            P(None, "blk", None, "ch"),
            P(None, "blk", None, "ch"),
            P(),
            P(),
            P(),
            P(None, None, "ch"),
            P(None, None, None, "ch"),
            P(None, None, None, "ch"),
            P(None, None, "ch"),
            P(None, "ch"),
            P("ch"),
            P("ch"),
            P("ch"),
            P("ch"),
            P("ch"),
            P("ch"),
            P(None, None, "ch"),
            P("ch", None),
            P("ch", None, None),
        ),
        out_specs=(
            P(None, "blk", None, "ch"),
            P(None, "blk", None, "ch"),
            P(None, None, None, "ch"),
            P(None, None, None, "ch"),
            P(None, None, "ch"),
            P(None, "ch"),
            P("ch"),
            P("ch"),
            P("ch"),
            P("ch"),
            P("ch"),
            P("ch"),
            P(None, None, "ch"),
            P("ch", None),
            P("ch", None, None),
        ),
        check_vma=False,
    )
```

profile of v0, /device:TPU:0, one launch (start us, length us, event | category | flops | bytes accessed | tf_op | source)
XLA Modules:
  0.0 344.2 jit_solution(15843482330248277971)
XLA Ops:
  9.1 4.1 %collective-permute-start.5 = (bf16[576,128]{1,0:T(8,128)(2,1)S(1)}, bf16[576,128]{1,0:T(8,128)(2,1)}, u32[]{:S(2)}, u32[]{:S(2)}) collective-permute-start(bf16[576,128]{1,0:T(8,128)(2,1)S(1)} %constant_dynamic-slice_fusion.4.refs_2_), channel_id=1, source_target_pairs={{0,2},{1,3},{2,0},{3,1},{4,6},{5,7},{6,4},{7,5},{8,10},{9,11},{10,... | collective-permute-start | bytes 442376 | tf_op jit(solution)/shard_map/ppermute | solution.py:833
  13.8 1.7 shard_map.298
  18.1 2.0 concatenate.41.refs_2_.refs_3_
  20.1 1.9 collective-permute-start.1
  22.0 1.8 shard_map.299.refs_2_.refs_3_
  23.8 4.8 %all-to-all-start = ((f32[32,16,128]{2,1,0:T(8,128)}), f32[32,16,128]{2,1,0:T(8,128)S(1)}, u32[]{:S(2)}, u32[]{:S(2)}) async-start(f32[32,16,128]{2,1,0:T(8,128)} %shard_map.299.refs_2_.refs_3_), calls=%async_computation | async-start | bytes 524288 | tf_op jit(solution)/shard_map/all_to_all | solution.py:908
  34.3 2.7 collective-permute-start.14
  42.6 1.7 shard_map.301
  52.2 2.2 collective-permute-start.4
  57.8 3.5 %shard_map.300.refs_6_.refs_2_ = bf16[4608,256]{1,0:T(8,128)(2,1)} custom-call(s32[8]{0:T(128)} %stack.81.refs_0_, bf16[4608,128]{1,0:T(8,128)(2,1)} %bitcast.92, bf16[576,128]{1,0:T(8,128)(2,1)} %collective-permute-done.5.refs_2_, bf16[576,128]{1,0:T(8,128)(2,1)} %copy-done.22, bf16[576,128]{1,0:T(8,128)(2,1)} %collective-permute-done.7.refs_4_.refs_3_, ...), custom_call_target="tpu_custom_call" | custom-call | flops 1 | bytes 1 | tf_op jit(solution)/shard_map/pallas_call | solution.py:758
  62.1 5.5 %shard_map.302 = (bf16[640,256]{1,0:T(8,128)(2,1)}, f32[16,8,256]{2,1,0:T(8,128)}, bf16[512,512]{1,0:T(8,128)(2,1)}, f32[4,16,128]{2,1,0:T(8,128)}) custom-call(s32[8]{0:T(128)} %stack.81.refs_0_, bf16[512,256]{1,0:T(8,128)(2,1)} %pad_maximum_fusion.refs_1_.refs_6_.refs_3_, bf16[512,256]{1,0:T(8,128)(2,1)} %pad_maximum_fusion.1.refs_2_.refs_4_, ...), custom_call_target="tpu_custom_call" | custom-call | flops 1 | bytes 1 | tf_op jit(solution)/shard_map/pallas_call | solution.py:758
  68.2 3.8 %all-to-all-start.1 = ((f32[16,8,256]{2,1,0:T(8,128)}), f32[16,8,256]{2,1,0:T(8,128)S(1)}, u32[]{:S(2)}, u32[]{:S(2)}) async-start(f32[16,8,256]{2,1,0:T(8,128)} %get-tuple-element.88), calls=%async_computation.1 | async-start | bytes 262144 | tf_op jit(solution)/shard_map/all_to_all | solution.py:852
  72.1 3.5 %all-gather.5.cloned.1.call-done = bf16[6656,128]{1,0:T(8,128)(2,1)} async-done(((bf16[832,128]{1,0:T(8,128)(2,1)}), bf16[6656,128]{1,0:T(8,128)(2,1)}) %all-gather.5.cloned.1.call-update) | async-done | bytes 1703952 | tf_op jit(solution)/shard_map/all_gather | solution.py:926
  75.6 3.6 %shard_map.305.refs_5_.refs_3_.refs_2_ = bf16[4608,256]{1,0:T(8,128)(2,1)} custom-call(s32[8]{0:T(128)} %stack.81.refs_0_, bf16[4608,128]{1,0:T(8,128)(2,1)} %bitcast.94, bf16[8,832,128]{2,1,0:T(8,128)(2,1)} %bitcast.82), custom_call_target="tpu_custom_call" | custom-call | flops 1 | bytes 1 | tf_op jit(solution)/shard_map/pallas_call | solution.py:758
  80.0 2.4 collective-permute-start.16
  83.1 5.5 %shard_map.306 = (f32[512,256]{1,0:T(8,128)}, bf16[512,256]{1,0:T(8,128)(2,1)}, f32[16,8,256]{2,1,0:T(8,128)}, bf16[256,512]{1,0:T(8,128)(2,1)}, bf16[768,512]{1,0:T(8,128)(2,1)}, /*index=5*/bf16[2,128,256]{2,1,0:T(8,128)(2,1)}) custom-call(s32[8]{0:T(128)} %stack.81.refs_0_, bf16[640,256]{1,0:T(8,128)(2,1)} %get-tuple-element.87.refs_1_.refs_3_, ...), custom_call_target="tpu_custom_call" | custom-call | flops 1 | bytes 1 | tf_op jit(solution)/shard_map/pallas_call | solution.py:758
  90.0 14.8 %all-to-all-start.2 = ((f32[16,8,256]{2,1,0:T(8,128)}), f32[16,8,256]{2,1,0:T(8,128)S(1)}, u32[]{:S(2)}, u32[]{:S(2)}) async-start(f32[16,8,256]{2,1,0:T(8,128)} %get-tuple-element.93), calls=%async_computation.2 | async-start | bytes 262144 | tf_op jit(solution)/shard_map/all_to_all | solution.py:852
  104.8 1.7 collective-permute-start.17
  108.4 2.9 shard_map.308.refs_7_.refs_2_
  112.3 2.3 collective-permute-done.18
  116.0 4.3 %shard_map.309 = (bf16[4,512,256]{2,1,0:T(8,128)(2,1)}, bf16[512,512]{1,0:T(8,128)(2,1)}, bf16[512,512]{1,0:T(8,128)(2,1)}, bf16[2,128,256]{2,1,0:T(8,128)(2,1)}) custom-call(s32[8]{0:T(128)} %stack.81.refs_0_, bf16[512,256]{1,0:T(8,128)(2,1)} %get-tuple-element.92.refs_1_.refs_3_.refs_5_, bf16[512,256]{1,0:T(8,128)(2,1)} %copy-done.8, ...), custom_call_target="tpu_custom_call" | custom-call | flops 1 | bytes 1 | tf_op jit(solution)/shard_map/pallas_call | solution.py:758
  120.4 3.9 %all-to-all-start.3 = ((bf16[8,256,256]{2,1,0:T(8,128)(2,1)}), bf16[8,256,256]{2,1,0:T(8,128)(2,1)S(1)}, u32[]{:S(2)}, u32[]{:S(2)}) async-start(bf16[8,256,256]{2,1,0:T(8,128)(2,1)} %bitcast.87), calls=%async_computation.4 | async-start | bytes 2097152 | tf_op jit(solution)/shard_map/all_to_all | solution.py:1010
  125.7 2.2 collective-permute-start.20
  128.6 2.6 collective-permute-start.22
  131.2 9.3 %collective-permute-done.19.refs_1_.refs_6_ = bf16[128,256]{1,0:T(8,128)(2,1)S(1)} collective-permute-done((bf16[128,256]{1,0:T(8,128)(2,1)S(1)}, bf16[128,256]{1,0:T(8,128)(2,1)S(1)}, u32[]{:S(2)}, u32[]{:S(2)}) %collective-permute-start.19) | collective-permute-done | bytes 65568 | tf_op jit(solution)/shard_map/ppermute | solution.py:839
  147.9 33.4 %shard_map.312 = (bf16[2048,128]{1,0:T(8,128)(2,1)}, f32[2048,128]{1,0:T(8,128)}, bf16[2048,128]{1,0:T(8,128)(2,1)}, f32[272,128]{1,0:T(8,128)}) custom-call(s32[1]{0:T(128)} %bitcast.28.refs_10_.refs_0_, bf16[2048,256]{1,0:T(8,128)(2,1)} %bitcast.85, bf16[2048,256]{1,0:T(8,128)(2,1)} %bitcast.86, bf16[2048,128]{1,0:T(8,128)(2,1)} %copy-done.73, ...), custom_call_target="tpu_custom_call" | custom-call | flops 43699998720 | bytes 1 | tf_op jit(solution)/shard_map/pallas_call | solution.py:711
  184.3 2.7 shard_map.313
  187.0 3.7 %all-to-all-start.4 = ((bf16[8,256,256]{2,1,0:T(8,128)(2,1)}), bf16[8,256,256]{2,1,0:T(8,128)(2,1)S(1)}, u32[]{:S(2)}, u32[]{:S(2)}) async-start(bf16[8,256,256]{2,1,0:T(8,128)(2,1)} %bitcast.88), calls=%async_computation.5 | async-start | bytes 2097152 | tf_op jit(solution)/shard_map/all_to_all | solution.py:1045
  193.7 3.0 collective-permute-start.30
  197.7 3.4 collective-permute-done.29.refs_4_
  202.3 2.5 shard_map.314.refs_7_
  207.0 3.5 %shard_map.315 = (f32[512,256]{1,0:T(8,128)}, bf16[512,256]{1,0:T(8,128)(2,1)}, f32[16,8,256]{2,1,0:T(8,128)}) custom-call(s32[8]{0:T(128)} %stack.81.refs_0_, bf16[4,512,256]{2,1,0:T(8,128)(2,1)} %bitcast.80, bf16[512,1024]{1,0:T(8,128)(2,1)} %shard_map.308.refs_7_.refs_2_, bf16[512,256]{1,0:T(8,128)(2,1)} %get-tuple-element.92.refs_1_.refs_3_.refs_5_, ...), custom_call_target="tpu_custom_call" | custom-call | flops 1 | bytes 1 | tf_op jit(solution)/shard_map/pallas_call | solution.py:758
  210.7 4.4 %all-to-all-start.5 = ((f32[16,8,256]{2,1,0:T(8,128)}), f32[16,8,256]{2,1,0:T(8,128)S(1)}, u32[]{:S(2)}, u32[]{:S(2)}) async-start(f32[16,8,256]{2,1,0:T(8,128)} %get-tuple-element.114), calls=%async_computation.6 | async-start | bytes 262144 | tf_op jit(solution)/shard_map/all_to_all | solution.py:852
  215.2 1.9 collective-permute-done.31.refs_5_.refs_2_
  218.2 2.6 collective-permute-start.33
  220.9 4.9 %shard_map.316 = (f32[512,256]{1,0:T(8,128)}, bf16[512,256]{1,0:T(8,128)(2,1)}, bf16[2,2048,128]{2,1,0:T(8,128)(2,1)}) custom-call(s32[8]{0:T(128)} %stack.81.refs_0_, bf16[4,512,256]{2,1,0:T(8,128)(2,1)} %bitcast.81, bf16[512,1024]{1,0:T(8,128)(2,1)} %shard_map.308.refs_7_.refs_2_, bf16[512,512]{1,0:T(8,128)(2,1)} %get-tuple-element.107.refs_3_, ...), custom_call_target="tpu_custom_call" | custom-call | flops 1 | bytes 1 | tf_op jit(solution)/shard_map/pallas_call | solution.py:758
  226.5 3.1 shard_map.317
  229.6 1.7 collective-permute-start.35
  231.3 5.3 %shard_map.318 = (f32[640,256]{1,0:T(8,128)}, bf16[640,256]{1,0:T(8,128)(2,1)}, f32[16,8,256]{2,1,0:T(8,128)}) custom-call(s32[8]{0:T(128)} %stack.81.refs_0_, bf16[768,256]{1,0:T(8,128)(2,1)} %get-tuple-element.115.refs_1_.refs_3_, bf16[4608,256]{1,0:T(8,128)(2,1)} %shard_map.305.refs_5_.refs_3_.refs_2_, ...), custom_call_target="tpu_custom_call" | custom-call | flops 9200000000 | bytes 1 | tf_op jit(solution)/shard_map/pallas_call | solution.py:758
  236.8 3.2 collective-permute-done.35.refs_1_.refs_4_
  240.7 3.5 %all-to-all-start.6 = ((f32[16,8,256]{2,1,0:T(8,128)}), f32[16,8,256]{2,1,0:T(8,128)S(1)}, u32[]{:S(2)}, u32[]{:S(2)}) async-start(f32[16,8,256]{2,1,0:T(8,128)} %shard_map.319), calls=%async_computation.7 | async-start | bytes 262144 | tf_op jit(solution)/shard_map/all_to_all | solution.py:852
  244.2 2.7 collective-permute-done.34.refs_6_.refs_2_
  247.7 5.0 %shard_map.320.refs_7_ = bf16[8,1088,128]{2,1,0:T(8,128)(2,1)} custom-call(s32[8]{0:T(128)} %stack.81.refs_0_, bf16[768,512]{1,0:T(8,128)(2,1)} %get-tuple-element.106.refs_1_.refs_2_, bf16[768,512]{1,0:T(8,128)(2,1)} %copy-done.6, bf16[768,256]{1,0:T(8,128)(2,1)} %get-tuple-element.115.refs_1_.refs_3_, bf16[640,128]{1,0:T(8,128)(2,1)} %copy-done.20, ...), custom_call_target="tpu_custom_call" | custom-call | flops 1 | bytes 1 | tf_op jit(solution)/shard_map/pallas_call | solution.py:758
  253.3 3.8 %all-to-all-start.7 = ((bf16[8,1088,128]{2,1,0:T(8,128)(2,1)}), bf16[8,1088,128]{2,1,0:T(8,128)(2,1)S(1)}, u32[]{:S(2)}, u32[]{:S(2)}) async-start(bf16[8,1088,128]{2,1,0:T(8,128)(2,1)} %shard_map.320.refs_7_), calls=%async_computation.8 | async-start | bytes 4456448 | tf_op jit(solution)/shard_map/all_to_all | solution.py:1114
  257.1 3.1 shard_map.321
  260.6 4.8 %shard_map.323 = (f32[512,256]{1,0:T(8,128)}, bf16[512,256]{1,0:T(8,128)(2,1)}, f32[16,8,256]{2,1,0:T(8,128)}) custom-call(s32[8]{0:T(128)} %stack.81.refs_0_, bf16[640,256]{1,0:T(8,128)(2,1)} %get-tuple-element.122.refs_1_.refs_5_, bf16[4608,256]{1,0:T(8,128)(2,1)} %shard_map.300.refs_6_.refs_2_, bf16[512,256]{1,0:T(8,128)(2,1)} %pad_maximum_fusion.refs_1_.refs_6_.refs_3_, ...), custom_call_target="tpu_custom_call" | custom-call | flops 9200000000 | bytes 1 | tf_op jit(solution)/shard_map/pallas_call | solution.py:758
  265.4 5.0 %collective-permute-done.36.refs_1_.refs_6_ = bf16[640,128]{1,0:T(8,128)(2,1)S(1)} collective-permute-done((bf16[640,128]{1,0:T(8,128)(2,1)}, bf16[640,128]{1,0:T(8,128)(2,1)S(1)}, u32[]{:S(2)}, u32[]{:S(2)}) %collective-permute-start.36) | collective-permute-done | bytes 163872 | tf_op jit(solution)/shard_map/ppermute | solution.py:833
  271.1 4.9 %shard_map.324 = (f32[4,576,128]{2,1,0:T(8,128)}, bf16[4,576,128]{2,1,0:T(8,128)(2,1)}) custom-call(s32[8]{0:T(128)} %stack.81.refs_0_, bf16[256,512]{1,0:T(8,128)(2,1)} %get-tuple-element.102.refs_1_, bf16[768,512]{1,0:T(8,128)(2,1)} %get-tuple-element.106.refs_1_.refs_2_, bf16[256,512]{1,0:T(8,128)(2,1)} %copy-done.44, bf16[768,512]{1,0:T(8,128)(2,1)} %copy-done.6, ...), custom_call_target="tpu_custom_call" | custom-call | flops 23000000512 | bytes 1 | tf_op jit(solution)/shard_map/pallas_call | solution.py:758
  276.2 2.1 collective-permute-done.38.refs_2_
  279.1 2.4 shard_map.325
  281.5 1.7 collective-permute-start.40
  286.5 2.3 shard_map.326
  289.4 2.1 collective-permute-start.44
  291.4 4.1 %all-to-all-start.8 = ((f32[16,8,256]{2,1,0:T(8,128)}), f32[16,8,256]{2,1,0:T(8,128)S(1)}, u32[]{:S(2)}, u32[]{:S(2)}) async-start(f32[16,8,256]{2,1,0:T(8,128)} %shard_map.329), calls=%async_computation.9 | async-start | bytes 262144 | tf_op jit(solution)/shard_map/all_to_all | solution.py:852
  295.6 2.0 collective-permute-start.37
  298.9 2.8 shard_map.327.refs_4_.refs_8_.refs_5_.refs_2_.refs_1_
  305.2 3.8 %shard_map.332.refs_10_ = f32[512,2,512]{2,1,0:T(2,128)} custom-call(s32[8]{0:T(128)} %stack.81.refs_0_, bf16[8,256,256]{2,1,0:T(8,128)(2,1)} %bitcast.97, bf16[1408,128]{1,0:T(8,128)(2,1)} %shard_map.327.refs_4_.refs_8_.refs_5_.refs_2_.refs_1_), custom_call_target="tpu_custom_call" | custom-call | flops 11500000256 | bytes 1 | tf_op jit(solution)/shard_map/pallas_call | solution.py:758
  309.7 2.0 shard_map.328
  311.8 1.7 collective-permute-start.43
  314.1 1.7 shard_map.333
  317.1 3.0 shard_map.330
  321.8 5.1 %shard_map.334 = (f32[2,128]{1,0:T(2,128)}, f32[1,128]{1,0:T(1,128)}, f32[1,128]{1,0:T(1,128)}, f32[1,128]{1,0:T(1,128)}, f32[1,128]{1,0:T(1,128)}, /*index=5*/f...) custom-call(s32[8]{0:T(128)} %stack.81.refs_0_, f32[8,128]{1,0:T(8,128)} %get-tuple-element.139.refs_1_, ...), custom_call_target="tpu_custom_call" | custom-call | flops 17250000896 | bytes 1 | tf_op jit(solution)/shard_map/pallas_call | solution.py:758
  328.7 2.0 shard_map.331
  331.9 4.7 %shard_map.335 = (f32[4608,128]{1,0:T(8,128)}, f32[4608,128]{1,0:T(8,128)}, f32[1536,128]{1,0:T(8,128)}, f32[128,512]{1,0:T(8,128)}) custom-call(s32[8]{0:T(128)} %stack.81.refs_0_, bf16[1408,128]{1,0:T(8,128)(2,1)} %shard_map.327.refs_4_.refs_8_.refs_5_.refs_2_.refs_1_, bf16[1408,128]{1,0:T(8,128)(2,1)} %copy-done.36, bf16[1408,128]{1,0:T(8,128)(2,1)} %copy-done.37, ...), custom_call_target="tpu_custom_call" | custom-call | flops 1 | bytes 1 | tf_op jit(solution)/shard_map/pallas_call | solution.py:758
  (320 shorter events, 75.7 us)
Async XLA Ops:
  9.1 29.3 %collective-permute-start.5 = (bf16[576,128]{1,0:T(8,128)(2,1)S(1)}, bf16[576,128]{1,0:T(8,128)(2,1)}, u32[]{:S(2)}, u32[]{:S(2)}) collective-permute-start(bf16[576,128]{1,0:T(8,128)(2,1)S(1)} %constant_dynamic-slice_fusion.4.refs_2_), channel_id=1, source_target_pairs={{0,2},{1,3},{2,0},{3,1},{4,6},{5,7},{6,4},{7,5},{8,10},{9,11},{10,... | collective-permute-start | bytes 442376 | tf_op jit(solution)/shard_map/ppermute | solution.py:833
  15.5 17.5 %collective-permute-start = (bf16[512,128]{1,0:T(8,128)(2,1)}, bf16[512,128]{1,0:T(8,128)(2,1)S(1)}, u32[]{:S(2)}, u32[]{:S(2)}) collective-permute-start(bf16[512,128]{1,0:T(8,128)(2,1)} %get-tuple-element.85), channel_id=1, source_target_pairs={{0,2},{1,3},{2,0},{3,1},{4,6},{5,7},{6,4},{7,5},{8,10},{9,11},{10,... | collective-permute-start | bytes 393224 | tf_op jit(solution)/shard_map/ppermute | solution.py:833
  20.1 12.8 %collective-permute-start.1 = (bf16[512,128]{1,0:T(8,128)(2,1)}, bf16[512,128]{1,0:T(8,128)(2,1)S(1)}, u32[]{:S(2)}, u32[]{:S(2)}) collective-permute-start(bf16[512,128]{1,0:T(8,128)(2,1)} %get-tuple-element.84.refs_3_), channel_id=1, source_target_pairs={{0,1},{1,0},{2,3},{3,2},{4,5},{5,4},{6,7},{7,6},{8,9},{9,8},{10,11... | collective-permute-start | bytes 393224 | tf_op jit(solution)/shard_map/ppermute | solution.py:833
  23.8 37.6 %all-to-all-start = ((f32[32,16,128]{2,1,0:T(8,128)}), f32[32,16,128]{2,1,0:T(8,128)S(1)}, u32[]{:S(2)}, u32[]{:S(2)}) async-start(f32[32,16,128]{2,1,0:T(8,128)} %shard_map.299.refs_2_.refs_3_), calls=%async_computation | async-start | bytes 524288 | tf_op jit(solution)/shard_map/all_to_all | solution.py:908
  28.6 47.0 %all-gather.5.cloned.1.call-start = ((), (), s32[]{:S(2)}) async-start(), calls=%async_computation.11 | async-start | bytes 1916928 | tf_op jit(solution)/shard_map/all_gather | solution.py:926
  34.3 14.3 %collective-permute-start.14 = (bf16[832,128]{1,0:T(8,128)(2,1)}, bf16[832,128]{1,0:T(8,128)(2,1)S(1)}, u32[]{:S(2)}, u32[]{:S(2)}) collective-permute-start(bf16[832,128]{1,0:T(8,128)(2,1)} %shard_map.303), channel_id=1, source_target_pairs={{0,2},{1,3},{2,0},{3,1},{4,6},{5,7},{6,4},{7,5},{8,10},{9,11},{10,... | collective-permute-start | bytes 638984 | tf_op jit(solution)/shard_map/ppermute | solution.py:833
  37.0 11.4 %collective-permute-start.2 = (bf16[512,128]{1,0:T(8,128)(2,1)}, bf16[512,128]{1,0:T(8,128)(2,1)}, u32[]{:S(2)}, u32[]{:S(2)}) collective-permute-start(bf16[512,128]{1,0:T(8,128)(2,1)} %copy-done.31), channel_id=1, source_target_pairs={{0,1},{1,0},{2,3},{3,2},{4,5},{5,4},{6,7},{7,6},{8,9},{9,8},{10,11... | collective-permute-start | bytes 393224 | tf_op jit(solution)/shard_map/ppermute | solution.py:833
  38.5 9.9 %collective-permute-start.6 = (bf16[576,128]{1,0:T(8,128)(2,1)}, bf16[576,128]{1,0:T(8,128)(2,1)S(1)}, u32[]{:S(2)}, u32[]{:S(2)}) collective-permute-start(bf16[576,128]{1,0:T(8,128)(2,1)} %collective-permute-done.5.refs_2_), channel_id=1, source_target_pairs={{0,8},{4,12},{8,0},{12,4},{16,24},{20,28},{24,16},{28,20},{1,9},{5... | collective-permute-start | bytes 442376 | tf_op jit(solution)/shard_map/ppermute | solution.py:836
  40.0 8.6 %collective-permute-start.7 = (bf16[576,128]{1,0:T(8,128)(2,1)}, bf16[576,128]{1,0:T(8,128)(2,1)}, u32[]{:S(2)}, u32[]{:S(2)}) collective-permute-start(bf16[576,128]{1,0:T(8,128)(2,1)} %collective-permute-done.5.refs_2_), channel_id=1, source_target_pairs={{0,16},{4,20},{8,24},{12,28},{16,0},{20,4},{24,8},{28,12},{1,17},{... | collective-permute-start | bytes 442376 | tf_op jit(solution)/shard_map/ppermute | solution.py:836
  41.4 7.1 %collective-permute-start.8 = (bf16[576,128]{1,0:T(8,128)(2,1)}, bf16[576,128]{1,0:T(8,128)(2,1)}, u32[]{:S(2)}, u32[]{:S(2)}) collective-permute-start(bf16[576,128]{1,0:T(8,128)(2,1)} %collective-permute-done.5.refs_2_), channel_id=1, source_target_pairs={{0,24},{4,28},{8,16},{12,20},{16,8},{20,12},{24,0},{28,4},{1,25},{... | collective-permute-start | bytes 442376 | tf_op jit(solution)/shard_map/ppermute | solution.py:836
  50.5 4.4 %collective-permute-start.9 = (bf16[576,128]{1,0:T(8,128)(2,1)}, bf16[576,128]{1,0:T(8,128)(2,1)S(1)}, u32[]{:S(2)}, u32[]{:S(2)}) collective-permute-start(bf16[576,128]{1,0:T(8,128)(2,1)} %collective-permute-done.5.refs_2_), channel_id=1, source_target_pairs={{0,4},{4,0},{8,12},{12,8},{16,20},{20,16},{24,28},{28,24},{1,5},{5... | collective-permute-start | bytes 442376 | tf_op jit(solution)/shard_map/ppermute | solution.py:836
  51.6 9.7 %collective-permute-start.3 = (bf16[128,512]{1,0:T(8,128)(2,1)S(1)}, bf16[128,512]{1,0:T(8,128)(2,1)S(1)}, u32[]{:S(2)}, u32[]{:S(2)}) collective-permute-start(bf16[128,512]{1,0:T(8,128)(2,1)S(1)} %pad_maximum_fusion.5), channel_id=1, source_target_pairs={{0,4},{4,8},{8,12},{12,16},{16,20},{20,24},{24,28},{28,0},{1,5},{5... | collective-permute-start | bytes 393224 | tf_op jit(solution)/shard_map/ppermute | solution.py:839
  52.2 9.2 %collective-permute-start.4 = (bf16[128,512]{1,0:T(8,128)(2,1)S(1)}, bf16[128,512]{1,0:T(8,128)(2,1)S(1)}, u32[]{:S(2)}, u32[]{:S(2)}) collective-permute-start(bf16[128,512]{1,0:T(8,128)(2,1)S(1)} %pad_maximum_fusion.6), channel_id=1, source_target_pairs={{0,28},{4,0},{8,4},{12,8},{16,12},{20,16},{24,20},{28,24},{1,29},{... | collective-permute-start | bytes 393224 | tf_op jit(solution)/shard_map/ppermute | solution.py:839
  54.4 2.1 collective-permute-start.10
  54.4 2.1 collective-permute-start.11
  67.6 11.6 %collective-permute-start.13 = (bf16[640,256]{1,0:T(8,128)(2,1)}, bf16[640,256]{1,0:T(8,128)(2,1)S(1)}, u32[]{:S(2)}, u32[]{:S(2)}) collective-permute-start(bf16[640,256]{1,0:T(8,128)(2,1)} %get-tuple-element.87.refs_1_.refs_3_), channel_id=1, source_target_pairs={{0,1},{1,0},{2,3},{3,2},{4,5},{5,4},{6,7},{7,6},{8,9},{9,8},{10,11... | collective-permute-start | bytes 983048 | tf_op jit(solution)/shard_map/ppermute | solution.py:833
  68.2 14.2 %all-to-all-start.1 = ((f32[16,8,256]{2,1,0:T(8,128)}), f32[16,8,256]{2,1,0:T(8,128)S(1)}, u32[]{:S(2)}, u32[]{:S(2)}) async-start(f32[16,8,256]{2,1,0:T(8,128)} %get-tuple-element.88), calls=%async_computation.1 | async-start | bytes 262144 | tf_op jit(solution)/shard_map/all_to_all | solution.py:852
  72.0 43.4 %reduce-scatter.2.cloned.1.call-start = ((), (), s32[]{:S(2)}) async-start(), calls=%async_computation.10 | async-start | bytes 348160 | tf_op jit(solution)/shard_map/reduce_scatter | solution.py:947
  80.0 26.6 %collective-permute-start.16 = (bf16[512,128]{1,0:T(8,128)(2,1)}, bf16[512,128]{1,0:T(8,128)(2,1)S(1)}, u32[]{:S(2)}, u32[]{:S(2)}) collective-permute-start(bf16[512,128]{1,0:T(8,128)(2,1)} %get-tuple-element.96), channel_id=1, source_target_pairs={{0,2},{1,3},{2,0},{3,1},{4,6},{5,7},{6,4},{7,5},{8,10},{9,11},{10,... | collective-permute-start | bytes 393224 | tf_op jit(solution)/shard_map/ppermute | solution.py:833
  88.5 19.1 %collective-permute-start.15 = (bf16[512,256]{1,0:T(8,128)(2,1)}, bf16[512,256]{1,0:T(8,128)(2,1)S(1)}, u32[]{:S(2)}, u32[]{:S(2)}) collective-permute-start(bf16[512,256]{1,0:T(8,128)(2,1)} %get-tuple-element.92.refs_1_.refs_3_.refs_5_), channel_id=1, source_target_pairs={{0,1},{1,0},{2,3},{3,2},{4,5},{5,4},{6,7},{7,6},{8,9},{9,8},{10,11... | collective-permute-start | bytes 786440 | tf_op jit(solution)/shard_map/ppermute | solution.py:833
  90.0 25.4 %all-to-all-start.2 = ((f32[16,8,256]{2,1,0:T(8,128)}), f32[16,8,256]{2,1,0:T(8,128)S(1)}, u32[]{:S(2)}, u32[]{:S(2)}) async-start(f32[16,8,256]{2,1,0:T(8,128)} %get-tuple-element.93), calls=%async_computation.2 | async-start | bytes 262144 | tf_op jit(solution)/shard_map/all_to_all | solution.py:852
  104.8 7.4 %collective-permute-start.17 = (bf16[512,128]{1,0:T(8,128)(2,1)S(1)}, bf16[512,128]{1,0:T(8,128)(2,1)S(1)}, u32[]{:S(2)}, u32[]{:S(2)}) collective-permute-start(bf16[512,128]{1,0:T(8,128)(2,1)S(1)} %copy-done.13), channel_id=1, source_target_pairs={{0,1},{1,0},{2,3},{3,2},{4,5},{5,4},{6,7},{7,6},{8,9},{9,8},{10,11... | collective-permute-start | bytes 393224 | tf_op jit(solution)/shard_map/ppermute | solution.py:833
  106.5 8.1 %collective-permute-start.18 = (bf16[512,128]{1,0:T(8,128)(2,1)S(1)}, bf16[512,128]{1,0:T(8,128)(2,1)S(1)}, u32[]{:S(2)}, u32[]{:S(2)}) collective-permute-start(bf16[512,128]{1,0:T(8,128)(2,1)S(1)} %collective-permute-done.16), channel_id=1, source_target_pairs={{0,1},{1,0},{2,3},{3,2},{4,5},{5,4},{6,7},{7,6},{8,9},{9,8},{10,11... | collective-permute-start | bytes 393224 | tf_op jit(solution)/shard_map/ppermute | solution.py:833
  120.4 21.9 %all-to-all-start.3 = ((bf16[8,256,256]{2,1,0:T(8,128)(2,1)}), bf16[8,256,256]{2,1,0:T(8,128)(2,1)S(1)}, u32[]{:S(2)}, u32[]{:S(2)}) async-start(bf16[8,256,256]{2,1,0:T(8,128)(2,1)} %bitcast.87), calls=%async_computation.4 | async-start | bytes 2097152 | tf_op jit(solution)/shard_map/all_to_all | solution.py:1010
  125.2 15.4 %collective-permute-start.19 = (bf16[128,256]{1,0:T(8,128)(2,1)S(1)}, bf16[128,256]{1,0:T(8,128)(2,1)S(1)}, u32[]{:S(2)}, u32[]{:S(2)}) collective-permute-start(bf16[128,256]{1,0:T(8,128)(2,1)S(1)} %get-tuple-element.175), channel_id=1, source_target_pairs={{0,4},{4,8},{8,12},{12,16},{16,20},{20,24},{24,28},{28,0},{1,5},{5... | collective-permute-start | bytes 196616 | tf_op jit(solution)/shard_map/ppermute | solution.py:839
  125.7 14.8 %collective-permute-start.20 = (bf16[128,256]{1,0:T(8,128)(2,1)S(1)}, bf16[128,256]{1,0:T(8,128)(2,1)S(1)}, u32[]{:S(2)}, u32[]{:S(2)}) collective-permute-start(bf16[128,256]{1,0:T(8,128)(2,1)S(1)} %get-tuple-element.174), channel_id=1, source_target_pairs={{0,28},{4,0},{8,4},{12,8},{16,12},{20,16},{24,20},{28,24},{1,29},{... | collective-permute-start | bytes 196616 | tf_op jit(solution)/shard_map/ppermute | solution.py:839
  128.0 14.3 %collective-permute-start.23 = (bf16[256,512]{1,0:T(8,128)(2,1)}, bf16[256,512]{1,0:T(8,128)(2,1)S(1)}, u32[]{:S(2)}, u32[]{:S(2)}) collective-permute-start(bf16[256,512]{1,0:T(8,128)(2,1)} %get-tuple-element.102.refs_1_), channel_id=1, source_target_pairs={{0,2},{1,3},{2,0},{3,1},{4,6},{5,7},{6,4},{7,5},{8,10},{9,11},{10,... | collective-permute-start | bytes 786440 | tf_op jit(solution)/shard_map/ppermute | solution.py:833
  128.5 13.5 %collective-permute-start.21 = (bf16[128,256]{1,0:T(8,128)(2,1)S(1)}, bf16[128,256]{1,0:T(8,128)(2,1)S(1)}, u32[]{:S(2)}, u32[]{:S(2)}) collective-permute-start(bf16[128,256]{1,0:T(8,128)(2,1)S(1)} %get-tuple-element.173), channel_id=1, source_target_pairs={{0,4},{4,8},{8,12},{12,16},{16,20},{20,24},{24,28},{28,0},{1,5},{5... | collective-permute-start | bytes 196616 | tf_op jit(solution)/shard_map/ppermute | solution.py:839
  128.6 13.4 %collective-permute-start.22 = (bf16[128,256]{1,0:T(8,128)(2,1)S(1)}, bf16[128,256]{1,0:T(8,128)(2,1)S(1)}, u32[]{:S(2)}, u32[]{:S(2)}) collective-permute-start(bf16[128,256]{1,0:T(8,128)(2,1)S(1)} %get-tuple-element.172), channel_id=1, source_target_pairs={{0,28},{4,0},{8,4},{12,8},{16,12},{20,16},{24,20},{28,24},{1,29},{... | collective-permute-start | bytes 196616 | tf_op jit(solution)/shard_map/ppermute | solution.py:839
  145.1 2.0 collective-permute-start.24
  145.2 37.4 %collective-permute-start.26 = (bf16[768,512]{1,0:T(8,128)(2,1)S(1)}, bf16[768,512]{1,0:T(8,128)(2,1)S(1)}, u32[]{:S(2)}, u32[]{:S(2)}) collective-permute-start(bf16[768,512]{1,0:T(8,128)(2,1)S(1)} %copy-done.19), channel_id=1, source_target_pairs={{0,2},{1,3},{2,0},{3,1},{4,6},{5,7},{6,4},{7,5},{8,10},{9,11},{10,... | collective-permute-start | bytes 2359304 | tf_op jit(solution)/shard_map/ppermute | solution.py:833
  181.3 2.2 collective-permute-start.25
  187.0 19.0 %all-to-all-start.4 = ((bf16[8,256,256]{2,1,0:T(8,128)(2,1)}), bf16[8,256,256]{2,1,0:T(8,128)(2,1)S(1)}, u32[]{:S(2)}, u32[]{:S(2)}) async-start(bf16[8,256,256]{2,1,0:T(8,128)(2,1)} %bitcast.88), calls=%async_computation.5 | async-start | bytes 2097152 | tf_op jit(solution)/shard_map/all_to_all | solution.py:1045
  190.7 66.4 %all-gather.7.cloned.1.call-start = ((), (), s32[]{:S(2)}) async-start(), calls=%async_computation.12 | async-start | bytes 1179648 | tf_op jit(solution)/shard_map/all_gather | solution.py:1056
  192.2 5.5 %collective-permute-start.28 = (bf16[260,128]{1,0:T(8,128)(2,1)S(1)}, bf16[260,128]{1,0:T(8,128)(2,1)S(1)}, u32[]{:S(2)}, u32[]{:S(2)}) collective-permute-start(bf16[260,128]{1,0:T(8,128)(2,1)S(1)} %fusion.5.refs_2_), channel_id=1, source_target_pairs={{0,1},{1,0},{2,3},{3,2},{4,5},{5,4},{6,7},{7,6},{8,9},{9,8},{10,11... | collective-permute-start | bytes 199688 | tf_op jit(solution)/shard_map/ppermute | solution.py:833
  192.5 8.6 %collective-permute-start.29 = (bf16[260,128]{1,0:T(8,128)(2,1)S(1)}, bf16[260,128]{1,0:T(8,128)(2,1)S(1)}, u32[]{:S(2)}, u32[]{:S(2)}) collective-permute-start(bf16[260,128]{1,0:T(8,128)(2,1)S(1)} %fusion.5.refs_2_), channel_id=1, source_target_pairs={{0,2},{1,3},{2,0},{3,1},{4,6},{5,7},{6,4},{7,5},{8,10},{9,11},{10,... | collective-permute-start | bytes 199688 | tf_op jit(solution)/shard_map/ppermute | solution.py:833
  193.7 7.5 %collective-permute-start.30 = (bf16[260,128]{1,0:T(8,128)(2,1)S(1)}, bf16[260,128]{1,0:T(8,128)(2,1)S(1)}, u32[]{:S(2)}, u32[]{:S(2)}) collective-permute-start(bf16[260,128]{1,0:T(8,128)(2,1)S(1)} %fusion.5.refs_2_), channel_id=1, source_target_pairs={{0,3},{1,2},{2,1},{3,0},{4,7},{5,6},{6,5},{7,4},{8,11},{9,10},{10,... | collective-permute-start | bytes 199688 | tf_op jit(solution)/shard_map/ppermute | solution.py:833
  210.5 6.6 %collective-permute-start.31 = (bf16[512,256]{1,0:T(8,128)(2,1)}, bf16[512,256]{1,0:T(8,128)(2,1)S(1)}, u32[]{:S(2)}, u32[]{:S(2)}) collective-permute-start(bf16[512,256]{1,0:T(8,128)(2,1)} %get-tuple-element.110), channel_id=1, source_target_pairs={{0,1},{1,0},{2,3},{3,2},{4,5},{5,4},{6,7},{7,6},{8,9},{9,8},{10,11... | collective-permute-start | bytes 786440 | tf_op jit(solution)/shard_map/ppermute | solution.py:833
  210.7 15.1 %all-to-all-start.5 = ((f32[16,8,256]{2,1,0:T(8,128)}), f32[16,8,256]{2,1,0:T(8,128)S(1)}, u32[]{:S(2)}, u32[]{:S(2)}) async-start(f32[16,8,256]{2,1,0:T(8,128)} %get-tuple-element.114), calls=%async_computation.6 | async-start | bytes 262144 | tf_op jit(solution)/shard_map/all_to_all | solution.py:852
  218.2 7.7 %collective-permute-start.32 = (bf16[128,256]{1,0:T(8,128)(2,1)S(1)}, bf16[128,256]{1,0:T(8,128)(2,1)S(1)}, u32[]{:S(2)}, u32[]{:S(2)}) collective-permute-start(bf16[128,256]{1,0:T(8,128)(2,1)S(1)} %get-tuple-element.156), channel_id=1, source_target_pairs={{0,4},{4,8},{8,12},{12,16},{16,20},{20,24},{24,28},{28,0},{1,5},{5... | collective-permute-start | bytes 196616 | tf_op jit(solution)/shard_map/ppermute | solution.py:839
  218.2 7.6 %collective-permute-start.33 = (bf16[128,256]{1,0:T(8,128)(2,1)S(1)}, bf16[128,256]{1,0:T(8,128)(2,1)S(1)}, u32[]{:S(2)}, u32[]{:S(2)}) collective-permute-start(bf16[128,256]{1,0:T(8,128)(2,1)S(1)} %get-tuple-element.155), channel_id=1, source_target_pairs={{0,28},{4,0},{8,4},{12,8},{16,12},{20,16},{24,20},{28,24},{1,29},{... | collective-permute-start | bytes 196616 | tf_op jit(solution)/shard_map/ppermute | solution.py:839
  229.6 10.5 %collective-permute-start.35 = (bf16[640,128]{1,0:T(8,128)(2,1)}, bf16[640,128]{1,0:T(8,128)(2,1)S(1)}, u32[]{:S(2)}, u32[]{:S(2)}) collective-permute-start(bf16[640,128]{1,0:T(8,128)(2,1)} %get-tuple-element.119), channel_id=1, source_target_pairs={{0,2},{1,3},{2,0},{3,1},{4,6},{5,7},{6,4},{7,5},{8,10},{9,11},{10,... | collective-permute-start | bytes 491528 | tf_op jit(solution)/shard_map/ppermute | solution.py:833
  236.6 10.4 %collective-permute-start.34 = (bf16[640,256]{1,0:T(8,128)(2,1)}, bf16[640,256]{1,0:T(8,128)(2,1)S(1)}, u32[]{:S(2)}, u32[]{:S(2)}) collective-permute-start(bf16[640,256]{1,0:T(8,128)(2,1)} %get-tuple-element.117), channel_id=1, source_target_pairs={{0,1},{1,0},{2,3},{3,2},{4,5},{5,4},{6,7},{7,6},{8,9},{9,8},{10,11... | collective-permute-start | bytes 983048 | tf_op jit(solution)/shard_map/ppermute | solution.py:833
  240.7 12.0 %all-to-all-start.6 = ((f32[16,8,256]{2,1,0:T(8,128)}), f32[16,8,256]{2,1,0:T(8,128)S(1)}, u32[]{:S(2)}, u32[]{:S(2)}) async-start(f32[16,8,256]{2,1,0:T(8,128)} %shard_map.319), calls=%async_computation.7 | async-start | bytes 262144 | tf_op jit(solution)/shard_map/all_to_all | solution.py:852
  253.3 31.8 %all-to-all-start.7 = ((bf16[8,1088,128]{2,1,0:T(8,128)(2,1)}), bf16[8,1088,128]{2,1,0:T(8,128)(2,1)S(1)}, u32[]{:S(2)}, u32[]{:S(2)}) async-start(bf16[8,1088,128]{2,1,0:T(8,128)(2,1)} %shard_map.320.refs_7_), calls=%async_computation.8 | async-start | bytes 4456448 | tf_op jit(solution)/shard_map/all_to_all | solution.py:1114
  260.2 10.3 %collective-permute-start.36 = (bf16[640,128]{1,0:T(8,128)(2,1)}, bf16[640,128]{1,0:T(8,128)(2,1)S(1)}, u32[]{:S(2)}, u32[]{:S(2)}) collective-permute-start(bf16[640,128]{1,0:T(8,128)(2,1)} %get-tuple-element.121), channel_id=1, source_target_pairs={{0,2},{1,3},{2,0},{3,1},{4,6},{5,7},{6,4},{7,5},{8,10},{9,11},{10,... | collective-permute-start | bytes 491528 | tf_op jit(solution)/shard_map/ppermute | solution.py:833
  276.1 2.2 collective-permute-start.38
  281.5 14.1 %collective-permute-start.40 = (bf16[576,128]{1,0:T(8,128)(2,1)}, bf16[576,128]{1,0:T(8,128)(2,1)S(1)}, u32[]{:S(2)}, u32[]{:S(2)}) collective-permute-start(bf16[576,128]{1,0:T(8,128)(2,1)} %get-tuple-element.127), channel_id=1, source_target_pairs={{0,8},{4,12},{8,0},{12,4},{16,24},{20,28},{24,16},{28,20},{1,9},{5... | collective-permute-start | bytes 442376 | tf_op jit(solution)/shard_map/ppermute | solution.py:836
  283.1 14.4 %collective-permute-start.41 = (bf16[576,128]{1,0:T(8,128)(2,1)}, bf16[576,128]{1,0:T(8,128)(2,1)S(1)}, u32[]{:S(2)}, u32[]{:S(2)}) collective-permute-start(bf16[576,128]{1,0:T(8,128)(2,1)} %get-tuple-element.128), channel_id=1, source_target_pairs={{0,16},{4,20},{8,24},{12,28},{16,0},{20,4},{24,8},{28,12},{1,17},{... | collective-permute-start | bytes 442376 | tf_op jit(solution)/shard_map/ppermute | solution.py:836
  284.6 12.9 %collective-permute-start.42 = (bf16[576,128]{1,0:T(8,128)(2,1)}, bf16[576,128]{1,0:T(8,128)(2,1)S(1)}, u32[]{:S(2)}, u32[]{:S(2)}) collective-permute-start(bf16[576,128]{1,0:T(8,128)(2,1)} %get-tuple-element.129), channel_id=1, source_target_pairs={{0,24},{4,28},{8,16},{12,20},{16,8},{20,12},{24,0},{28,4},{1,25},{... | collective-permute-start | bytes 442376 | tf_op jit(solution)/shard_map/ppermute | solution.py:836
  288.8 8.8 %collective-permute-start.39 = (bf16[256,128]{1,0:T(8,128)(2,1)}, bf16[256,128]{1,0:T(8,128)(2,1)S(1)}, u32[]{:S(2)}, u32[]{:S(2)}) collective-permute-start(bf16[256,128]{1,0:T(8,128)(2,1)} %shard_map.326), channel_id=1, source_target_pairs={{0,2},{1,3},{2,0},{3,1},{4,6},{5,7},{6,4},{7,5},{8,10},{9,11},{10,... | collective-permute-start | bytes 196616 | tf_op jit(solution)/shard_map/ppermute | solution.py:833
  289.4 26.4 %collective-permute-start.44 = (bf16[512,256]{1,0:T(8,128)(2,1)}, bf16[512,256]{1,0:T(8,128)(2,1)S(1)}, u32[]{:S(2)}, u32[]{:S(2)}) collective-permute-start(bf16[512,256]{1,0:T(8,128)(2,1)} %get-tuple-element.132), channel_id=1, source_target_pairs={{0,1},{1,0},{2,3},{3,2},{4,5},{5,4},{6,7},{7,6},{8,9},{9,8},{10,11... | collective-permute-start | bytes 786440 | tf_op jit(solution)/shard_map/ppermute | solution.py:833
  291.4 22.0 %all-to-all-start.8 = ((f32[16,8,256]{2,1,0:T(8,128)}), f32[16,8,256]{2,1,0:T(8,128)S(1)}, u32[]{:S(2)}, u32[]{:S(2)}) async-start(f32[16,8,256]{2,1,0:T(8,128)} %shard_map.329), calls=%async_computation.9 | async-start | bytes 262144 | tf_op jit(solution)/shard_map/all_to_all | solution.py:852
  295.6 13.4 %collective-permute-start.37 = (bf16[512,256]{1,0:T(8,128)(2,1)S(1)}, bf16[512,256]{1,0:T(8,128)(2,1)S(1)}, u32[]{:S(2)}, u32[]{:S(2)}) collective-permute-start(bf16[512,256]{1,0:T(8,128)(2,1)S(1)} %copy-done.50), channel_id=1, source_target_pairs={{0,1},{1,0},{2,3},{3,2},{4,5},{5,4},{6,7},{7,6},{8,9},{9,8},{10,11... | collective-permute-start | bytes 786440 | tf_op jit(solution)/shard_map/ppermute | solution.py:833
  301.7 25.4 %collective-permute-start.46 = (bf16[1408,128]{1,0:T(8,128)(2,1)}, bf16[1408,128]{1,0:T(8,128)(2,1)S(1)}, u32[]{:S(2)}, u32[]{:S(2)}) collective-permute-start(bf16[1408,128]{1,0:T(8,128)(2,1)} %shard_map.327.refs_4_.refs_8_.refs_5_.refs_2_.refs_1_), channel_id=1, source_target_pairs={{0,8},{4,12},{8,0},{12,4},{16,24},{20,28},{24,16},{28,20},{1,9},{5... | collective-permute-start | bytes 1081352 | tf_op jit(solution)/shard_map/ppermute | solution.py:836
  303.2 24.4 %collective-permute-start.47 = (bf16[1408,128]{1,0:T(8,128)(2,1)}, bf16[1408,128]{1,0:T(8,128)(2,1)S(1)}, u32[]{:S(2)}, u32[]{:S(2)}) collective-permute-start(bf16[1408,128]{1,0:T(8,128)(2,1)} %shard_map.327.refs_4_.refs_8_.refs_5_.refs_2_.refs_1_), channel_id=1, source_target_pairs={{0,16},{4,20},{8,24},{12,28},{16,0},{20,4},{24,8},{28,12},{1,17},{... | collective-permute-start | bytes 1081352 | tf_op jit(solution)/shard_map/ppermute | solution.py:836
  304.6 23.0 %collective-permute-start.48 = (bf16[1408,128]{1,0:T(8,128)(2,1)}, bf16[1408,128]{1,0:T(8,128)(2,1)S(1)}, u32[]{:S(2)}, u32[]{:S(2)}) collective-permute-start(bf16[1408,128]{1,0:T(8,128)(2,1)} %shard_map.327.refs_4_.refs_8_.refs_5_.refs_2_.refs_1_), channel_id=1, source_target_pairs={{0,24},{4,28},{8,16},{12,20},{16,8},{20,12},{24,0},{28,4},{1,25},{... | collective-permute-start | bytes 1081352 | tf_op jit(solution)/shard_map/ppermute | solution.py:836
  311.8 15.2 %collective-permute-start.43 = (bf16[512,128]{1,0:T(8,128)(2,1)}, bf16[512,128]{1,0:T(8,128)(2,1)S(1)}, u32[]{:S(2)}, u32[]{:S(2)}) collective-permute-start(bf16[512,128]{1,0:T(8,128)(2,1)} %get-tuple-element.131), channel_id=1, source_target_pairs={{0,2},{1,3},{2,0},{3,1},{4,6},{5,7},{6,4},{7,5},{8,10},{9,11},{10,... | collective-permute-start | bytes 393224 | tf_op jit(solution)/shard_map/ppermute | solution.py:833
  315.7 4.8 %collective-permute-start.53 = (f32[8,128]{1,0:T(8,128)}, f32[8,128]{1,0:T(8,128)S(1)}, u32[]{:S(2)}, u32[]{:S(2)}) collective-permute-start(f32[8,128]{1,0:T(8,128)} %get-tuple-element.140), channel_id=1, source_target_pairs={{0,2},{1,3},{2,0},{3,1},{4,6},{5,7},{6,4},{7,5},{8,10},{9,11},{10,... | collective-permute-start | bytes 12296 | tf_op jit(solution)/shard_map/ppermute | solution.py:833
  320.5 7.6 %collective-permute-start.45 = (bf16[512,128]{1,0:T(8,128)(2,1)}, bf16[512,128]{1,0:T(8,128)(2,1)S(1)}, u32[]{:S(2)}, u32[]{:S(2)}) collective-permute-start(bf16[512,128]{1,0:T(8,128)(2,1)} %get-tuple-element.136), channel_id=1, source_target_pairs={{0,2},{1,3},{2,0},{3,1},{4,6},{5,7},{6,4},{7,5},{8,10},{9,11},{10,... | collective-permute-start | bytes 393224 | tf_op jit(solution)/shard_map/ppermute | solution.py:833
  327.0 3.8 %collective-permute-start.49 = (bf16[1408,128]{1,0:T(8,128)(2,1)S(1)}, bf16[1408,128]{1,0:T(8,128)(2,1)S(1)}, u32[]{:S(2)}, u32[]{:S(2)}) collective-permute-start(bf16[1408,128]{1,0:T(8,128)(2,1)S(1)} %copy-done.5), channel_id=1, source_target_pairs={{0,4},{4,0},{8,12},{12,8},{16,20},{20,16},{24,28},{28,24},{1,5},{5... | collective-permute-start | bytes 1081352 | tf_op jit(solution)/shard_map/ppermute | solution.py:836
  327.1 3.7 %collective-permute-start.50 = (bf16[1408,128]{1,0:T(8,128)(2,1)S(1)}, bf16[1408,128]{1,0:T(8,128)(2,1)S(1)}, u32[]{:S(2)}, u32[]{:S(2)}) collective-permute-start(bf16[1408,128]{1,0:T(8,128)(2,1)S(1)} %collective-permute-done.46.refs_2_), channel_id=1, source_target_pairs={{0,4},{4,0},{8,12},{12,8},{16,20},{20,16},{24,28},{28,24},{1,5},{5... | collective-permute-start | bytes 1081352 | tf_op jit(solution)/shard_map/ppermute | solution.py:836
  327.6 3.3 collective-permute-start.51
  327.7 3.2 collective-permute-start.52
  (80 other events, 265.3 us)
Sparse Core Ops, SparseCore 0:
  49.8 25.6 all-gather.4
  205.0 23.9 all-gather.6
Sparse Core Ops, SparseCore 1:
  82.5 19.4 reduce-scatter.1
where the time goes:
time: 351 us; the launch traced here: 344 us
  Pallas kernels  134 us (38%)
  starting transfers between devices  104 us (30%)
  waiting for transfers between devices  43.3 us (12%)
  local copies, waits for them, and re-layouts  35.5 us (10%)
  between operations  18 us (5%)
  other arithmetic  8.31 us (2%)
    pallas_call x29, Pallas kernels, call(): pl.pallas_call(inner, in_specs=[in_smem] + [in_vmem] * (count - 1) + [any...  100 us
    ppermute x25, starting transfers between devices, over_ch(): return lax.ppermute(value, 'ch', [(n, n ^ mask) for n in range(4)])  33.5 us
    pallas_call x1, Pallas kernels, attend(): pl.pallas_call(inner, grid=(queries // block,), in_specs=[pl.BlockSpec(me...  33.4 us
    all_to_all x5, starting transfers between devices, to_image(): return lax.all_to_all(value, ('blk', 'ch'), 0, 0, axis_index_groups=pairs)  30.7 us
    unnamed x162, local copies, waits for them, and re-layouts  24.3 us
    ppermute x25, waiting for transfers between devices, over_ch(): return lax.ppermute(value, 'ch', [(n, n ^ mask) for n in range(4)])  21.6 us
    ppermute x21, starting transfers between devices, over_blk(): return lax.ppermute(value, 'blk', [(n, n ^ mask) for n in range(blocks)])  13 us
    ppermute x8, starting transfers between devices, ring(): lax.ppermute(value, 'blk', [(n, (n + step) % blocks) for n in range(block...  10.9 us
  transfers between devices with their start and end apart: 66, of which 21 were waited for; matrix products, arithmetic and copies ran while one was open for 6% of the time, Pallas kernels for 35%

commit v1 on v0

--- a/solution.py
+++ b/solution.py
@@ -907,9 +907,8 @@
     )[0]
     sums1 = lax.all_to_all(x_sums, ("blk", "ch"), 0, 0)
     two_source = jnp.concatenate([chunk_of(w2_own), chunk_of(wp_own)], axis=0)
-    (two_source,) = after((two_source,), x_two, x_one, x_sums)
     two_chunk = over_ch(two_source, 2)
-    (two_chunk,) = after((two_chunk,), x_three, *w1_pieces[1:4])
+    (two_chunk,) = after((two_chunk,), x_one, x_sums, x_three, *w1_pieces[1:4])
     wide = dict(axis=1)
     x_own = jnp.concatenate(by_image(x_mine, x_two), **wide)
     x_oth = jnp.concatenate(by_image(x_one, x_three), **wide)

time: 351 us -> 349 us (level)
    unnamed x162 -> x160, local copies, waits for them, and re-layouts: 24.3 us -> 23.3 us
  transfers between devices with their start and end apart: 66 -> 66, of which waited for: 21 -> 23; matrix products, arithmetic and copies ran while one was open for 6% -> 6% of each run, Pallas kernels for 35% -> 36%
where the time goes in v1:
time: 349 us; the launch traced here: 343 us
  Pallas kernels  134 us (38%)
  starting transfers between devices  104 us (30%)
  waiting for transfers between devices  42.5 us (12%)
  local copies, waits for them, and re-layouts  34.5 us (10%)
  between operations  17.9 us (5%)
  other arithmetic  9.23 us (3%)
    pallas_call x29, Pallas kernels, call(): pl.pallas_call(inner, in_specs=[in_smem] + [in_vmem] * (count - 1) + [any...  100 us
    pallas_call x1, Pallas kernels, attend(): pl.pallas_call(inner, grid=(queries // block,), in_specs=[pl.BlockSpec(me...  33.5 us
    ppermute x25, starting transfers between devices, over_ch(): return lax.ppermute(value, 'ch', [(n, n ^ mask) for n in range(4)])  32.8 us
    all_to_all x5, starting transfers between devices, to_image(): return lax.all_to_all(value, ('blk', 'ch'), 0, 0, axis_index_groups=pairs)  30.8 us
    unnamed x160, local copies, waits for them, and re-layouts  23.3 us
    ppermute x25, waiting for transfers between devices, over_ch(): return lax.ppermute(value, 'ch', [(n, n ^ mask) for n in range(4)])  22.4 us
    ppermute x21, starting transfers between devices, over_blk(): return lax.ppermute(value, 'blk', [(n, n ^ mask) for n in range(blocks)])  13 us
    ppermute x8, starting transfers between devices, ring(): lax.ppermute(value, 'blk', [(n, (n + step) % blocks) for n in range(block...  10.9 us
  transfers between devices with their start and end apart: 66, of which 23 were waited for; matrix products, arithmetic and copies ran while one was open for 6% of the time, Pallas kernels for 36%

profile of v1, /device:TPU:0, one launch (start us, length us, event | category | flops | bytes accessed | tf_op | source)
XLA Modules:
  0.0 342.8 jit_solution(3274562960894221205)
XLA Ops:
  9.1 4.1 %collective-permute-start.5 = (bf16[576,128]{1,0:T(8,128)(2,1)S(1)}, bf16[576,128]{1,0:T(8,128)(2,1)}, u32[]{:S(2)}, u32[]{:S(2)}) collective-permute-start(bf16[576,128]{1,0:T(8,128)(2,1)S(1)} %constant_dynamic-slice_fusion.4.refs_2_), channel_id=1, source_target_pairs={{0,2},{1,3},{2,0},{3,1},{4,6},{5,7},{6,4},{7,5},{8,10},{9,11},{10,... | collective-permute-start | bytes 442376 | tf_op jit(solution)/shard_map/ppermute | solution.py:833
  13.8 1.7 shard_map.298
  18.1 1.9 concatenate.41.refs_2_.refs_3_
  20.1 1.9 collective-permute-start.1
  21.9 1.8 shard_map.299.refs_2_
  23.7 4.8 %all-to-all-start = ((f32[32,16,128]{2,1,0:T(8,128)}), f32[32,16,128]{2,1,0:T(8,128)S(1)}, u32[]{:S(2)}, u32[]{:S(2)}) async-start(f32[32,16,128]{2,1,0:T(8,128)} %shard_map.299.refs_2_), calls=%async_computation | async-start | bytes 524288 | tf_op jit(solution)/shard_map/all_to_all | solution.py:908
  31.3 2.7 collective-permute-start.14
  41.2 1.7 shard_map.301
  51.9 2.2 collective-permute-start.4
  57.7 3.5 %shard_map.300.refs_6_.refs_2_ = bf16[4608,256]{1,0:T(8,128)(2,1)} custom-call(s32[8]{0:T(128)} %stack.81.refs_0_, bf16[4608,128]{1,0:T(8,128)(2,1)} %bitcast.92, bf16[576,128]{1,0:T(8,128)(2,1)} %collective-permute-done.5.refs_2_, bf16[576,128]{1,0:T(8,128)(2,1)} %copy-done.21, bf16[576,128]{1,0:T(8,128)(2,1)} %copy-done.23, bf16[576,128]{1,0:T(8,128)(2,1)} %copy-done.25, ...), custom_call_target="tpu_custom_call" | custom-call | flops 1 | bytes 1 | tf_op jit(solution)/shard_map/pallas_call | solution.py:758
  62.0 5.4 %shard_map.302 = (bf16[640,256]{1,0:T(8,128)(2,1)}, f32[16,8,256]{2,1,0:T(8,128)}, bf16[512,512]{1,0:T(8,128)(2,1)}, f32[4,16,128]{2,1,0:T(8,128)}) custom-call(s32[8]{0:T(128)} %stack.81.refs_0_, bf16[512,256]{1,0:T(8,128)(2,1)} %pad_maximum_fusion.refs_1_.refs_6_.refs_3_, bf16[512,256]{1,0:T(8,128)(2,1)} %pad_maximum_fusion.1.refs_2_.refs_4_, ...), custom_call_target="tpu_custom_call" | custom-call | flops 1 | bytes 1 | tf_op jit(solution)/shard_map/pallas_call | solution.py:758
  67.8 3.9 %all-to-all-start.1 = ((f32[16,8,256]{2,1,0:T(8,128)}), f32[16,8,256]{2,1,0:T(8,128)S(1)}, u32[]{:S(2)}, u32[]{:S(2)}) async-start(f32[16,8,256]{2,1,0:T(8,128)} %get-tuple-element.88), calls=%async_computation.1 | async-start | bytes 262144 | tf_op jit(solution)/shard_map/all_to_all | solution.py:852
  71.8 2.2 all-gather.5.cloned.1.call-done
  74.0 3.6 %shard_map.304.refs_5_.refs_3_.refs_2_ = bf16[4608,256]{1,0:T(8,128)(2,1)} custom-call(s32[8]{0:T(128)} %stack.81.refs_0_, bf16[4608,128]{1,0:T(8,128)(2,1)} %bitcast.94, bf16[8,832,128]{2,1,0:T(8,128)(2,1)} %bitcast.82), custom_call_target="tpu_custom_call" | custom-call | flops 1 | bytes 1 | tf_op jit(solution)/shard_map/pallas_call | solution.py:758
  78.9 1.9 collective-permute-start.16
  81.5 5.5 %shard_map.305 = (f32[512,256]{1,0:T(8,128)}, bf16[512,256]{1,0:T(8,128)(2,1)}, f32[16,8,256]{2,1,0:T(8,128)}, bf16[256,512]{1,0:T(8,128)(2,1)}, bf16[768,512]{1,0:T(8,128)(2,1)}, /*index=5*/bf16[2,128,256]{2,1,0:T(8,128)(2,1)}) custom-call(s32[8]{0:T(128)} %stack.81.refs_0_, bf16[640,256]{1,0:T(8,128)(2,1)} %get-tuple-element.87.refs_1_.refs_3_, ...), custom_call_target="tpu_custom_call" | custom-call | flops 1 | bytes 1 | tf_op jit(solution)/shard_map/pallas_call | solution.py:758
  88.5 14.8 %all-to-all-start.2 = ((f32[16,8,256]{2,1,0:T(8,128)}), f32[16,8,256]{2,1,0:T(8,128)S(1)}, u32[]{:S(2)}, u32[]{:S(2)}) async-start(f32[16,8,256]{2,1,0:T(8,128)} %get-tuple-element.93), calls=%async_computation.2 | async-start | bytes 262144 | tf_op jit(solution)/shard_map/all_to_all | solution.py:852
  103.3 1.7 collective-permute-start.17
  106.8 2.9 shard_map.307.refs_7_.refs_2_
  110.7 2.3 collective-permute-done.18
  114.5 4.3 %shard_map.308 = (bf16[4,512,256]{2,1,0:T(8,128)(2,1)}, bf16[512,512]{1,0:T(8,128)(2,1)}, bf16[512,512]{1,0:T(8,128)(2,1)}, bf16[2,128,256]{2,1,0:T(8,128)(2,1)}) custom-call(s32[8]{0:T(128)} %stack.81.refs_0_, bf16[512,256]{1,0:T(8,128)(2,1)} %get-tuple-element.92.refs_1_.refs_3_.refs_5_, bf16[512,256]{1,0:T(8,128)(2,1)} %copy-done.8, ...), custom_call_target="tpu_custom_call" | custom-call | flops 1 | bytes 1 | tf_op jit(solution)/shard_map/pallas_call | solution.py:758
  118.8 3.9 %all-to-all-start.3 = ((bf16[8,256,256]{2,1,0:T(8,128)(2,1)}), bf16[8,256,256]{2,1,0:T(8,128)(2,1)S(1)}, u32[]{:S(2)}, u32[]{:S(2)}) async-start(bf16[8,256,256]{2,1,0:T(8,128)(2,1)} %bitcast.87), calls=%async_computation.4 | async-start | bytes 2097152 | tf_op jit(solution)/shard_map/all_to_all | solution.py:1009
  124.2 2.2 collective-permute-start.20
  127.0 2.6 collective-permute-start.22
  129.7 9.3 %collective-permute-done.19.refs_1_.refs_6_ = bf16[128,256]{1,0:T(8,128)(2,1)S(1)} collective-permute-done((bf16[128,256]{1,0:T(8,128)(2,1)S(1)}, bf16[128,256]{1,0:T(8,128)(2,1)S(1)}, u32[]{:S(2)}, u32[]{:S(2)}) %collective-permute-start.19) | collective-permute-done | bytes 65568 | tf_op jit(solution)/shard_map/ppermute | solution.py:839
  146.3 33.5 %shard_map.311 = (bf16[2048,128]{1,0:T(8,128)(2,1)}, f32[2048,128]{1,0:T(8,128)}, bf16[2048,128]{1,0:T(8,128)(2,1)}, f32[272,128]{1,0:T(8,128)}) custom-call(s32[1]{0:T(128)} %bitcast.28.refs_10_.refs_0_, bf16[2048,256]{1,0:T(8,128)(2,1)} %bitcast.85, bf16[2048,256]{1,0:T(8,128)(2,1)} %bitcast.86, bf16[2048,128]{1,0:T(8,128)(2,1)} %copy-done.72, ...), custom_call_target="tpu_custom_call" | custom-call | flops 43699998720 | bytes 1 | tf_op jit(solution)/shard_map/pallas_call | solution.py:711
  182.8 2.7 shard_map.312
  185.5 3.7 %all-to-all-start.4 = ((bf16[8,256,256]{2,1,0:T(8,128)(2,1)}), bf16[8,256,256]{2,1,0:T(8,128)(2,1)S(1)}, u32[]{:S(2)}, u32[]{:S(2)}) async-start(bf16[8,256,256]{2,1,0:T(8,128)(2,1)} %bitcast.88), calls=%async_computation.5 | async-start | bytes 2097152 | tf_op jit(solution)/shard_map/all_to_all | solution.py:1044
  192.2 3.0 collective-permute-start.30
  196.2 3.4 collective-permute-done.29.refs_4_
  200.9 2.5 shard_map.313.refs_7_
  205.5 3.5 %shard_map.314 = (f32[512,256]{1,0:T(8,128)}, bf16[512,256]{1,0:T(8,128)(2,1)}, f32[16,8,256]{2,1,0:T(8,128)}) custom-call(s32[8]{0:T(128)} %stack.81.refs_0_, bf16[4,512,256]{2,1,0:T(8,128)(2,1)} %bitcast.80, bf16[512,1024]{1,0:T(8,128)(2,1)} %shard_map.307.refs_7_.refs_2_, bf16[512,256]{1,0:T(8,128)(2,1)} %get-tuple-element.92.refs_1_.refs_3_.refs_5_, ...), custom_call_target="tpu_custom_call" | custom-call | flops 1 | bytes 1 | tf_op jit(solution)/shard_map/pallas_call | solution.py:758
  209.3 4.4 %all-to-all-start.5 = ((f32[16,8,256]{2,1,0:T(8,128)}), f32[16,8,256]{2,1,0:T(8,128)S(1)}, u32[]{:S(2)}, u32[]{:S(2)}) async-start(f32[16,8,256]{2,1,0:T(8,128)} %get-tuple-element.114), calls=%async_computation.6 | async-start | bytes 262144 | tf_op jit(solution)/shard_map/all_to_all | solution.py:852
  213.7 1.9 collective-permute-done.31.refs_5_.refs_2_
  216.7 2.6 collective-permute-start.33
  219.4 5.0 %shard_map.315 = (f32[512,256]{1,0:T(8,128)}, bf16[512,256]{1,0:T(8,128)(2,1)}, bf16[2,2048,128]{2,1,0:T(8,128)(2,1)}) custom-call(s32[8]{0:T(128)} %stack.81.refs_0_, bf16[4,512,256]{2,1,0:T(8,128)(2,1)} %bitcast.81, bf16[512,1024]{1,0:T(8,128)(2,1)} %shard_map.307.refs_7_.refs_2_, bf16[512,512]{1,0:T(8,128)(2,1)} %get-tuple-element.107.refs_3_, ...), custom_call_target="tpu_custom_call" | custom-call | flops 1 | bytes 1 | tf_op jit(solution)/shard_map/pallas_call | solution.py:758
  225.0 3.1 shard_map.316
  228.1 1.7 collective-permute-start.35
  229.8 5.3 %shard_map.317 = (f32[640,256]{1,0:T(8,128)}, bf16[640,256]{1,0:T(8,128)(2,1)}, f32[16,8,256]{2,1,0:T(8,128)}) custom-call(s32[8]{0:T(128)} %stack.81.refs_0_, bf16[768,256]{1,0:T(8,128)(2,1)} %get-tuple-element.115.refs_1_.refs_3_, bf16[4608,256]{1,0:T(8,128)(2,1)} %shard_map.304.refs_5_.refs_3_.refs_2_, ...), custom_call_target="tpu_custom_call" | custom-call | flops 9200000000 | bytes 1 | tf_op jit(solution)/shard_map/pallas_call | solution.py:758
  235.4 3.2 collective-permute-done.35.refs_1_.refs_4_
  239.3 3.5 %all-to-all-start.6 = ((f32[16,8,256]{2,1,0:T(8,128)}), f32[16,8,256]{2,1,0:T(8,128)S(1)}, u32[]{:S(2)}, u32[]{:S(2)}) async-start(f32[16,8,256]{2,1,0:T(8,128)} %shard_map.318), calls=%async_computation.7 | async-start | bytes 262144 | tf_op jit(solution)/shard_map/all_to_all | solution.py:852
  242.8 2.7 collective-permute-done.34.refs_6_.refs_2_
  246.3 5.0 %shard_map.319.refs_7_ = bf16[8,1088,128]{2,1,0:T(8,128)(2,1)} custom-call(s32[8]{0:T(128)} %stack.81.refs_0_, bf16[768,512]{1,0:T(8,128)(2,1)} %get-tuple-element.106.refs_1_.refs_2_, bf16[768,512]{1,0:T(8,128)(2,1)} %copy-done.6, bf16[768,256]{1,0:T(8,128)(2,1)} %get-tuple-element.115.refs_1_.refs_3_, bf16[640,128]{1,0:T(8,128)(2,1)} %copy-done.19, ...), custom_call_target="tpu_custom_call" | custom-call | flops 1 | bytes 1 | tf_op jit(solution)/shard_map/pallas_call | solution.py:758
  251.9 3.8 %all-to-all-start.7 = ((bf16[8,1088,128]{2,1,0:T(8,128)(2,1)}), bf16[8,1088,128]{2,1,0:T(8,128)(2,1)S(1)}, u32[]{:S(2)}, u32[]{:S(2)}) async-start(bf16[8,1088,128]{2,1,0:T(8,128)(2,1)} %shard_map.319.refs_7_), calls=%async_computation.8 | async-start | bytes 4456448 | tf_op jit(solution)/shard_map/all_to_all | solution.py:1113
  255.7 3.1 shard_map.320
  259.1 4.9 %shard_map.322 = (f32[512,256]{1,0:T(8,128)}, bf16[512,256]{1,0:T(8,128)(2,1)}, f32[16,8,256]{2,1,0:T(8,128)}) custom-call(s32[8]{0:T(128)} %stack.81.refs_0_, bf16[640,256]{1,0:T(8,128)(2,1)} %get-tuple-element.122.refs_1_.refs_5_, bf16[4608,256]{1,0:T(8,128)(2,1)} %shard_map.300.refs_6_.refs_2_, bf16[512,256]{1,0:T(8,128)(2,1)} %pad_maximum_fusion.refs_1_.refs_6_.refs_3_, ...), custom_call_target="tpu_custom_call" | custom-call | flops 9200000000 | bytes 1 | tf_op jit(solution)/shard_map/pallas_call | solution.py:758
  263.9 5.1 %collective-permute-done.36.refs_1_.refs_6_ = bf16[640,128]{1,0:T(8,128)(2,1)S(1)} collective-permute-done((bf16[640,128]{1,0:T(8,128)(2,1)}, bf16[640,128]{1,0:T(8,128)(2,1)S(1)}, u32[]{:S(2)}, u32[]{:S(2)}) %collective-permute-start.36) | collective-permute-done | bytes 163872 | tf_op jit(solution)/shard_map/ppermute | solution.py:833
  269.7 4.9 %shard_map.323 = (f32[4,576,128]{2,1,0:T(8,128)}, bf16[4,576,128]{2,1,0:T(8,128)(2,1)}) custom-call(s32[8]{0:T(128)} %stack.81.refs_0_, bf16[256,512]{1,0:T(8,128)(2,1)} %get-tuple-element.102.refs_1_, bf16[768,512]{1,0:T(8,128)(2,1)} %get-tuple-element.106.refs_1_.refs_2_, bf16[256,512]{1,0:T(8,128)(2,1)} %copy-done.45, bf16[768,512]{1,0:T(8,128)(2,1)} %copy-done.6, ...), custom_call_target="tpu_custom_call" | custom-call | flops 23000000512 | bytes 1 | tf_op jit(solution)/shard_map/pallas_call | solution.py:758
  274.7 2.1 collective-permute-done.38.refs_2_
  277.7 2.4 shard_map.324
  280.0 1.7 collective-permute-start.40
  285.0 2.3 shard_map.325
  287.8 2.1 collective-permute-start.44
  289.9 4.1 %all-to-all-start.8 = ((f32[16,8,256]{2,1,0:T(8,128)}), f32[16,8,256]{2,1,0:T(8,128)S(1)}, u32[]{:S(2)}, u32[]{:S(2)}) async-start(f32[16,8,256]{2,1,0:T(8,128)} %shard_map.328), calls=%async_computation.9 | async-start | bytes 262144 | tf_op jit(solution)/shard_map/all_to_all | solution.py:852
  294.1 2.0 collective-permute-start.37
  297.4 2.8 shard_map.326.refs_4_.refs_8_.refs_5_.refs_2_.refs_1_
  303.7 3.8 %shard_map.331.refs_10_ = f32[512,2,512]{2,1,0:T(2,128)} custom-call(s32[8]{0:T(128)} %stack.81.refs_0_, bf16[8,256,256]{2,1,0:T(8,128)(2,1)} %bitcast.97, bf16[1408,128]{1,0:T(8,128)(2,1)} %shard_map.326.refs_4_.refs_8_.refs_5_.refs_2_.refs_1_), custom_call_target="tpu_custom_call" | custom-call | flops 11500000256 | bytes 1 | tf_op jit(solution)/shard_map/pallas_call | solution.py:758
  308.2 2.0 shard_map.327
  310.3 1.7 collective-permute-start.43
  312.6 1.7 shard_map.332
  315.6 3.0 shard_map.329
  320.4 5.1 %shard_map.333 = (f32[2,128]{1,0:T(2,128)}, f32[1,128]{1,0:T(1,128)}, f32[1,128]{1,0:T(1,128)}, f32[1,128]{1,0:T(1,128)}, f32[1,128]{1,0:T(1,128)}, /*index=5*/f...) custom-call(s32[8]{0:T(128)} %stack.81.refs_0_, f32[8,128]{1,0:T(8,128)} %get-tuple-element.139.refs_1_, ...), custom_call_target="tpu_custom_call" | custom-call | flops 17250000896 | bytes 1 | tf_op jit(solution)/shard_map/pallas_call | solution.py:758
  327.3 2.0 shard_map.330
  330.5 4.7 %shard_map.334 = (f32[4608,128]{1,0:T(8,128)}, f32[4608,128]{1,0:T(8,128)}, f32[1536,128]{1,0:T(8,128)}, f32[128,512]{1,0:T(8,128)}) custom-call(s32[8]{0:T(128)} %stack.81.refs_0_, bf16[1408,128]{1,0:T(8,128)(2,1)} %shard_map.326.refs_4_.refs_8_.refs_5_.refs_2_.refs_1_, bf16[1408,128]{1,0:T(8,128)(2,1)} %copy-done.37, bf16[1408,128]{1,0:T(8,128)(2,1)} %copy-done.38, ...), custom_call_target="tpu_custom_call" | custom-call | flops 1 | bytes 1 | tf_op jit(solution)/shard_map/pallas_call | solution.py:758
  (317 shorter events, 75.9 us)
Async XLA Ops:
  9.1 28.0 %collective-permute-start.5 = (bf16[576,128]{1,0:T(8,128)(2,1)S(1)}, bf16[576,128]{1,0:T(8,128)(2,1)}, u32[]{:S(2)}, u32[]{:S(2)}) collective-permute-start(bf16[576,128]{1,0:T(8,128)(2,1)S(1)} %constant_dynamic-slice_fusion.4.refs_2_), channel_id=1, source_target_pairs={{0,2},{1,3},{2,0},{3,1},{4,6},{5,7},{6,4},{7,5},{8,10},{9,11},{10,... | collective-permute-start | bytes 442376 | tf_op jit(solution)/shard_map/ppermute | solution.py:833
  15.5 20.1 %collective-permute-start = (bf16[512,128]{1,0:T(8,128)(2,1)}, bf16[512,128]{1,0:T(8,128)(2,1)}, u32[]{:S(2)}, u32[]{:S(2)}) collective-permute-start(bf16[512,128]{1,0:T(8,128)(2,1)} %get-tuple-element.85), channel_id=1, source_target_pairs={{0,2},{1,3},{2,0},{3,1},{4,6},{5,7},{6,4},{7,5},{8,10},{9,11},{10,... | collective-permute-start | bytes 393224 | tf_op jit(solution)/shard_map/ppermute | solution.py:833
  20.1 20.1 %collective-permute-start.1 = (bf16[512,128]{1,0:T(8,128)(2,1)}, bf16[512,128]{1,0:T(8,128)(2,1)S(1)}, u32[]{:S(2)}, u32[]{:S(2)}) collective-permute-start(bf16[512,128]{1,0:T(8,128)(2,1)} %get-tuple-element.84.refs_3_), channel_id=1, source_target_pairs={{0,1},{1,0},{2,3},{3,2},{4,5},{5,4},{6,7},{7,6},{8,9},{9,8},{10,11... | collective-permute-start | bytes 393224 | tf_op jit(solution)/shard_map/ppermute | solution.py:833
  23.7 37.5 %all-to-all-start = ((f32[32,16,128]{2,1,0:T(8,128)}), f32[32,16,128]{2,1,0:T(8,128)S(1)}, u32[]{:S(2)}, u32[]{:S(2)}) async-start(f32[32,16,128]{2,1,0:T(8,128)} %shard_map.299.refs_2_), calls=%async_computation | async-start | bytes 524288 | tf_op jit(solution)/shard_map/all_to_all | solution.py:908
  28.5 45.5 %all-gather.5.cloned.1.call-start = ((), (), s32[]{:S(2)}) async-start(), calls=%async_computation.11 | async-start | bytes 1916928 | tf_op jit(solution)/shard_map/all_gather | solution.py:925
  31.3 15.8 %collective-permute-start.14 = (bf16[832,128]{1,0:T(8,128)(2,1)}, bf16[832,128]{1,0:T(8,128)(2,1)}, u32[]{:S(2)}, u32[]{:S(2)}) collective-permute-start(bf16[832,128]{1,0:T(8,128)(2,1)} %pad_maximum_fusion.4), channel_id=1, source_target_pairs={{0,2},{1,3},{2,0},{3,1},{4,6},{5,7},{6,4},{7,5},{8,10},{9,11},{10,... | collective-permute-start | bytes 638984 | tf_op jit(solution)/shard_map/ppermute | solution.py:833
  35.6 11.6 %collective-permute-start.2 = (bf16[512,128]{1,0:T(8,128)(2,1)}, bf16[512,128]{1,0:T(8,128)(2,1)}, u32[]{:S(2)}, u32[]{:S(2)}) collective-permute-start(bf16[512,128]{1,0:T(8,128)(2,1)} %collective-permute-done), channel_id=1, source_target_pairs={{0,1},{1,0},{2,3},{3,2},{4,5},{5,4},{6,7},{7,6},{8,9},{9,8},{10,11... | collective-permute-start | bytes 393224 | tf_op jit(solution)/shard_map/ppermute | solution.py:833
  37.1 10.0 %collective-permute-start.6 = (bf16[576,128]{1,0:T(8,128)(2,1)}, bf16[576,128]{1,0:T(8,128)(2,1)S(1)}, u32[]{:S(2)}, u32[]{:S(2)}) collective-permute-start(bf16[576,128]{1,0:T(8,128)(2,1)} %collective-permute-done.5.refs_2_), channel_id=1, source_target_pairs={{0,8},{4,12},{8,0},{12,4},{16,24},{20,28},{24,16},{28,20},{1,9},{5... | collective-permute-start | bytes 442376 | tf_op jit(solution)/shard_map/ppermute | solution.py:836
  38.6 8.6 %collective-permute-start.7 = (bf16[576,128]{1,0:T(8,128)(2,1)}, bf16[576,128]{1,0:T(8,128)(2,1)S(1)}, u32[]{:S(2)}, u32[]{:S(2)}) collective-permute-start(bf16[576,128]{1,0:T(8,128)(2,1)} %collective-permute-done.5.refs_2_), channel_id=1, source_target_pairs={{0,16},{4,20},{8,24},{12,28},{16,0},{20,4},{24,8},{28,12},{1,17},{... | collective-permute-start | bytes 442376 | tf_op jit(solution)/shard_map/ppermute | solution.py:836
  40.1 7.1 %collective-permute-start.8 = (bf16[576,128]{1,0:T(8,128)(2,1)}, bf16[576,128]{1,0:T(8,128)(2,1)S(1)}, u32[]{:S(2)}, u32[]{:S(2)}) collective-permute-start(bf16[576,128]{1,0:T(8,128)(2,1)} %collective-permute-done.5.refs_2_), channel_id=1, source_target_pairs={{0,24},{4,28},{8,16},{12,20},{16,8},{20,12},{24,0},{28,4},{1,25},{... | collective-permute-start | bytes 442376 | tf_op jit(solution)/shard_map/ppermute | solution.py:836
  50.3 4.4 %collective-permute-start.9 = (bf16[576,128]{1,0:T(8,128)(2,1)}, bf16[576,128]{1,0:T(8,128)(2,1)S(1)}, u32[]{:S(2)}, u32[]{:S(2)}) collective-permute-start(bf16[576,128]{1,0:T(8,128)(2,1)} %collective-permute-done.5.refs_2_), channel_id=1, source_target_pairs={{0,4},{4,0},{8,12},{12,8},{16,20},{20,16},{24,28},{28,24},{1,5},{5... | collective-permute-start | bytes 442376 | tf_op jit(solution)/shard_map/ppermute | solution.py:836
  51.4 9.8 %collective-permute-start.3 = (bf16[128,512]{1,0:T(8,128)(2,1)S(1)}, bf16[128,512]{1,0:T(8,128)(2,1)S(1)}, u32[]{:S(2)}, u32[]{:S(2)}) collective-permute-start(bf16[128,512]{1,0:T(8,128)(2,1)S(1)} %pad_maximum_fusion.5), channel_id=1, source_target_pairs={{0,4},{4,8},{8,12},{12,16},{16,20},{20,24},{24,28},{28,0},{1,5},{5... | collective-permute-start | bytes 393224 | tf_op jit(solution)/shard_map/ppermute | solution.py:839
  51.9 9.2 %collective-permute-start.4 = (bf16[128,512]{1,0:T(8,128)(2,1)S(1)}, bf16[128,512]{1,0:T(8,128)(2,1)S(1)}, u32[]{:S(2)}, u32[]{:S(2)}) collective-permute-start(bf16[128,512]{1,0:T(8,128)(2,1)S(1)} %pad_maximum_fusion.6), channel_id=1, source_target_pairs={{0,28},{4,0},{8,4},{12,8},{16,12},{20,16},{24,20},{28,24},{1,29},{... | collective-permute-start | bytes 393224 | tf_op jit(solution)/shard_map/ppermute | solution.py:839
  54.1 2.1 collective-permute-start.10
  54.2 2.1 collective-permute-start.11
  67.4 10.7 %collective-permute-start.13 = (bf16[640,256]{1,0:T(8,128)(2,1)}, bf16[640,256]{1,0:T(8,128)(2,1)S(1)}, u32[]{:S(2)}, u32[]{:S(2)}) collective-permute-start(bf16[640,256]{1,0:T(8,128)(2,1)} %get-tuple-element.87.refs_1_.refs_3_), channel_id=1, source_target_pairs={{0,1},{1,0},{2,3},{3,2},{4,5},{5,4},{6,7},{7,6},{8,9},{9,8},{10,11... | collective-permute-start | bytes 983048 | tf_op jit(solution)/shard_map/ppermute | solution.py:833
  67.8 13.0 %all-to-all-start.1 = ((f32[16,8,256]{2,1,0:T(8,128)}), f32[16,8,256]{2,1,0:T(8,128)S(1)}, u32[]{:S(2)}, u32[]{:S(2)}) async-start(f32[16,8,256]{2,1,0:T(8,128)} %get-tuple-element.88), calls=%async_computation.1 | async-start | bytes 262144 | tf_op jit(solution)/shard_map/all_to_all | solution.py:852
  71.7 42.1 %reduce-scatter.2.cloned.1.call-start = ((), (), s32[]{:S(2)}) async-start(), calls=%async_computation.10 | async-start | bytes 348160 | tf_op jit(solution)/shard_map/reduce_scatter | solution.py:946
  78.9 26.0 %collective-permute-start.16 = (bf16[512,128]{1,0:T(8,128)(2,1)}, bf16[512,128]{1,0:T(8,128)(2,1)S(1)}, u32[]{:S(2)}, u32[]{:S(2)}) collective-permute-start(bf16[512,128]{1,0:T(8,128)(2,1)} %get-tuple-element.96), channel_id=1, source_target_pairs={{0,2},{1,3},{2,0},{3,1},{4,6},{5,7},{6,4},{7,5},{8,10},{9,11},{10,... | collective-permute-start | bytes 393224 | tf_op jit(solution)/shard_map/ppermute | solution.py:833
  87.0 19.1 %collective-permute-start.15 = (bf16[512,256]{1,0:T(8,128)(2,1)}, bf16[512,256]{1,0:T(8,128)(2,1)S(1)}, u32[]{:S(2)}, u32[]{:S(2)}) collective-permute-start(bf16[512,256]{1,0:T(8,128)(2,1)} %get-tuple-element.92.refs_1_.refs_3_.refs_5_), channel_id=1, source_target_pairs={{0,1},{1,0},{2,3},{3,2},{4,5},{5,4},{6,7},{7,6},{8,9},{9,8},{10,11... | collective-permute-start | bytes 786440 | tf_op jit(solution)/shard_map/ppermute | solution.py:833
  88.5 25.4 %all-to-all-start.2 = ((f32[16,8,256]{2,1,0:T(8,128)}), f32[16,8,256]{2,1,0:T(8,128)S(1)}, u32[]{:S(2)}, u32[]{:S(2)}) async-start(f32[16,8,256]{2,1,0:T(8,128)} %get-tuple-element.93), calls=%async_computation.2 | async-start | bytes 262144 | tf_op jit(solution)/shard_map/all_to_all | solution.py:852
  103.3 7.4 %collective-permute-start.17 = (bf16[512,128]{1,0:T(8,128)(2,1)S(1)}, bf16[512,128]{1,0:T(8,128)(2,1)S(1)}, u32[]{:S(2)}, u32[]{:S(2)}) collective-permute-start(bf16[512,128]{1,0:T(8,128)(2,1)S(1)} %copy-done.13), channel_id=1, source_target_pairs={{0,1},{1,0},{2,3},{3,2},{4,5},{5,4},{6,7},{7,6},{8,9},{9,8},{10,11... | collective-permute-start | bytes 393224 | tf_op jit(solution)/shard_map/ppermute | solution.py:833
  105.0 8.1 %collective-permute-start.18 = (bf16[512,128]{1,0:T(8,128)(2,1)S(1)}, bf16[512,128]{1,0:T(8,128)(2,1)S(1)}, u32[]{:S(2)}, u32[]{:S(2)}) collective-permute-start(bf16[512,128]{1,0:T(8,128)(2,1)S(1)} %collective-permute-done.16), channel_id=1, source_target_pairs={{0,1},{1,0},{2,3},{3,2},{4,5},{5,4},{6,7},{7,6},{8,9},{9,8},{10,11... | collective-permute-start | bytes 393224 | tf_op jit(solution)/shard_map/ppermute | solution.py:833
  118.8 21.9 %all-to-all-start.3 = ((bf16[8,256,256]{2,1,0:T(8,128)(2,1)}), bf16[8,256,256]{2,1,0:T(8,128)(2,1)S(1)}, u32[]{:S(2)}, u32[]{:S(2)}) async-start(bf16[8,256,256]{2,1,0:T(8,128)(2,1)} %bitcast.87), calls=%async_computation.4 | async-start | bytes 2097152 | tf_op jit(solution)/shard_map/all_to_all | solution.py:1009
  123.6 15.4 %collective-permute-start.19 = (bf16[128,256]{1,0:T(8,128)(2,1)S(1)}, bf16[128,256]{1,0:T(8,128)(2,1)S(1)}, u32[]{:S(2)}, u32[]{:S(2)}) collective-permute-start(bf16[128,256]{1,0:T(8,128)(2,1)S(1)} %get-tuple-element.175), channel_id=1, source_target_pairs={{0,4},{4,8},{8,12},{12,16},{16,20},{20,24},{24,28},{28,0},{1,5},{5... | collective-permute-start | bytes 196616 | tf_op jit(solution)/shard_map/ppermute | solution.py:839
  124.2 14.8 %collective-permute-start.20 = (bf16[128,256]{1,0:T(8,128)(2,1)S(1)}, bf16[128,256]{1,0:T(8,128)(2,1)S(1)}, u32[]{:S(2)}, u32[]{:S(2)}) collective-permute-start(bf16[128,256]{1,0:T(8,128)(2,1)S(1)} %get-tuple-element.174), channel_id=1, source_target_pairs={{0,28},{4,0},{8,4},{12,8},{16,12},{20,16},{24,20},{28,24},{1,29},{... | collective-permute-start | bytes 196616 | tf_op jit(solution)/shard_map/ppermute | solution.py:839
  126.4 14.3 %collective-permute-start.23 = (bf16[256,512]{1,0:T(8,128)(2,1)}, bf16[256,512]{1,0:T(8,128)(2,1)S(1)}, u32[]{:S(2)}, u32[]{:S(2)}) collective-permute-start(bf16[256,512]{1,0:T(8,128)(2,1)} %get-tuple-element.102.refs_1_), channel_id=1, source_target_pairs={{0,2},{1,3},{2,0},{3,1},{4,6},{5,7},{6,4},{7,5},{8,10},{9,11},{10,... | collective-permute-start | bytes 786440 | tf_op jit(solution)/shard_map/ppermute | solution.py:833
  127.0 13.4 %collective-permute-start.21 = (bf16[128,256]{1,0:T(8,128)(2,1)S(1)}, bf16[128,256]{1,0:T(8,128)(2,1)S(1)}, u32[]{:S(2)}, u32[]{:S(2)}) collective-permute-start(bf16[128,256]{1,0:T(8,128)(2,1)S(1)} %get-tuple-element.173), channel_id=1, source_target_pairs={{0,4},{4,8},{8,12},{12,16},{16,20},{20,24},{24,28},{28,0},{1,5},{5... | collective-permute-start | bytes 196616 | tf_op jit(solution)/shard_map/ppermute | solution.py:839
  127.0 13.4 %collective-permute-start.22 = (bf16[128,256]{1,0:T(8,128)(2,1)S(1)}, bf16[128,256]{1,0:T(8,128)(2,1)S(1)}, u32[]{:S(2)}, u32[]{:S(2)}) collective-permute-start(bf16[128,256]{1,0:T(8,128)(2,1)S(1)} %get-tuple-element.172), channel_id=1, source_target_pairs={{0,28},{4,0},{8,4},{12,8},{16,12},{20,16},{24,20},{28,24},{1,29},{... | collective-permute-start | bytes 196616 | tf_op jit(solution)/shard_map/ppermute | solution.py:839
  143.5 2.0 collective-permute-start.24
  143.6 37.4 %collective-permute-start.26 = (bf16[768,512]{1,0:T(8,128)(2,1)S(1)}, bf16[768,512]{1,0:T(8,128)(2,1)S(1)}, u32[]{:S(2)}, u32[]{:S(2)}) collective-permute-start(bf16[768,512]{1,0:T(8,128)(2,1)S(1)} %copy-done.18), channel_id=1, source_target_pairs={{0,2},{1,3},{2,0},{3,1},{4,6},{5,7},{6,4},{7,5},{8,10},{9,11},{10,... | collective-permute-start | bytes 2359304 | tf_op jit(solution)/shard_map/ppermute | solution.py:833
  179.8 2.2 collective-permute-start.25
  185.5 19.0 %all-to-all-start.4 = ((bf16[8,256,256]{2,1,0:T(8,128)(2,1)}), bf16[8,256,256]{2,1,0:T(8,128)(2,1)S(1)}, u32[]{:S(2)}, u32[]{:S(2)}) async-start(bf16[8,256,256]{2,1,0:T(8,128)(2,1)} %bitcast.88), calls=%async_computation.5 | async-start | bytes 2097152 | tf_op jit(solution)/shard_map/all_to_all | solution.py:1044
  189.2 66.5 %all-gather.7.cloned.1.call-start = ((), (), s32[]{:S(2)}) async-start(), calls=%async_computation.12 | async-start | bytes 1179648 | tf_op jit(solution)/shard_map/all_gather | solution.py:1055
  190.7 5.5 %collective-permute-start.28 = (bf16[260,128]{1,0:T(8,128)(2,1)S(1)}, bf16[260,128]{1,0:T(8,128)(2,1)S(1)}, u32[]{:S(2)}, u32[]{:S(2)}) collective-permute-start(bf16[260,128]{1,0:T(8,128)(2,1)S(1)} %fusion.5.refs_2_), channel_id=1, source_target_pairs={{0,1},{1,0},{2,3},{3,2},{4,5},{5,4},{6,7},{7,6},{8,9},{9,8},{10,11... | collective-permute-start | bytes 199688 | tf_op jit(solution)/shard_map/ppermute | solution.py:833
  191.1 8.6 %collective-permute-start.29 = (bf16[260,128]{1,0:T(8,128)(2,1)S(1)}, bf16[260,128]{1,0:T(8,128)(2,1)S(1)}, u32[]{:S(2)}, u32[]{:S(2)}) collective-permute-start(bf16[260,128]{1,0:T(8,128)(2,1)S(1)} %fusion.5.refs_2_), channel_id=1, source_target_pairs={{0,2},{1,3},{2,0},{3,1},{4,6},{5,7},{6,4},{7,5},{8,10},{9,11},{10,... | collective-permute-start | bytes 199688 | tf_op jit(solution)/shard_map/ppermute | solution.py:833
  192.2 7.5 %collective-permute-start.30 = (bf16[260,128]{1,0:T(8,128)(2,1)S(1)}, bf16[260,128]{1,0:T(8,128)(2,1)S(1)}, u32[]{:S(2)}, u32[]{:S(2)}) collective-permute-start(bf16[260,128]{1,0:T(8,128)(2,1)S(1)} %fusion.5.refs_2_), channel_id=1, source_target_pairs={{0,3},{1,2},{2,1},{3,0},{4,7},{5,6},{6,5},{7,4},{8,11},{9,10},{10,... | collective-permute-start | bytes 199688 | tf_op jit(solution)/shard_map/ppermute | solution.py:833
  209.0 6.6 %collective-permute-start.31 = (bf16[512,256]{1,0:T(8,128)(2,1)}, bf16[512,256]{1,0:T(8,128)(2,1)S(1)}, u32[]{:S(2)}, u32[]{:S(2)}) collective-permute-start(bf16[512,256]{1,0:T(8,128)(2,1)} %get-tuple-element.110), channel_id=1, source_target_pairs={{0,1},{1,0},{2,3},{3,2},{4,5},{5,4},{6,7},{7,6},{8,9},{9,8},{10,11... | collective-permute-start | bytes 786440 | tf_op jit(solution)/shard_map/ppermute | solution.py:833
  209.3 15.1 %all-to-all-start.5 = ((f32[16,8,256]{2,1,0:T(8,128)}), f32[16,8,256]{2,1,0:T(8,128)S(1)}, u32[]{:S(2)}, u32[]{:S(2)}) async-start(f32[16,8,256]{2,1,0:T(8,128)} %get-tuple-element.114), calls=%async_computation.6 | async-start | bytes 262144 | tf_op jit(solution)/shard_map/all_to_all | solution.py:852
  216.7 7.7 %collective-permute-start.32 = (bf16[128,256]{1,0:T(8,128)(2,1)S(1)}, bf16[128,256]{1,0:T(8,128)(2,1)S(1)}, u32[]{:S(2)}, u32[]{:S(2)}) collective-permute-start(bf16[128,256]{1,0:T(8,128)(2,1)S(1)} %get-tuple-element.156), channel_id=1, source_target_pairs={{0,4},{4,8},{8,12},{12,16},{16,20},{20,24},{24,28},{28,0},{1,5},{5... | collective-permute-start | bytes 196616 | tf_op jit(solution)/shard_map/ppermute | solution.py:839
  216.7 7.6 %collective-permute-start.33 = (bf16[128,256]{1,0:T(8,128)(2,1)S(1)}, bf16[128,256]{1,0:T(8,128)(2,1)S(1)}, u32[]{:S(2)}, u32[]{:S(2)}) collective-permute-start(bf16[128,256]{1,0:T(8,128)(2,1)S(1)} %get-tuple-element.155), channel_id=1, source_target_pairs={{0,28},{4,0},{8,4},{12,8},{16,12},{20,16},{24,20},{28,24},{1,29},{... | collective-permute-start | bytes 196616 | tf_op jit(solution)/shard_map/ppermute | solution.py:839
  228.1 10.5 %collective-permute-start.35 = (bf16[640,128]{1,0:T(8,128)(2,1)}, bf16[640,128]{1,0:T(8,128)(2,1)S(1)}, u32[]{:S(2)}, u32[]{:S(2)}) collective-permute-start(bf16[640,128]{1,0:T(8,128)(2,1)} %get-tuple-element.119), channel_id=1, source_target_pairs={{0,2},{1,3},{2,0},{3,1},{4,6},{5,7},{6,4},{7,5},{8,10},{9,11},{10,... | collective-permute-start | bytes 491528 | tf_op jit(solution)/shard_map/ppermute | solution.py:833
  235.1 10.4 %collective-permute-start.34 = (bf16[640,256]{1,0:T(8,128)(2,1)}, bf16[640,256]{1,0:T(8,128)(2,1)S(1)}, u32[]{:S(2)}, u32[]{:S(2)}) collective-permute-start(bf16[640,256]{1,0:T(8,128)(2,1)} %get-tuple-element.117), channel_id=1, source_target_pairs={{0,1},{1,0},{2,3},{3,2},{4,5},{5,4},{6,7},{7,6},{8,9},{9,8},{10,11... | collective-permute-start | bytes 983048 | tf_op jit(solution)/shard_map/ppermute | solution.py:833
  239.3 12.0 %all-to-all-start.6 = ((f32[16,8,256]{2,1,0:T(8,128)}), f32[16,8,256]{2,1,0:T(8,128)S(1)}, u32[]{:S(2)}, u32[]{:S(2)}) async-start(f32[16,8,256]{2,1,0:T(8,128)} %shard_map.318), calls=%async_computation.7 | async-start | bytes 262144 | tf_op jit(solution)/shard_map/all_to_all | solution.py:852
  251.9 31.8 %all-to-all-start.7 = ((bf16[8,1088,128]{2,1,0:T(8,128)(2,1)}), bf16[8,1088,128]{2,1,0:T(8,128)(2,1)S(1)}, u32[]{:S(2)}, u32[]{:S(2)}) async-start(bf16[8,1088,128]{2,1,0:T(8,128)(2,1)} %shard_map.319.refs_7_), calls=%async_computation.8 | async-start | bytes 4456448 | tf_op jit(solution)/shard_map/all_to_all | solution.py:1113
  258.8 10.3 %collective-permute-start.36 = (bf16[640,128]{1,0:T(8,128)(2,1)}, bf16[640,128]{1,0:T(8,128)(2,1)S(1)}, u32[]{:S(2)}, u32[]{:S(2)}) collective-permute-start(bf16[640,128]{1,0:T(8,128)(2,1)} %get-tuple-element.121), channel_id=1, source_target_pairs={{0,2},{1,3},{2,0},{3,1},{4,6},{5,7},{6,4},{7,5},{8,10},{9,11},{10,... | collective-permute-start | bytes 491528 | tf_op jit(solution)/shard_map/ppermute | solution.py:833
  274.6 2.2 collective-permute-start.38
  280.0 14.0 %collective-permute-start.40 = (bf16[576,128]{1,0:T(8,128)(2,1)}, bf16[576,128]{1,0:T(8,128)(2,1)S(1)}, u32[]{:S(2)}, u32[]{:S(2)}) collective-permute-start(bf16[576,128]{1,0:T(8,128)(2,1)} %get-tuple-element.127), channel_id=1, source_target_pairs={{0,8},{4,12},{8,0},{12,4},{16,24},{20,28},{24,16},{28,20},{1,9},{5... | collective-permute-start | bytes 442376 | tf_op jit(solution)/shard_map/ppermute | solution.py:836
  281.7 14.3 %collective-permute-start.41 = (bf16[576,128]{1,0:T(8,128)(2,1)}, bf16[576,128]{1,0:T(8,128)(2,1)S(1)}, u32[]{:S(2)}, u32[]{:S(2)}) collective-permute-start(bf16[576,128]{1,0:T(8,128)(2,1)} %get-tuple-element.128), channel_id=1, source_target_pairs={{0,16},{4,20},{8,24},{12,28},{16,0},{20,4},{24,8},{28,12},{1,17},{... | collective-permute-start | bytes 442376 | tf_op jit(solution)/shard_map/ppermute | solution.py:836
  283.2 12.9 %collective-permute-start.42 = (bf16[576,128]{1,0:T(8,128)(2,1)}, bf16[576,128]{1,0:T(8,128)(2,1)S(1)}, u32[]{:S(2)}, u32[]{:S(2)}) collective-permute-start(bf16[576,128]{1,0:T(8,128)(2,1)} %get-tuple-element.129), channel_id=1, source_target_pairs={{0,24},{4,28},{8,16},{12,20},{16,8},{20,12},{24,0},{28,4},{1,25},{... | collective-permute-start | bytes 442376 | tf_op jit(solution)/shard_map/ppermute | solution.py:836
  287.4 8.7 %collective-permute-start.39 = (bf16[256,128]{1,0:T(8,128)(2,1)}, bf16[256,128]{1,0:T(8,128)(2,1)S(1)}, u32[]{:S(2)}, u32[]{:S(2)}) collective-permute-start(bf16[256,128]{1,0:T(8,128)(2,1)} %shard_map.325), channel_id=1, source_target_pairs={{0,2},{1,3},{2,0},{3,1},{4,6},{5,7},{6,4},{7,5},{8,10},{9,11},{10,... | collective-permute-start | bytes 196616 | tf_op jit(solution)/shard_map/ppermute | solution.py:833
  287.8 26.5 %collective-permute-start.44 = (bf16[512,256]{1,0:T(8,128)(2,1)}, bf16[512,256]{1,0:T(8,128)(2,1)S(1)}, u32[]{:S(2)}, u32[]{:S(2)}) collective-permute-start(bf16[512,256]{1,0:T(8,128)(2,1)} %get-tuple-element.132), channel_id=1, source_target_pairs={{0,1},{1,0},{2,3},{3,2},{4,5},{5,4},{6,7},{7,6},{8,9},{9,8},{10,11... | collective-permute-start | bytes 786440 | tf_op jit(solution)/shard_map/ppermute | solution.py:833
  289.9 22.1 %all-to-all-start.8 = ((f32[16,8,256]{2,1,0:T(8,128)}), f32[16,8,256]{2,1,0:T(8,128)S(1)}, u32[]{:S(2)}, u32[]{:S(2)}) async-start(f32[16,8,256]{2,1,0:T(8,128)} %shard_map.328), calls=%async_computation.9 | async-start | bytes 262144 | tf_op jit(solution)/shard_map/all_to_all | solution.py:852
  294.1 13.4 %collective-permute-start.37 = (bf16[512,256]{1,0:T(8,128)(2,1)S(1)}, bf16[512,256]{1,0:T(8,128)(2,1)S(1)}, u32[]{:S(2)}, u32[]{:S(2)}) collective-permute-start(bf16[512,256]{1,0:T(8,128)(2,1)S(1)} %copy-done.51), channel_id=1, source_target_pairs={{0,1},{1,0},{2,3},{3,2},{4,5},{5,4},{6,7},{7,6},{8,9},{9,8},{10,11... | collective-permute-start | bytes 786440 | tf_op jit(solution)/shard_map/ppermute | solution.py:833
  300.2 25.4 %collective-permute-start.46 = (bf16[1408,128]{1,0:T(8,128)(2,1)}, bf16[1408,128]{1,0:T(8,128)(2,1)S(1)}, u32[]{:S(2)}, u32[]{:S(2)}) collective-permute-start(bf16[1408,128]{1,0:T(8,128)(2,1)} %shard_map.326.refs_4_.refs_8_.refs_5_.refs_2_.refs_1_), channel_id=1, source_target_pairs={{0,8},{4,12},{8,0},{12,4},{16,24},{20,28},{24,16},{28,20},{1,9},{5... | collective-permute-start | bytes 1081352 | tf_op jit(solution)/shard_map/ppermute | solution.py:836
  301.7 24.4 %collective-permute-start.47 = (bf16[1408,128]{1,0:T(8,128)(2,1)}, bf16[1408,128]{1,0:T(8,128)(2,1)S(1)}, u32[]{:S(2)}, u32[]{:S(2)}) collective-permute-start(bf16[1408,128]{1,0:T(8,128)(2,1)} %shard_map.326.refs_4_.refs_8_.refs_5_.refs_2_.refs_1_), channel_id=1, source_target_pairs={{0,16},{4,20},{8,24},{12,28},{16,0},{20,4},{24,8},{28,12},{1,17},{... | collective-permute-start | bytes 1081352 | tf_op jit(solution)/shard_map/ppermute | solution.py:836
  303.2 23.1 %collective-permute-start.48 = (bf16[1408,128]{1,0:T(8,128)(2,1)}, bf16[1408,128]{1,0:T(8,128)(2,1)S(1)}, u32[]{:S(2)}, u32[]{:S(2)}) collective-permute-start(bf16[1408,128]{1,0:T(8,128)(2,1)} %shard_map.326.refs_4_.refs_8_.refs_5_.refs_2_.refs_1_), channel_id=1, source_target_pairs={{0,24},{4,28},{8,16},{12,20},{16,8},{20,12},{24,0},{28,4},{1,25},{... | collective-permute-start | bytes 1081352 | tf_op jit(solution)/shard_map/ppermute | solution.py:836
  310.3 15.3 %collective-permute-start.43 = (bf16[512,128]{1,0:T(8,128)(2,1)}, bf16[512,128]{1,0:T(8,128)(2,1)S(1)}, u32[]{:S(2)}, u32[]{:S(2)}) collective-permute-start(bf16[512,128]{1,0:T(8,128)(2,1)} %get-tuple-element.131), channel_id=1, source_target_pairs={{0,2},{1,3},{2,0},{3,1},{4,6},{5,7},{6,4},{7,5},{8,10},{9,11},{10,... | collective-permute-start | bytes 393224 | tf_op jit(solution)/shard_map/ppermute | solution.py:833
  314.3 4.8 %collective-permute-start.53 = (f32[8,128]{1,0:T(8,128)}, f32[8,128]{1,0:T(8,128)S(1)}, u32[]{:S(2)}, u32[]{:S(2)}) collective-permute-start(f32[8,128]{1,0:T(8,128)} %get-tuple-element.140), channel_id=1, source_target_pairs={{0,2},{1,3},{2,0},{3,1},{4,6},{5,7},{6,4},{7,5},{8,10},{9,11},{10,... | collective-permute-start | bytes 12296 | tf_op jit(solution)/shard_map/ppermute | solution.py:833
  319.1 7.6 %collective-permute-start.45 = (bf16[512,128]{1,0:T(8,128)(2,1)}, bf16[512,128]{1,0:T(8,128)(2,1)S(1)}, u32[]{:S(2)}, u32[]{:S(2)}) collective-permute-start(bf16[512,128]{1,0:T(8,128)(2,1)} %get-tuple-element.136), channel_id=1, source_target_pairs={{0,2},{1,3},{2,0},{3,1},{4,6},{5,7},{6,4},{7,5},{8,10},{9,11},{10,... | collective-permute-start | bytes 393224 | tf_op jit(solution)/shard_map/ppermute | solution.py:833
  325.6 3.8 %collective-permute-start.49 = (bf16[1408,128]{1,0:T(8,128)(2,1)S(1)}, bf16[1408,128]{1,0:T(8,128)(2,1)S(1)}, u32[]{:S(2)}, u32[]{:S(2)}) collective-permute-start(bf16[1408,128]{1,0:T(8,128)(2,1)S(1)} %copy-done.5), channel_id=1, source_target_pairs={{0,4},{4,0},{8,12},{12,8},{16,20},{20,16},{24,28},{28,24},{1,5},{5... | collective-permute-start | bytes 1081352 | tf_op jit(solution)/shard_map/ppermute | solution.py:836
  325.7 3.7 %collective-permute-start.50 = (bf16[1408,128]{1,0:T(8,128)(2,1)S(1)}, bf16[1408,128]{1,0:T(8,128)(2,1)S(1)}, u32[]{:S(2)}, u32[]{:S(2)}) collective-permute-start(bf16[1408,128]{1,0:T(8,128)(2,1)S(1)} %collective-permute-done.46.refs_2_), channel_id=1, source_target_pairs={{0,4},{4,0},{8,12},{12,8},{16,20},{20,16},{24,28},{28,24},{1,5},{5... | collective-permute-start | bytes 1081352 | tf_op jit(solution)/shard_map/ppermute | solution.py:836
  326.1 3.3 collective-permute-start.51
  326.2 3.2 collective-permute-start.52
  (79 other events, 261.2 us)
Sparse Core Ops, SparseCore 0:
  48.7 25.2 all-gather.4
  203.5 23.8 all-gather.6
Sparse Core Ops, SparseCore 1:
  80.9 19.5 reduce-scatter.1

commit v2 on v1

--- a/solution.py
+++ b/solution.py
@@ -1123,13 +1123,24 @@
     (proj_late,) = after((proj_oth,), there1)
     r1 = over_ch(p1_oth, 1)
     stats1 = to_image(st1)
+    if blocks == 8:
+        ctx_grad = call(
+            functools.partial(context_place_kernel, split=split),
+            [scal, ctx_all],
+            [((context.shape[2], 2, channels), F32)],
+            deps=[p1_own],
+            time=10.0,
+        )[0]
+    else:
+        ctx_grad = ctx_all.reshape(2, 2, split, features, 2, 2, HEAD)
+        ctx_grad = jnp.transpose(ctx_grad, (2, 3, 5, 0, 4, 1, 6)).astype(F32)
     half_shape = (4, 9 * channels // 8, LANES)
     keep1, send1 = call(
         weight_grad_one_kernel,
         [scal, act_first, act_rest, first_there, rest_there, ext1, there1],
         [(half_shape, F32), (half_shape, BF)],
         [((2 * pix, 9 * LANES), BF), ((9 * channels, LANES), F32)],
-        deps=[p1_own],
+        deps=[p1_own, ctx_grad],
         time=20.0,
     )
     if blocks == 8:
@@ -1187,23 +1198,14 @@
         time=10.0,
     )
     if blocks == 8:
-        ctx_grad = call(
-            functools.partial(context_place_kernel, split=split),
-            [scal, ctx_all],
-            [((context.shape[2], 2, channels), F32)],
-            deps=[total],
-            time=10.0,
-        )[0]
         grad1, grad2, qkv_grad, out_grad = call(
             place_kernel,
             [scal] + plane(total),
             [((9 * channels, LANES), F32)] * 2
             + [((3 * channels, LANES), F32), ((LANES, channels), F32)],
-            deps=[block_output, ctx_grad, bias_grad],
+            deps=[block_output, bias_grad],
         )
     else:
-        ctx_grad = ctx_all.reshape(2, 2, split, features, 2, 2, HEAD)
-        ctx_grad = jnp.transpose(ctx_grad, (2, 3, 5, 0, 4, 1, 6)).astype(F32)
         flip = lambda c: jnp.where(b % 2 == 0, *((keep1.astype(BF), send1)[:: 1 - 2 * c]))
         grad1 = lax.psum(jnp.concatenate([flip(0), flip(1)], axis=0), "blk").astype(F32)
         sums = lax.psum(part2, "blk").astype(F32)

time: 349 us -> 352 us (level)
  waiting for transfers between devices: 42.5 us -> 48.9 us
    all_to_all x1, waiting for transfers between devices: 0.12 us -> 6.88 us  [body(): parts2 = lax.all_to_all(part2, 'blk', 0, 0)]
    unnamed x160 -> x158, local copies, waits for them, and re-layouts: 23.3 us -> 22.5 us
  transfers between devices with their start and end apart: 66 -> 66, of which waited for: 23 -> 24; matrix products, arithmetic and copies ran while one was open for 6% -> 6% of each run, Pallas kernels for 36% -> 35%
where the time goes in v2:
time: 352 us; the launch traced here: 346 us
  Pallas kernels  134 us (38%)
  starting transfers between devices  101 us (29%)
  waiting for transfers between devices  48.9 us (14%)
  local copies, waits for them, and re-layouts  33.8 us (10%)
  between operations  17.9 us (5%)
  other arithmetic  9.19 us (3%)
    pallas_call x29, Pallas kernels, call(): pl.pallas_call(inner, in_specs=[in_smem] + [in_vmem] * (count - 1) + [any...  100 us
    pallas_call x1, Pallas kernels, attend(): pl.pallas_call(inner, grid=(queries // block,), in_specs=[pl.BlockSpec(me...  33.5 us
    ppermute x25, starting transfers between devices, over_ch(): return lax.ppermute(value, 'ch', [(n, n ^ mask) for n in range(4)])  31 us
    all_to_all x5, starting transfers between devices, to_image(): return lax.all_to_all(value, ('blk', 'ch'), 0, 0, axis_index_groups=pairs)  30.2 us
    unnamed x158, local copies, waits for them, and re-layouts  22.5 us
    ppermute x25, waiting for transfers between devices, over_ch(): return lax.ppermute(value, 'ch', [(n, n ^ mask) for n in range(4)])  19.5 us
    ppermute x21, starting transfers between devices, over_blk(): return lax.ppermute(value, 'blk', [(n, n ^ mask) for n in range(blocks)])  13 us
    ppermute x8, starting transfers between devices, ring(): lax.ppermute(value, 'blk', [(n, (n + step) % blocks) for n in range(block...  10.9 us
  transfers between devices with their start and end apart: 66, of which 24 were waited for; matrix products, arithmetic and copies ran while one was open for 6% of the time, Pallas kernels for 35%

profile of v2, /device:TPU:0, one launch (start us, length us, event | category | flops | bytes accessed | tf_op | source)
XLA Modules:
  0.0 346.0 jit_solution(12363407790183394041)
XLA Ops:
  9.1 4.1 %collective-permute-start.5 = (bf16[576,128]{1,0:T(8,128)(2,1)S(1)}, bf16[576,128]{1,0:T(8,128)(2,1)}, u32[]{:S(2)}, u32[]{:S(2)}) collective-permute-start(bf16[576,128]{1,0:T(8,128)(2,1)S(1)} %constant_dynamic-slice_fusion.4.refs_2_), channel_id=1, source_target_pairs={{0,2},{1,3},{2,0},{3,1},{4,6},{5,7},{6,4},{7,5},{8,10},{9,11},{10,... | collective-permute-start | bytes 442376 | tf_op jit(solution)/shard_map/ppermute | solution.py:833
  13.9 1.7 shard_map.298
  18.2 1.9 concatenate.41.refs_2_.refs_3_
  20.1 1.9 collective-permute-start.1
  22.0 1.8 shard_map.299.refs_2_
  23.7 4.8 %all-to-all-start = ((f32[32,16,128]{2,1,0:T(8,128)}), f32[32,16,128]{2,1,0:T(8,128)S(1)}, u32[]{:S(2)}, u32[]{:S(2)}) async-start(f32[32,16,128]{2,1,0:T(8,128)} %shard_map.299.refs_2_), calls=%async_computation | async-start | bytes 524288 | tf_op jit(solution)/shard_map/all_to_all | solution.py:908
  31.4 2.7 collective-permute-start.14
  41.3 1.7 shard_map.301
  52.0 2.2 collective-permute-start.4
  57.7 3.5 %shard_map.300.refs_6_.refs_2_ = bf16[4608,256]{1,0:T(8,128)(2,1)} custom-call(s32[8]{0:T(128)} %stack.81.refs_0_, bf16[4608,128]{1,0:T(8,128)(2,1)} %bitcast.92, bf16[576,128]{1,0:T(8,128)(2,1)} %collective-permute-done.5.refs_2_, bf16[576,128]{1,0:T(8,128)(2,1)} %copy-done.21, bf16[576,128]{1,0:T(8,128)(2,1)} %copy-done.23, bf16[576,128]{1,0:T(8,128)(2,1)} %copy-done.25, ...), custom_call_target="tpu_custom_call" | custom-call | flops 1 | bytes 1 | tf_op jit(solution)/shard_map/pallas_call | solution.py:758
  62.0 5.5 %shard_map.302 = (bf16[640,256]{1,0:T(8,128)(2,1)}, f32[16,8,256]{2,1,0:T(8,128)}, bf16[512,512]{1,0:T(8,128)(2,1)}, f32[4,16,128]{2,1,0:T(8,128)}) custom-call(s32[8]{0:T(128)} %stack.81.refs_0_, bf16[512,256]{1,0:T(8,128)(2,1)} %pad_maximum_fusion.refs_1_.refs_6_.refs_3_, bf16[512,256]{1,0:T(8,128)(2,1)} %pad_maximum_fusion.1.refs_2_.refs_4_, ...), custom_call_target="tpu_custom_call" | custom-call | flops 1 | bytes 1 | tf_op jit(solution)/shard_map/pallas_call | solution.py:758
  67.9 3.9 %all-to-all-start.1 = ((f32[16,8,256]{2,1,0:T(8,128)}), f32[16,8,256]{2,1,0:T(8,128)S(1)}, u32[]{:S(2)}, u32[]{:S(2)}) async-start(f32[16,8,256]{2,1,0:T(8,128)} %get-tuple-element.88), calls=%async_computation.1 | async-start | bytes 262144 | tf_op jit(solution)/shard_map/all_to_all | solution.py:852
  71.8 2.2 all-gather.5.cloned.1.call-done
  74.0 3.6 %shard_map.304.refs_5_.refs_3_.refs_2_ = bf16[4608,256]{1,0:T(8,128)(2,1)} custom-call(s32[8]{0:T(128)} %stack.81.refs_0_, bf16[4608,128]{1,0:T(8,128)(2,1)} %bitcast.94, bf16[8,832,128]{2,1,0:T(8,128)(2,1)} %bitcast.82), custom_call_target="tpu_custom_call" | custom-call | flops 1 | bytes 1 | tf_op jit(solution)/shard_map/pallas_call | solution.py:758
  79.0 1.9 collective-permute-start.16
  81.5 5.5 %shard_map.305 = (f32[512,256]{1,0:T(8,128)}, bf16[512,256]{1,0:T(8,128)(2,1)}, f32[16,8,256]{2,1,0:T(8,128)}, bf16[256,512]{1,0:T(8,128)(2,1)}, bf16[768,512]{1,0:T(8,128)(2,1)}, /*index=5*/bf16[2,128,256]{2,1,0:T(8,128)(2,1)}) custom-call(s32[8]{0:T(128)} %stack.81.refs_0_, bf16[640,256]{1,0:T(8,128)(2,1)} %get-tuple-element.87.refs_1_.refs_3_, ...), custom_call_target="tpu_custom_call" | custom-call | flops 1 | bytes 1 | tf_op jit(solution)/shard_map/pallas_call | solution.py:758
  88.5 14.8 %all-to-all-start.2 = ((f32[16,8,256]{2,1,0:T(8,128)}), f32[16,8,256]{2,1,0:T(8,128)S(1)}, u32[]{:S(2)}, u32[]{:S(2)}) async-start(f32[16,8,256]{2,1,0:T(8,128)} %get-tuple-element.93), calls=%async_computation.2 | async-start | bytes 262144 | tf_op jit(solution)/shard_map/all_to_all | solution.py:852
  103.3 1.7 collective-permute-start.17
  106.8 2.9 shard_map.307.refs_7_.refs_2_
  110.7 2.3 collective-permute-done.18
  114.5 4.3 %shard_map.308 = (bf16[4,512,256]{2,1,0:T(8,128)(2,1)}, bf16[512,512]{1,0:T(8,128)(2,1)}, bf16[512,512]{1,0:T(8,128)(2,1)}, bf16[2,128,256]{2,1,0:T(8,128)(2,1)}) custom-call(s32[8]{0:T(128)} %stack.81.refs_0_, bf16[512,256]{1,0:T(8,128)(2,1)} %get-tuple-element.92.refs_1_.refs_3_.refs_5_, bf16[512,256]{1,0:T(8,128)(2,1)} %copy-done.8, ...), custom_call_target="tpu_custom_call" | custom-call | flops 1 | bytes 1 | tf_op jit(solution)/shard_map/pallas_call | solution.py:758
  118.8 3.9 %all-to-all-start.3 = ((bf16[8,256,256]{2,1,0:T(8,128)(2,1)}), bf16[8,256,256]{2,1,0:T(8,128)(2,1)S(1)}, u32[]{:S(2)}, u32[]{:S(2)}) async-start(bf16[8,256,256]{2,1,0:T(8,128)(2,1)} %bitcast.87), calls=%async_computation.4 | async-start | bytes 2097152 | tf_op jit(solution)/shard_map/all_to_all | solution.py:1009
  124.2 2.2 collective-permute-start.20
  127.0 2.6 collective-permute-start.22
  129.7 9.3 %collective-permute-done.19.refs_1_.refs_6_ = bf16[128,256]{1,0:T(8,128)(2,1)S(1)} collective-permute-done((bf16[128,256]{1,0:T(8,128)(2,1)S(1)}, bf16[128,256]{1,0:T(8,128)(2,1)S(1)}, u32[]{:S(2)}, u32[]{:S(2)}) %collective-permute-start.19) | collective-permute-done | bytes 65568 | tf_op jit(solution)/shard_map/ppermute | solution.py:839
  146.3 33.5 %shard_map.311 = (bf16[2048,128]{1,0:T(8,128)(2,1)}, f32[2048,128]{1,0:T(8,128)}, bf16[2048,128]{1,0:T(8,128)(2,1)}, f32[272,128]{1,0:T(8,128)}) custom-call(s32[1]{0:T(128)} %bitcast.28.refs_10_.refs_0_, bf16[2048,256]{1,0:T(8,128)(2,1)} %bitcast.85, bf16[2048,256]{1,0:T(8,128)(2,1)} %bitcast.86, bf16[2048,128]{1,0:T(8,128)(2,1)} %copy-done.71, ...), custom_call_target="tpu_custom_call" | custom-call | flops 43699998720 | bytes 1 | tf_op jit(solution)/shard_map/pallas_call | solution.py:711
  182.8 2.7 shard_map.312
  185.5 3.7 %all-to-all-start.4 = ((bf16[8,256,256]{2,1,0:T(8,128)(2,1)}), bf16[8,256,256]{2,1,0:T(8,128)(2,1)S(1)}, u32[]{:S(2)}, u32[]{:S(2)}) async-start(bf16[8,256,256]{2,1,0:T(8,128)(2,1)} %bitcast.88), calls=%async_computation.5 | async-start | bytes 2097152 | tf_op jit(solution)/shard_map/all_to_all | solution.py:1044
  192.1 3.0 collective-permute-start.30
  196.2 3.4 collective-permute-done.29.refs_4_
  200.8 2.5 shard_map.313.refs_7_
  205.5 3.5 %shard_map.314 = (f32[512,256]{1,0:T(8,128)}, bf16[512,256]{1,0:T(8,128)(2,1)}, f32[16,8,256]{2,1,0:T(8,128)}) custom-call(s32[8]{0:T(128)} %stack.81.refs_0_, bf16[4,512,256]{2,1,0:T(8,128)(2,1)} %bitcast.80, bf16[512,1024]{1,0:T(8,128)(2,1)} %shard_map.307.refs_7_.refs_2_, bf16[512,256]{1,0:T(8,128)(2,1)} %get-tuple-element.92.refs_1_.refs_3_.refs_5_, ...), custom_call_target="tpu_custom_call" | custom-call | flops 1 | bytes 1 | tf_op jit(solution)/shard_map/pallas_call | solution.py:758
  209.2 4.4 %all-to-all-start.5 = ((f32[16,8,256]{2,1,0:T(8,128)}), f32[16,8,256]{2,1,0:T(8,128)S(1)}, u32[]{:S(2)}, u32[]{:S(2)}) async-start(f32[16,8,256]{2,1,0:T(8,128)} %get-tuple-element.114), calls=%async_computation.6 | async-start | bytes 262144 | tf_op jit(solution)/shard_map/all_to_all | solution.py:852
  213.7 1.9 collective-permute-done.31.refs_5_.refs_2_
  216.7 2.6 collective-permute-start.33
  219.4 5.0 %shard_map.315 = (f32[512,256]{1,0:T(8,128)}, bf16[512,256]{1,0:T(8,128)(2,1)}, bf16[2,2048,128]{2,1,0:T(8,128)(2,1)}) custom-call(s32[8]{0:T(128)} %stack.81.refs_0_, bf16[4,512,256]{2,1,0:T(8,128)(2,1)} %bitcast.81, bf16[512,1024]{1,0:T(8,128)(2,1)} %shard_map.307.refs_7_.refs_2_, bf16[512,512]{1,0:T(8,128)(2,1)} %get-tuple-element.107.refs_3_, ...), custom_call_target="tpu_custom_call" | custom-call | flops 1 | bytes 1 | tf_op jit(solution)/shard_map/pallas_call | solution.py:758
  225.0 3.1 shard_map.316
  228.1 1.7 collective-permute-start.35
  229.8 5.3 %shard_map.317 = (f32[640,256]{1,0:T(8,128)}, bf16[640,256]{1,0:T(8,128)(2,1)}, f32[16,8,256]{2,1,0:T(8,128)}) custom-call(s32[8]{0:T(128)} %stack.81.refs_0_, bf16[768,256]{1,0:T(8,128)(2,1)} %get-tuple-element.115.refs_1_.refs_3_, bf16[4608,256]{1,0:T(8,128)(2,1)} %shard_map.304.refs_5_.refs_3_.refs_2_, ...), custom_call_target="tpu_custom_call" | custom-call | flops 9200000000 | bytes 1 | tf_op jit(solution)/shard_map/pallas_call | solution.py:758
  235.3 3.2 collective-permute-done.35.refs_1_.refs_4_
  239.2 3.5 %all-to-all-start.6 = ((f32[16,8,256]{2,1,0:T(8,128)}), f32[16,8,256]{2,1,0:T(8,128)S(1)}, u32[]{:S(2)}, u32[]{:S(2)}) async-start(f32[16,8,256]{2,1,0:T(8,128)} %shard_map.318), calls=%async_computation.7 | async-start | bytes 262144 | tf_op jit(solution)/shard_map/all_to_all | solution.py:852
  242.7 2.7 collective-permute-done.34.refs_6_.refs_2_
  246.2 5.0 %shard_map.319.refs_7_ = bf16[8,1088,128]{2,1,0:T(8,128)(2,1)} custom-call(s32[8]{0:T(128)} %stack.81.refs_0_, bf16[768,512]{1,0:T(8,128)(2,1)} %get-tuple-element.106.refs_1_.refs_2_, bf16[768,512]{1,0:T(8,128)(2,1)} %copy-done.6, bf16[768,256]{1,0:T(8,128)(2,1)} %get-tuple-element.115.refs_1_.refs_3_, bf16[640,128]{1,0:T(8,128)(2,1)} %copy-done.19, ...), custom_call_target="tpu_custom_call" | custom-call | flops 1 | bytes 1 | tf_op jit(solution)/shard_map/pallas_call | solution.py:758
  251.8 3.8 %all-to-all-start.7 = ((bf16[8,1088,128]{2,1,0:T(8,128)(2,1)}), bf16[8,1088,128]{2,1,0:T(8,128)(2,1)S(1)}, u32[]{:S(2)}, u32[]{:S(2)}) async-start(bf16[8,1088,128]{2,1,0:T(8,128)(2,1)} %shard_map.319.refs_7_), calls=%async_computation.8 | async-start | bytes 4456448 | tf_op jit(solution)/shard_map/all_to_all | solution.py:1113
  255.7 3.1 shard_map.320
  259.1 4.8 %shard_map.322 = (f32[512,256]{1,0:T(8,128)}, bf16[512,256]{1,0:T(8,128)(2,1)}, f32[16,8,256]{2,1,0:T(8,128)}) custom-call(s32[8]{0:T(128)} %stack.81.refs_0_, bf16[640,256]{1,0:T(8,128)(2,1)} %get-tuple-element.122.refs_1_.refs_5_, bf16[4608,256]{1,0:T(8,128)(2,1)} %shard_map.300.refs_6_.refs_2_, bf16[512,256]{1,0:T(8,128)(2,1)} %pad_maximum_fusion.refs_1_.refs_6_.refs_3_, ...), custom_call_target="tpu_custom_call" | custom-call | flops 9200000000 | bytes 1 | tf_op jit(solution)/shard_map/pallas_call | solution.py:758
  264.0 3.8 %shard_map.323.refs_8_ = f32[512,2,512]{2,1,0:T(2,128)} custom-call(s32[8]{0:T(128)} %stack.81.refs_0_, bf16[8,256,256]{2,1,0:T(8,128)(2,1)} %bitcast.97, f32[512,256]{1,0:T(8,128)} %get-tuple-element.123.refs_2_.refs_7_.refs_1_), custom_call_target="tpu_custom_call" | custom-call | flops 11500000256 | bytes 1 | tf_op jit(solution)/shard_map/pallas_call | solution.py:758
  269.7 4.9 %shard_map.324 = (f32[4,576,128]{2,1,0:T(8,128)}, bf16[4,576,128]{2,1,0:T(8,128)(2,1)}) custom-call(s32[8]{0:T(128)} %stack.81.refs_0_, bf16[256,512]{1,0:T(8,128)(2,1)} %get-tuple-element.102.refs_1_, bf16[768,512]{1,0:T(8,128)(2,1)} %get-tuple-element.106.refs_1_.refs_2_, bf16[256,512]{1,0:T(8,128)(2,1)} %copy-done.45, bf16[768,512]{1,0:T(8,128)(2,1)} %copy-done.6, ...), custom_call_target="tpu_custom_call" | custom-call | flops 23000000512 | bytes 1 | tf_op jit(solution)/shard_map/pallas_call | solution.py:758
  275.1 1.7 collective-permute-start.44
  276.7 6.9 %all-to-all-done.7.refs_1_.refs_2_ = bf16[8,1088,128]{2,1,0:T(8,128)(2,1)S(1)} async-done(((bf16[8,1088,128]{2,1,0:T(8,128)(2,1)}), bf16[8,1088,128]{2,1,0:T(8,128)(2,1)S(1)}, u32[]{:S(2)}, u32[]{:S(2)}) %all-to-all-start.7) | async-done | bytes 2228256 | tf_op jit(solution)/shard_map/all_to_all | solution.py:1113
  285.0 3.5 %all-to-all-start.8 = ((f32[16,8,256]{2,1,0:T(8,128)}), f32[16,8,256]{2,1,0:T(8,128)S(1)}, u32[]{:S(2)}, u32[]{:S(2)}) async-start(f32[16,8,256]{2,1,0:T(8,128)} %shard_map.329), calls=%async_computation.9 | async-start | bytes 262144 | tf_op jit(solution)/shard_map/all_to_all | solution.py:852
  289.3 2.4 shard_map.325
  291.7 1.8 collective-permute-start.40
  295.2 2.3 shard_map.326
  298.8 3.7 %collective-permute-done.41.refs_5_ = bf16[576,128]{1,0:T(8,128)(2,1)S(1)} collective-permute-done((bf16[576,128]{1,0:T(8,128)(2,1)}, bf16[576,128]{1,0:T(8,128)(2,1)S(1)}, u32[]{:S(2)}, u32[]{:S(2)}) %collective-permute-start.41) | collective-permute-done | bytes 147488 | tf_op jit(solution)/shard_map/ppermute | solution.py:836
  304.5 2.8 shard_map.327.refs_4_.refs_8_.refs_5_.refs_1_
  307.3 2.0 collective-permute-start.46
  311.5 2.0 shard_map.328
  316.3 2.5 collective-permute-start.53
  318.8 3.0 shard_map.330
  321.8 1.7 collective-permute-start.45
  323.5 5.1 %shard_map.333 = (f32[2,128]{1,0:T(2,128)}, f32[1,128]{1,0:T(1,128)}, f32[1,128]{1,0:T(1,128)}, f32[1,128]{1,0:T(1,128)}, f32[1,128]{1,0:T(1,128)}, /*index=5*/f...) custom-call(s32[8]{0:T(128)} %stack.81.refs_0_, f32[8,128]{1,0:T(8,128)} %get-tuple-element.139.refs_1_, ...), custom_call_target="tpu_custom_call" | custom-call | flops 17250000896 | bytes 1 | tf_op jit(solution)/shard_map/pallas_call | solution.py:758
  330.4 2.1 shard_map.331
  333.7 4.7 %shard_map.334 = (f32[4608,128]{1,0:T(8,128)}, f32[4608,128]{1,0:T(8,128)}, f32[1536,128]{1,0:T(8,128)}, f32[128,512]{1,0:T(8,128)}) custom-call(s32[8]{0:T(128)} %stack.81.refs_0_, bf16[1408,128]{1,0:T(8,128)(2,1)} %shard_map.327.refs_4_.refs_8_.refs_5_.refs_1_, bf16[1408,128]{1,0:T(8,128)(2,1)} %copy-done.37, bf16[1408,128]{1,0:T(8,128)(2,1)} %copy-done.38, ...), custom_call_target="tpu_custom_call" | custom-call | flops 1 | bytes 1 | tf_op jit(solution)/shard_map/pallas_call | solution.py:758
  (315 shorter events, 75.9 us)
Async XLA Ops:
  9.1 28.1 %collective-permute-start.5 = (bf16[576,128]{1,0:T(8,128)(2,1)S(1)}, bf16[576,128]{1,0:T(8,128)(2,1)}, u32[]{:S(2)}, u32[]{:S(2)}) collective-permute-start(bf16[576,128]{1,0:T(8,128)(2,1)S(1)} %constant_dynamic-slice_fusion.4.refs_2_), channel_id=1, source_target_pairs={{0,2},{1,3},{2,0},{3,1},{4,6},{5,7},{6,4},{7,5},{8,10},{9,11},{10,... | collective-permute-start | bytes 442376 | tf_op jit(solution)/shard_map/ppermute | solution.py:833
  15.5 20.1 %collective-permute-start = (bf16[512,128]{1,0:T(8,128)(2,1)}, bf16[512,128]{1,0:T(8,128)(2,1)}, u32[]{:S(2)}, u32[]{:S(2)}) collective-permute-start(bf16[512,128]{1,0:T(8,128)(2,1)} %get-tuple-element.85), channel_id=1, source_target_pairs={{0,2},{1,3},{2,0},{3,1},{4,6},{5,7},{6,4},{7,5},{8,10},{9,11},{10,... | collective-permute-start | bytes 393224 | tf_op jit(solution)/shard_map/ppermute | solution.py:833
  20.1 20.0 %collective-permute-start.1 = (bf16[512,128]{1,0:T(8,128)(2,1)}, bf16[512,128]{1,0:T(8,128)(2,1)S(1)}, u32[]{:S(2)}, u32[]{:S(2)}) collective-permute-start(bf16[512,128]{1,0:T(8,128)(2,1)} %get-tuple-element.84.refs_3_), channel_id=1, source_target_pairs={{0,1},{1,0},{2,3},{3,2},{4,5},{5,4},{6,7},{7,6},{8,9},{9,8},{10,11... | collective-permute-start | bytes 393224 | tf_op jit(solution)/shard_map/ppermute | solution.py:833
  23.7 37.5 %all-to-all-start = ((f32[32,16,128]{2,1,0:T(8,128)}), f32[32,16,128]{2,1,0:T(8,128)S(1)}, u32[]{:S(2)}, u32[]{:S(2)}) async-start(f32[32,16,128]{2,1,0:T(8,128)} %shard_map.299.refs_2_), calls=%async_computation | async-start | bytes 524288 | tf_op jit(solution)/shard_map/all_to_all | solution.py:908
  28.6 45.5 %all-gather.5.cloned.1.call-start = ((), (), s32[]{:S(2)}) async-start(), calls=%async_computation.11 | async-start | bytes 1916928 | tf_op jit(solution)/shard_map/all_gather | solution.py:925
  31.4 15.8 %collective-permute-start.14 = (bf16[832,128]{1,0:T(8,128)(2,1)}, bf16[832,128]{1,0:T(8,128)(2,1)}, u32[]{:S(2)}, u32[]{:S(2)}) collective-permute-start(bf16[832,128]{1,0:T(8,128)(2,1)} %pad_maximum_fusion.4), channel_id=1, source_target_pairs={{0,2},{1,3},{2,0},{3,1},{4,6},{5,7},{6,4},{7,5},{8,10},{9,11},{10,... | collective-permute-start | bytes 638984 | tf_op jit(solution)/shard_map/ppermute | solution.py:833
  35.6 11.6 %collective-permute-start.2 = (bf16[512,128]{1,0:T(8,128)(2,1)}, bf16[512,128]{1,0:T(8,128)(2,1)}, u32[]{:S(2)}, u32[]{:S(2)}) collective-permute-start(bf16[512,128]{1,0:T(8,128)(2,1)} %collective-permute-done), channel_id=1, source_target_pairs={{0,1},{1,0},{2,3},{3,2},{4,5},{5,4},{6,7},{7,6},{8,9},{9,8},{10,11... | collective-permute-start | bytes 393224 | tf_op jit(solution)/shard_map/ppermute | solution.py:833
  37.2 10.0 %collective-permute-start.6 = (bf16[576,128]{1,0:T(8,128)(2,1)}, bf16[576,128]{1,0:T(8,128)(2,1)S(1)}, u32[]{:S(2)}, u32[]{:S(2)}) collective-permute-start(bf16[576,128]{1,0:T(8,128)(2,1)} %collective-permute-done.5.refs_2_), channel_id=1, source_target_pairs={{0,8},{4,12},{8,0},{12,4},{16,24},{20,28},{24,16},{28,20},{1,9},{5... | collective-permute-start | bytes 442376 | tf_op jit(solution)/shard_map/ppermute | solution.py:836
  38.7 8.6 %collective-permute-start.7 = (bf16[576,128]{1,0:T(8,128)(2,1)}, bf16[576,128]{1,0:T(8,128)(2,1)S(1)}, u32[]{:S(2)}, u32[]{:S(2)}) collective-permute-start(bf16[576,128]{1,0:T(8,128)(2,1)} %collective-permute-done.5.refs_2_), channel_id=1, source_target_pairs={{0,16},{4,20},{8,24},{12,28},{16,0},{20,4},{24,8},{28,12},{1,17},{... | collective-permute-start | bytes 442376 | tf_op jit(solution)/shard_map/ppermute | solution.py:836
  40.2 7.1 %collective-permute-start.8 = (bf16[576,128]{1,0:T(8,128)(2,1)}, bf16[576,128]{1,0:T(8,128)(2,1)S(1)}, u32[]{:S(2)}, u32[]{:S(2)}) collective-permute-start(bf16[576,128]{1,0:T(8,128)(2,1)} %collective-permute-done.5.refs_2_), channel_id=1, source_target_pairs={{0,24},{4,28},{8,16},{12,20},{16,8},{20,12},{24,0},{28,4},{1,25},{... | collective-permute-start | bytes 442376 | tf_op jit(solution)/shard_map/ppermute | solution.py:836
  50.3 4.4 %collective-permute-start.9 = (bf16[576,128]{1,0:T(8,128)(2,1)}, bf16[576,128]{1,0:T(8,128)(2,1)S(1)}, u32[]{:S(2)}, u32[]{:S(2)}) collective-permute-start(bf16[576,128]{1,0:T(8,128)(2,1)} %collective-permute-done.5.refs_2_), channel_id=1, source_target_pairs={{0,4},{4,0},{8,12},{12,8},{16,20},{20,16},{24,28},{28,24},{1,5},{5... | collective-permute-start | bytes 442376 | tf_op jit(solution)/shard_map/ppermute | solution.py:836
  51.4 9.8 %collective-permute-start.3 = (bf16[128,512]{1,0:T(8,128)(2,1)S(1)}, bf16[128,512]{1,0:T(8,128)(2,1)S(1)}, u32[]{:S(2)}, u32[]{:S(2)}) collective-permute-start(bf16[128,512]{1,0:T(8,128)(2,1)S(1)} %pad_maximum_fusion.5), channel_id=1, source_target_pairs={{0,4},{4,8},{8,12},{12,16},{16,20},{20,24},{24,28},{28,0},{1,5},{5... | collective-permute-start | bytes 393224 | tf_op jit(solution)/shard_map/ppermute | solution.py:839
  52.0 9.2 %collective-permute-start.4 = (bf16[128,512]{1,0:T(8,128)(2,1)S(1)}, bf16[128,512]{1,0:T(8,128)(2,1)S(1)}, u32[]{:S(2)}, u32[]{:S(2)}) collective-permute-start(bf16[128,512]{1,0:T(8,128)(2,1)S(1)} %pad_maximum_fusion.6), channel_id=1, source_target_pairs={{0,28},{4,0},{8,4},{12,8},{16,12},{20,16},{24,20},{28,24},{1,29},{... | collective-permute-start | bytes 393224 | tf_op jit(solution)/shard_map/ppermute | solution.py:839
  54.2 2.1 collective-permute-start.10
  54.2 2.1 collective-permute-start.11
  67.5 10.7 %collective-permute-start.13 = (bf16[640,256]{1,0:T(8,128)(2,1)}, bf16[640,256]{1,0:T(8,128)(2,1)S(1)}, u32[]{:S(2)}, u32[]{:S(2)}) collective-permute-start(bf16[640,256]{1,0:T(8,128)(2,1)} %get-tuple-element.87.refs_1_.refs_3_), channel_id=1, source_target_pairs={{0,1},{1,0},{2,3},{3,2},{4,5},{5,4},{6,7},{7,6},{8,9},{9,8},{10,11... | collective-permute-start | bytes 983048 | tf_op jit(solution)/shard_map/ppermute | solution.py:833
  67.9 13.0 %all-to-all-start.1 = ((f32[16,8,256]{2,1,0:T(8,128)}), f32[16,8,256]{2,1,0:T(8,128)S(1)}, u32[]{:S(2)}, u32[]{:S(2)}) async-start(f32[16,8,256]{2,1,0:T(8,128)} %get-tuple-element.88), calls=%async_computation.1 | async-start | bytes 262144 | tf_op jit(solution)/shard_map/all_to_all | solution.py:852
  71.8 42.1 %reduce-scatter.2.cloned.1.call-start = ((), (), s32[]{:S(2)}) async-start(), calls=%async_computation.10 | async-start | bytes 348160 | tf_op jit(solution)/shard_map/reduce_scatter | solution.py:946
  79.0 26.0 %collective-permute-start.16 = (bf16[512,128]{1,0:T(8,128)(2,1)}, bf16[512,128]{1,0:T(8,128)(2,1)S(1)}, u32[]{:S(2)}, u32[]{:S(2)}) collective-permute-start(bf16[512,128]{1,0:T(8,128)(2,1)} %get-tuple-element.96), channel_id=1, source_target_pairs={{0,2},{1,3},{2,0},{3,1},{4,6},{5,7},{6,4},{7,5},{8,10},{9,11},{10,... | collective-permute-start | bytes 393224 | tf_op jit(solution)/shard_map/ppermute | solution.py:833
  87.0 19.1 %collective-permute-start.15 = (bf16[512,256]{1,0:T(8,128)(2,1)}, bf16[512,256]{1,0:T(8,128)(2,1)S(1)}, u32[]{:S(2)}, u32[]{:S(2)}) collective-permute-start(bf16[512,256]{1,0:T(8,128)(2,1)} %get-tuple-element.92.refs_1_.refs_3_.refs_5_), channel_id=1, source_target_pairs={{0,1},{1,0},{2,3},{3,2},{4,5},{5,4},{6,7},{7,6},{8,9},{9,8},{10,11... | collective-permute-start | bytes 786440 | tf_op jit(solution)/shard_map/ppermute | solution.py:833
  88.5 25.4 %all-to-all-start.2 = ((f32[16,8,256]{2,1,0:T(8,128)}), f32[16,8,256]{2,1,0:T(8,128)S(1)}, u32[]{:S(2)}, u32[]{:S(2)}) async-start(f32[16,8,256]{2,1,0:T(8,128)} %get-tuple-element.93), calls=%async_computation.2 | async-start | bytes 262144 | tf_op jit(solution)/shard_map/all_to_all | solution.py:852
  103.3 7.4 %collective-permute-start.17 = (bf16[512,128]{1,0:T(8,128)(2,1)S(1)}, bf16[512,128]{1,0:T(8,128)(2,1)S(1)}, u32[]{:S(2)}, u32[]{:S(2)}) collective-permute-start(bf16[512,128]{1,0:T(8,128)(2,1)S(1)} %copy-done.13), channel_id=1, source_target_pairs={{0,1},{1,0},{2,3},{3,2},{4,5},{5,4},{6,7},{7,6},{8,9},{9,8},{10,11... | collective-permute-start | bytes 393224 | tf_op jit(solution)/shard_map/ppermute | solution.py:833
  105.0 8.1 %collective-permute-start.18 = (bf16[512,128]{1,0:T(8,128)(2,1)S(1)}, bf16[512,128]{1,0:T(8,128)(2,1)S(1)}, u32[]{:S(2)}, u32[]{:S(2)}) collective-permute-start(bf16[512,128]{1,0:T(8,128)(2,1)S(1)} %collective-permute-done.16), channel_id=1, source_target_pairs={{0,1},{1,0},{2,3},{3,2},{4,5},{5,4},{6,7},{7,6},{8,9},{9,8},{10,11... | collective-permute-start | bytes 393224 | tf_op jit(solution)/shard_map/ppermute | solution.py:833
  118.8 21.9 %all-to-all-start.3 = ((bf16[8,256,256]{2,1,0:T(8,128)(2,1)}), bf16[8,256,256]{2,1,0:T(8,128)(2,1)S(1)}, u32[]{:S(2)}, u32[]{:S(2)}) async-start(bf16[8,256,256]{2,1,0:T(8,128)(2,1)} %bitcast.87), calls=%async_computation.4 | async-start | bytes 2097152 | tf_op jit(solution)/shard_map/all_to_all | solution.py:1009
  123.7 15.4 %collective-permute-start.19 = (bf16[128,256]{1,0:T(8,128)(2,1)S(1)}, bf16[128,256]{1,0:T(8,128)(2,1)S(1)}, u32[]{:S(2)}, u32[]{:S(2)}) collective-permute-start(bf16[128,256]{1,0:T(8,128)(2,1)S(1)} %get-tuple-element.175), channel_id=1, source_target_pairs={{0,4},{4,8},{8,12},{12,16},{16,20},{20,24},{24,28},{28,0},{1,5},{5... | collective-permute-start | bytes 196616 | tf_op jit(solution)/shard_map/ppermute | solution.py:839
  124.2 14.8 %collective-permute-start.20 = (bf16[128,256]{1,0:T(8,128)(2,1)S(1)}, bf16[128,256]{1,0:T(8,128)(2,1)S(1)}, u32[]{:S(2)}, u32[]{:S(2)}) collective-permute-start(bf16[128,256]{1,0:T(8,128)(2,1)S(1)} %get-tuple-element.174), channel_id=1, source_target_pairs={{0,28},{4,0},{8,4},{12,8},{16,12},{20,16},{24,20},{28,24},{1,29},{... | collective-permute-start | bytes 196616 | tf_op jit(solution)/shard_map/ppermute | solution.py:839
  126.4 14.3 %collective-permute-start.23 = (bf16[256,512]{1,0:T(8,128)(2,1)}, bf16[256,512]{1,0:T(8,128)(2,1)S(1)}, u32[]{:S(2)}, u32[]{:S(2)}) collective-permute-start(bf16[256,512]{1,0:T(8,128)(2,1)} %get-tuple-element.102.refs_1_), channel_id=1, source_target_pairs={{0,2},{1,3},{2,0},{3,1},{4,6},{5,7},{6,4},{7,5},{8,10},{9,11},{10,... | collective-permute-start | bytes 786440 | tf_op jit(solution)/shard_map/ppermute | solution.py:833
  127.0 13.5 %collective-permute-start.21 = (bf16[128,256]{1,0:T(8,128)(2,1)S(1)}, bf16[128,256]{1,0:T(8,128)(2,1)S(1)}, u32[]{:S(2)}, u32[]{:S(2)}) collective-permute-start(bf16[128,256]{1,0:T(8,128)(2,1)S(1)} %get-tuple-element.173), channel_id=1, source_target_pairs={{0,4},{4,8},{8,12},{12,16},{16,20},{20,24},{24,28},{28,0},{1,5},{5... | collective-permute-start | bytes 196616 | tf_op jit(solution)/shard_map/ppermute | solution.py:839
  127.0 13.4 %collective-permute-start.22 = (bf16[128,256]{1,0:T(8,128)(2,1)S(1)}, bf16[128,256]{1,0:T(8,128)(2,1)S(1)}, u32[]{:S(2)}, u32[]{:S(2)}) collective-permute-start(bf16[128,256]{1,0:T(8,128)(2,1)S(1)} %get-tuple-element.172), channel_id=1, source_target_pairs={{0,28},{4,0},{8,4},{12,8},{16,12},{20,16},{24,20},{28,24},{1,29},{... | collective-permute-start | bytes 196616 | tf_op jit(solution)/shard_map/ppermute | solution.py:839
  143.5 2.0 collective-permute-start.24
  143.6 37.4 %collective-permute-start.26 = (bf16[768,512]{1,0:T(8,128)(2,1)S(1)}, bf16[768,512]{1,0:T(8,128)(2,1)S(1)}, u32[]{:S(2)}, u32[]{:S(2)}) collective-permute-start(bf16[768,512]{1,0:T(8,128)(2,1)S(1)} %copy-done.18), channel_id=1, source_target_pairs={{0,2},{1,3},{2,0},{3,1},{4,6},{5,7},{6,4},{7,5},{8,10},{9,11},{10,... | collective-permute-start | bytes 2359304 | tf_op jit(solution)/shard_map/ppermute | solution.py:833
  179.8 2.2 collective-permute-start.25
  185.5 19.0 %all-to-all-start.4 = ((bf16[8,256,256]{2,1,0:T(8,128)(2,1)}), bf16[8,256,256]{2,1,0:T(8,128)(2,1)S(1)}, u32[]{:S(2)}, u32[]{:S(2)}) async-start(bf16[8,256,256]{2,1,0:T(8,128)(2,1)} %bitcast.88), calls=%async_computation.5 | async-start | bytes 2097152 | tf_op jit(solution)/shard_map/all_to_all | solution.py:1044
  189.2 66.5 %all-gather.7.cloned.1.call-start = ((), (), s32[]{:S(2)}) async-start(), calls=%async_computation.12 | async-start | bytes 1179648 | tf_op jit(solution)/shard_map/all_gather | solution.py:1055
  190.7 5.5 %collective-permute-start.28 = (bf16[260,128]{1,0:T(8,128)(2,1)S(1)}, bf16[260,128]{1,0:T(8,128)(2,1)S(1)}, u32[]{:S(2)}, u32[]{:S(2)}) collective-permute-start(bf16[260,128]{1,0:T(8,128)(2,1)S(1)} %fusion.5.refs_2_), channel_id=1, source_target_pairs={{0,1},{1,0},{2,3},{3,2},{4,5},{5,4},{6,7},{7,6},{8,9},{9,8},{10,11... | collective-permute-start | bytes 199688 | tf_op jit(solution)/shard_map/ppermute | solution.py:833
  191.0 8.6 %collective-permute-start.29 = (bf16[260,128]{1,0:T(8,128)(2,1)S(1)}, bf16[260,128]{1,0:T(8,128)(2,1)S(1)}, u32[]{:S(2)}, u32[]{:S(2)}) collective-permute-start(bf16[260,128]{1,0:T(8,128)(2,1)S(1)} %fusion.5.refs_2_), channel_id=1, source_target_pairs={{0,2},{1,3},{2,0},{3,1},{4,6},{5,7},{6,4},{7,5},{8,10},{9,11},{10,... | collective-permute-start | bytes 199688 | tf_op jit(solution)/shard_map/ppermute | solution.py:833
  192.1 7.5 %collective-permute-start.30 = (bf16[260,128]{1,0:T(8,128)(2,1)S(1)}, bf16[260,128]{1,0:T(8,128)(2,1)S(1)}, u32[]{:S(2)}, u32[]{:S(2)}) collective-permute-start(bf16[260,128]{1,0:T(8,128)(2,1)S(1)} %fusion.5.refs_2_), channel_id=1, source_target_pairs={{0,3},{1,2},{2,1},{3,0},{4,7},{5,6},{6,5},{7,4},{8,11},{9,10},{10,... | collective-permute-start | bytes 199688 | tf_op jit(solution)/shard_map/ppermute | solution.py:833
  209.0 6.6 %collective-permute-start.31 = (bf16[512,256]{1,0:T(8,128)(2,1)}, bf16[512,256]{1,0:T(8,128)(2,1)S(1)}, u32[]{:S(2)}, u32[]{:S(2)}) collective-permute-start(bf16[512,256]{1,0:T(8,128)(2,1)} %get-tuple-element.110), channel_id=1, source_target_pairs={{0,1},{1,0},{2,3},{3,2},{4,5},{5,4},{6,7},{7,6},{8,9},{9,8},{10,11... | collective-permute-start | bytes 786440 | tf_op jit(solution)/shard_map/ppermute | solution.py:833
  209.2 15.1 %all-to-all-start.5 = ((f32[16,8,256]{2,1,0:T(8,128)}), f32[16,8,256]{2,1,0:T(8,128)S(1)}, u32[]{:S(2)}, u32[]{:S(2)}) async-start(f32[16,8,256]{2,1,0:T(8,128)} %get-tuple-element.114), calls=%async_computation.6 | async-start | bytes 262144 | tf_op jit(solution)/shard_map/all_to_all | solution.py:852
  216.7 7.7 %collective-permute-start.32 = (bf16[128,256]{1,0:T(8,128)(2,1)S(1)}, bf16[128,256]{1,0:T(8,128)(2,1)S(1)}, u32[]{:S(2)}, u32[]{:S(2)}) collective-permute-start(bf16[128,256]{1,0:T(8,128)(2,1)S(1)} %get-tuple-element.156), channel_id=1, source_target_pairs={{0,4},{4,8},{8,12},{12,16},{16,20},{20,24},{24,28},{28,0},{1,5},{5... | collective-permute-start | bytes 196616 | tf_op jit(solution)/shard_map/ppermute | solution.py:839
  216.7 7.6 %collective-permute-start.33 = (bf16[128,256]{1,0:T(8,128)(2,1)S(1)}, bf16[128,256]{1,0:T(8,128)(2,1)S(1)}, u32[]{:S(2)}, u32[]{:S(2)}) collective-permute-start(bf16[128,256]{1,0:T(8,128)(2,1)S(1)} %get-tuple-element.155), channel_id=1, source_target_pairs={{0,28},{4,0},{8,4},{12,8},{16,12},{20,16},{24,20},{28,24},{1,29},{... | collective-permute-start | bytes 196616 | tf_op jit(solution)/shard_map/ppermute | solution.py:839
  228.1 10.5 %collective-permute-start.35 = (bf16[640,128]{1,0:T(8,128)(2,1)}, bf16[640,128]{1,0:T(8,128)(2,1)S(1)}, u32[]{:S(2)}, u32[]{:S(2)}) collective-permute-start(bf16[640,128]{1,0:T(8,128)(2,1)} %get-tuple-element.119), channel_id=1, source_target_pairs={{0,2},{1,3},{2,0},{3,1},{4,6},{5,7},{6,4},{7,5},{8,10},{9,11},{10,... | collective-permute-start | bytes 491528 | tf_op jit(solution)/shard_map/ppermute | solution.py:833
  235.1 10.4 %collective-permute-start.34 = (bf16[640,256]{1,0:T(8,128)(2,1)}, bf16[640,256]{1,0:T(8,128)(2,1)S(1)}, u32[]{:S(2)}, u32[]{:S(2)}) collective-permute-start(bf16[640,256]{1,0:T(8,128)(2,1)} %get-tuple-element.117), channel_id=1, source_target_pairs={{0,1},{1,0},{2,3},{3,2},{4,5},{5,4},{6,7},{7,6},{8,9},{9,8},{10,11... | collective-permute-start | bytes 983048 | tf_op jit(solution)/shard_map/ppermute | solution.py:833
  239.2 12.0 %all-to-all-start.6 = ((f32[16,8,256]{2,1,0:T(8,128)}), f32[16,8,256]{2,1,0:T(8,128)S(1)}, u32[]{:S(2)}, u32[]{:S(2)}) async-start(f32[16,8,256]{2,1,0:T(8,128)} %shard_map.318), calls=%async_computation.7 | async-start | bytes 262144 | tf_op jit(solution)/shard_map/all_to_all | solution.py:852
  251.8 31.8 %all-to-all-start.7 = ((bf16[8,1088,128]{2,1,0:T(8,128)(2,1)}), bf16[8,1088,128]{2,1,0:T(8,128)(2,1)S(1)}, u32[]{:S(2)}, u32[]{:S(2)}) async-start(bf16[8,1088,128]{2,1,0:T(8,128)(2,1)} %shard_map.319.refs_7_), calls=%async_computation.8 | async-start | bytes 4456448 | tf_op jit(solution)/shard_map/all_to_all | solution.py:1113
  258.8 10.3 %collective-permute-start.36 = (bf16[640,128]{1,0:T(8,128)(2,1)}, bf16[640,128]{1,0:T(8,128)(2,1)S(1)}, u32[]{:S(2)}, u32[]{:S(2)}) collective-permute-start(bf16[640,128]{1,0:T(8,128)(2,1)} %get-tuple-element.121), channel_id=1, source_target_pairs={{0,2},{1,3},{2,0},{3,1},{4,6},{5,7},{6,4},{7,5},{8,10},{9,11},{10,... | collective-permute-start | bytes 491528 | tf_op jit(solution)/shard_map/ppermute | solution.py:833
  274.6 13.9 %collective-permute-start.38 = (bf16[4,576,128]{2,1,0:T(8,128)(2,1)}, bf16[4,576,128]{2,1,0:T(8,128)(2,1)S(1)}, u32[]{:S(2)}, u32[]{:S(2)}) collective-permute-start(bf16[4,576,128]{2,1,0:T(8,128)(2,1)} %get-tuple-element.125), channel_id=1, source_target_pairs={{0,4},{4,0},{8,12},{12,8},{16,20},{20,16},{24,28},{28,24},{1,5},{5... | collective-permute-start | bytes 1769480 | tf_op jit(solution)/shard_map/ppermute | solution.py:836
  274.7 36.1 %collective-permute-start.37 = (bf16[512,256]{1,0:T(8,128)(2,1)}, bf16[512,256]{1,0:T(8,128)(2,1)S(1)}, u32[]{:S(2)}, u32[]{:S(2)}) collective-permute-start(bf16[512,256]{1,0:T(8,128)(2,1)} %shard_map.321), channel_id=1, source_target_pairs={{0,1},{1,0},{2,3},{3,2},{4,5},{5,4},{6,7},{7,6},{8,9},{9,8},{10,11... | collective-permute-start | bytes 786440 | tf_op jit(solution)/shard_map/ppermute | solution.py:833
  275.1 41.2 %collective-permute-start.44 = (bf16[512,256]{1,0:T(8,128)(2,1)S(1)}, bf16[512,256]{1,0:T(8,128)(2,1)}, u32[]{:S(2)}, u32[]{:S(2)}) collective-permute-start(bf16[512,256]{1,0:T(8,128)(2,1)S(1)} %copy-done.72), channel_id=1, source_target_pairs={{0,1},{1,0},{2,3},{3,2},{4,5},{5,4},{6,7},{7,6},{8,9},{9,8},{10,11... | collective-permute-start | bytes 786440 | tf_op jit(solution)/shard_map/ppermute | solution.py:833
  285.0 29.0 %all-to-all-start.8 = ((f32[16,8,256]{2,1,0:T(8,128)}), f32[16,8,256]{2,1,0:T(8,128)S(1)}, u32[]{:S(2)}, u32[]{:S(2)}) async-start(f32[16,8,256]{2,1,0:T(8,128)} %shard_map.329), calls=%async_computation.9 | async-start | bytes 262144 | tf_op jit(solution)/shard_map/all_to_all | solution.py:852
  291.7 6.8 %collective-permute-start.40 = (bf16[576,128]{1,0:T(8,128)(2,1)}, bf16[576,128]{1,0:T(8,128)(2,1)S(1)}, u32[]{:S(2)}, u32[]{:S(2)}) collective-permute-start(bf16[576,128]{1,0:T(8,128)(2,1)} %get-tuple-element.127), channel_id=1, source_target_pairs={{0,8},{4,12},{8,0},{12,4},{16,24},{20,28},{24,16},{28,20},{1,9},{5... | collective-permute-start | bytes 442376 | tf_op jit(solution)/shard_map/ppermute | solution.py:836
  293.5 9.0 %collective-permute-start.41 = (bf16[576,128]{1,0:T(8,128)(2,1)}, bf16[576,128]{1,0:T(8,128)(2,1)S(1)}, u32[]{:S(2)}, u32[]{:S(2)}) collective-permute-start(bf16[576,128]{1,0:T(8,128)(2,1)} %get-tuple-element.128), channel_id=1, source_target_pairs={{0,16},{4,20},{8,24},{12,28},{16,0},{20,4},{24,8},{28,12},{1,17},{... | collective-permute-start | bytes 442376 | tf_op jit(solution)/shard_map/ppermute | solution.py:836
  295.0 7.5 %collective-permute-start.42 = (bf16[576,128]{1,0:T(8,128)(2,1)}, bf16[576,128]{1,0:T(8,128)(2,1)S(1)}, u32[]{:S(2)}, u32[]{:S(2)}) collective-permute-start(bf16[576,128]{1,0:T(8,128)(2,1)} %get-tuple-element.129), channel_id=1, source_target_pairs={{0,24},{4,28},{8,16},{12,20},{16,8},{20,12},{24,0},{28,4},{1,25},{... | collective-permute-start | bytes 442376 | tf_op jit(solution)/shard_map/ppermute | solution.py:836
  298.4 5.4 %collective-permute-start.39 = (bf16[256,128]{1,0:T(8,128)(2,1)}, bf16[256,128]{1,0:T(8,128)(2,1)S(1)}, u32[]{:S(2)}, u32[]{:S(2)}) collective-permute-start(bf16[256,128]{1,0:T(8,128)(2,1)} %shard_map.326), channel_id=1, source_target_pairs={{0,2},{1,3},{2,0},{3,1},{4,6},{5,7},{6,4},{7,5},{8,10},{9,11},{10,... | collective-permute-start | bytes 196616 | tf_op jit(solution)/shard_map/ppermute | solution.py:833
  307.3 21.5 %collective-permute-start.46 = (bf16[1408,128]{1,0:T(8,128)(2,1)}, bf16[1408,128]{1,0:T(8,128)(2,1)S(1)}, u32[]{:S(2)}, u32[]{:S(2)}) collective-permute-start(bf16[1408,128]{1,0:T(8,128)(2,1)} %shard_map.327.refs_4_.refs_8_.refs_5_.refs_1_), channel_id=1, source_target_pairs={{0,8},{4,12},{8,0},{12,4},{16,24},{20,28},{24,16},{28,20},{1,9},{5... | collective-permute-start | bytes 1081352 | tf_op jit(solution)/shard_map/ppermute | solution.py:836
  309.2 20.0 %collective-permute-start.47 = (bf16[1408,128]{1,0:T(8,128)(2,1)}, bf16[1408,128]{1,0:T(8,128)(2,1)S(1)}, u32[]{:S(2)}, u32[]{:S(2)}) collective-permute-start(bf16[1408,128]{1,0:T(8,128)(2,1)} %shard_map.327.refs_4_.refs_8_.refs_5_.refs_1_), channel_id=1, source_target_pairs={{0,16},{4,20},{8,24},{12,28},{16,0},{20,4},{24,8},{28,12},{1,17},{... | collective-permute-start | bytes 1081352 | tf_op jit(solution)/shard_map/ppermute | solution.py:836
  310.7 18.6 %collective-permute-start.48 = (bf16[1408,128]{1,0:T(8,128)(2,1)}, bf16[1408,128]{1,0:T(8,128)(2,1)S(1)}, u32[]{:S(2)}, u32[]{:S(2)}) collective-permute-start(bf16[1408,128]{1,0:T(8,128)(2,1)} %shard_map.327.refs_4_.refs_8_.refs_5_.refs_1_), channel_id=1, source_target_pairs={{0,24},{4,28},{8,16},{12,20},{16,8},{20,12},{24,0},{28,4},{1,25},{... | collective-permute-start | bytes 1081352 | tf_op jit(solution)/shard_map/ppermute | solution.py:836
  313.5 15.1 %collective-permute-start.43 = (bf16[512,128]{1,0:T(8,128)(2,1)}, bf16[512,128]{1,0:T(8,128)(2,1)S(1)}, u32[]{:S(2)}, u32[]{:S(2)}) collective-permute-start(bf16[512,128]{1,0:T(8,128)(2,1)} %get-tuple-element.131), channel_id=1, source_target_pairs={{0,2},{1,3},{2,0},{3,1},{4,6},{5,7},{6,4},{7,5},{8,10},{9,11},{10,... | collective-permute-start | bytes 393224 | tf_op jit(solution)/shard_map/ppermute | solution.py:833
  316.3 5.5 %collective-permute-start.53 = (f32[8,128]{1,0:T(8,128)}, f32[8,128]{1,0:T(8,128)S(1)}, u32[]{:S(2)}, u32[]{:S(2)}) collective-permute-start(f32[8,128]{1,0:T(8,128)} %get-tuple-element.140), channel_id=1, source_target_pairs={{0,2},{1,3},{2,0},{3,1},{4,6},{5,7},{6,4},{7,5},{8,10},{9,11},{10,... | collective-permute-start | bytes 12296 | tf_op jit(solution)/shard_map/ppermute | solution.py:833
  321.8 8.0 %collective-permute-start.45 = (bf16[512,128]{1,0:T(8,128)(2,1)}, bf16[512,128]{1,0:T(8,128)(2,1)S(1)}, u32[]{:S(2)}, u32[]{:S(2)}) collective-permute-start(bf16[512,128]{1,0:T(8,128)(2,1)} %get-tuple-element.136), channel_id=1, source_target_pairs={{0,2},{1,3},{2,0},{3,1},{4,6},{5,7},{6,4},{7,5},{8,10},{9,11},{10,... | collective-permute-start | bytes 393224 | tf_op jit(solution)/shard_map/ppermute | solution.py:833
  328.6 3.9 %collective-permute-start.49 = (bf16[1408,128]{1,0:T(8,128)(2,1)S(1)}, bf16[1408,128]{1,0:T(8,128)(2,1)S(1)}, u32[]{:S(2)}, u32[]{:S(2)}) collective-permute-start(bf16[1408,128]{1,0:T(8,128)(2,1)S(1)} %copy-done.5), channel_id=1, source_target_pairs={{0,4},{4,0},{8,12},{12,8},{16,20},{20,16},{24,28},{28,24},{1,5},{5... | collective-permute-start | bytes 1081352 | tf_op jit(solution)/shard_map/ppermute | solution.py:836
  328.7 3.8 %collective-permute-start.50 = (bf16[1408,128]{1,0:T(8,128)(2,1)S(1)}, bf16[1408,128]{1,0:T(8,128)(2,1)S(1)}, u32[]{:S(2)}, u32[]{:S(2)}) collective-permute-start(bf16[1408,128]{1,0:T(8,128)(2,1)S(1)} %collective-permute-done.46.refs_2_), channel_id=1, source_target_pairs={{0,4},{4,0},{8,12},{12,8},{16,20},{20,16},{24,28},{28,24},{1,5},{5... | collective-permute-start | bytes 1081352 | tf_op jit(solution)/shard_map/ppermute | solution.py:836
  329.2 3.4 collective-permute-start.51
  329.3 3.3 collective-permute-start.52
  (78 other events, 270.6 us)
Sparse Core Ops, SparseCore 0:
  48.8 25.2 all-gather.4
  203.5 23.9 all-gather.6
Sparse Core Ops, SparseCore 1:
  81.0 19.5 reduce-scatter.1
